TPU v7x, 32 devices: a whole 2x2x4 slice. The times are simulated.
32 devices in a mesh: pipe: 2 (over x), dp: 4 (over y, core), inner: 4 (over z).
Axes of the slice: x: 2, y: 2, z: 4, core: 2. Of those that a mesh axis runs over, the one named last changes fastest.
Arguments:
- pixels: bfloat16 [16, 48, 16, 256], P('dp', 'inner'), may hold values from -6 to 6
- date_days: int32 [16, 16], P('dp'), may hold values from 0 to 364
- clear_count: int32 [16], P('dp'), may hold values from 3 to 16, as said below
- batch_slot: int32 [16], P('dp'), may hold values from 0 to 3, as said below
- labels: int32 [16, 48], P('dp'), may hold values from 0 to 15
- class_tokens: bfloat16 [16, 256], replicated, may hold values from -6 to 6
- section_gain: float32 [2, 256], P('pipe'), may hold values from 0.5 to 2
- segment_probe_lookup_content: bfloat16 [2, 256, 768], P('pipe'), may hold values from -0.375 to 0.375
- section_out: bfloat16 [2, 256, 256], P('pipe'), may hold values from -0.375 to 0.375
- head_vec: float32 [256], replicated, may hold values from -1 to 1
Outputs:
- batch_loss: float32 [4], replicated
- class_grad: float32 [16, 256], replicated
- section_gain_grad: float32 [2, 256], P('pipe')
- section_qkv_grad: float32 [2, 256, 768], P('pipe')
- section_out_grad: float32 [2, 256, 256], P('pipe')
- readout_derivative: float32 [256], replicated
Inputs may be any that keep to these rules, and one draw needn't show every extreme that they name: The clear dates of tile b are its dates 0 to clear_count[b] - 1. Some tile has all 16 dates clear and some tile has the fewest. `batch_slot`: within each aligned block of 4 tiles (the tiles of one index of dp) every micro-batch number appears exactly once.
All inputs are finite; a program needn't handle non-finite values.
Results may differ from a plain program's by a relative error of at most 0.0015.
The roundings to bfloat16 on the way count: a program that leaves them out, or rounds other values in their place, can miss the bound.
Values may be sent and summed in bfloat16 or wider, within the bound.
A program may use at most 64 MiB of HBM per device.

v0:
```python
import math

import jax
import jax.numpy as jnp
from jax import lax
from jax.sharding import PartitionSpec as P

HEADS = 8
CLASSES = 16
PATCHES = 48
MICRO = 4


normalizer_sharpness = 10.0
logit_cap = 15.0
norm_eps = 1e-05
head_eps = 1e-06


def matmul_f32(left_side, right_side):
    return jnp.einsum(
        "...d,de->...e",
        left_side,
        right_side.astype(jnp.bfloat16),
        preferred_element_type=jnp.float32,
    )


def rms_norm(inputs, gain_vec):
    inverse_rms = lax.rsqrt(jnp.mean(inputs * inputs, axis=-1, keepdims=True) + norm_eps)
    return inputs * inverse_rms * gain_vec


def unit_heads(values):
    shaped = values.reshape(values.shape[:-1] + (HEADS, values.shape[-1] // HEADS))
    return shaped * lax.rsqrt(jnp.sum(shaped * shaped, axis=-1, keepdims=True) + head_eps)


def temporal(pixel_rows, date_days, counts, params):
    class_init, gain_vec, w_qkv, w_out = params
    batch_count, patches, dates_max, model_width = pixel_rows.shape
    classes = class_init.shape[0]
    band_channel = jnp.arange(model_width)
    frequency = jnp.exp(
        (band_channel // 2 * 2).astype(jnp.float32) * (-math.log(10000.0) / model_width)
    )
    phases = date_days.astype(jnp.float32)[:, :, None] * frequency
    encoding = jnp.where(band_channel % 2 == 0, jnp.sin(phases), jnp.cos(phases))
    date_rows = pixel_rows.astype(jnp.float32) + encoding[:, None]
    class_rows = jnp.broadcast_to(class_init, (batch_count, patches, classes, model_width))
    sequence = jnp.concatenate([class_rows, date_rows], axis=2)
    normed = rms_norm(sequence, gain_vec).astype(jnp.bfloat16)
    probe_entry_lines = unit_heads(matmul_f32(normed[:, :, :classes], w_qkv[:, :model_width]))
    lookup_entry_lines = unit_heads(matmul_f32(normed, w_qkv[:, model_width : 2 * model_width]))
    value_rows = matmul_f32(normed, w_qkv[:, 2 * model_width :]).astype(jnp.bfloat16)
    value_heads = value_rows.reshape(
        batch_count, patches, classes + dates_max, HEADS, model_width // HEADS
    )
    affinity_logit_grid = normalizer_sharpness * jnp.einsum(
        "ohbyv,ohsyv->ohybs", probe_entry_lines, lookup_entry_lines, precision=lax.Precision.HIGHEST
    )
    position = jnp.arange(classes + dates_max)
    key_mask = (
        (position[None, :] < classes) | (position[None, :] - classes < counts[:, None])
    ).astype(jnp.float32)
    raised = jnp.exp(affinity_logit_grid) * key_mask[:, None, None, None, :]
    weights = (raised / jnp.sum(raised, axis=-1, keepdims=True)).astype(jnp.bfloat16)
    attended = jnp.einsum(
        "bphqk,bpkhe->bpqhe", weights, value_heads, preferred_element_type=jnp.float32
    )
    attended = attended.reshape(batch_count, patches, classes, model_width).astype(jnp.bfloat16)
    updated = sequence[:, :, :classes] + matmul_f32(attended, w_out)
    return jnp.swapaxes(updated, 1, 2).astype(jnp.bfloat16)


def spatial(inputs, params):
    gain_vec, w_qkv, w_out, head_vec = params
    batch_count, groups, classes, patches, model_width = inputs.shape
    class_seq = (
        jnp.swapaxes(inputs, 1, 2)
        .reshape(batch_count, classes, groups * patches, model_width)
        .astype(jnp.float32)
    )
    normed = rms_norm(class_seq, gain_vec).astype(jnp.bfloat16)
    probe_entry_lines = unit_heads(matmul_f32(normed, w_qkv[:, :model_width]))
    lookup_entry_lines = unit_heads(matmul_f32(normed, w_qkv[:, model_width : 2 * model_width]))
    value_rows = matmul_f32(normed, w_qkv[:, 2 * model_width :]).astype(jnp.bfloat16)
    value_heads = value_rows.reshape(
        batch_count, classes, groups * patches, HEADS, model_width // HEADS
    )
    affinity_logit_grid = normalizer_sharpness * jnp.einsum(
        "wisbx,wiqbx->wibsq", probe_entry_lines, lookup_entry_lines, precision=lax.Precision.HIGHEST
    )
    raised = jnp.exp(affinity_logit_grid)
    weights = (raised / jnp.sum(raised, axis=-1, keepdims=True)).astype(jnp.bfloat16)
    attended = jnp.einsum(
        "bchqk,bckhe->bcqhe", weights, value_heads, preferred_element_type=jnp.float32
    )
    attended = attended.reshape(batch_count, classes, groups * patches, model_width).astype(
        jnp.bfloat16
    )
    hidden = class_seq + matmul_f32(attended, w_out)
    raw_logits = jnp.einsum("bcpd,d->bcp", hidden, head_vec, precision=lax.Precision.HIGHEST)
    logits = logit_cap * jnp.tanh(raw_logits / logit_cap)
    return logits.reshape(batch_count, classes, groups, patches)


def shards(
    pixels,
    date_days,
    clear_count,
    batch_slot,
    labels,
    class_tokens,
    section_gain,
    segment_probe_lookup_content,
    section_out,
    head_vec,
):
    tiles_dev = pixels.shape[0]
    patches_dev = pixels.shape[1]
    model_width = pixels.shape[3]
    inner_count = lax.axis_size("inner")
    classes_dev = CLASSES // inner_count
    total_tiles = tiles_dev * lax.axis_size("dp")
    my_group = lax.axis_index("inner")
    class_ids = my_group * classes_dev + jnp.arange(classes_dev, dtype=jnp.int32)
    batch_norm = 1.0 / (total_tiles // MICRO * PATCHES)
    gains, qkv_all, out_all = (
        lax.all_gather(section_gain, "pipe", axis=0, tiled=True),
        lax.all_gather(
            segment_probe_lookup_content.astype(jnp.float32), "pipe", axis=0, tiled=True
        ),
        lax.all_gather(section_out.astype(jnp.float32), "pipe", axis=0, tiled=True),
    )
    pipe_pos = lax.axis_index("pipe")
    half_tiles = tiles_dev // 2
    first_params = (class_tokens.astype(jnp.float32), gains[0], qkv_all[0], out_all[0])
    second_params = (gains[1], qkv_all[1], out_all[1], head_vec)
    fold_shape = (1, inner_count, classes_dev, patches_dev, model_width)
    first_gradients = jax.tree.map(jnp.zeros_like, first_params)
    grads_second = jax.tree.map(jnp.zeros_like, second_params)
    loss_vec = jnp.zeros((MICRO,), jnp.float32)
    for tile_step in range(half_tiles):
        start = pipe_pos * half_tiles + tile_step
        single_pixel = lax.dynamic_slice_in_dim(pixels, start, 1, 0)
        days_one = lax.dynamic_slice_in_dim(date_days, start, 1, 0)
        count_one = lax.dynamic_slice_in_dim(clear_count, start, 1, 0)
        label_one = lax.dynamic_slice_in_dim(labels, start, 1, 0)
        slot_one = lax.dynamic_slice_in_dim(batch_slot, start, 1, 0)
        encoded, pull_first = jax.vjp(
            lambda params: temporal(single_pixel, days_one, count_one, params), first_params
        )
        arrived = lax.all_to_all(
            encoded.reshape(fold_shape), "inner", split_axis=1, concat_axis=1, tiled=True
        )
        logits, pull_second = jax.vjp(spatial, arrived, second_params)
        exp_logits = jnp.exp(logits)
        class_total = lax.psum(jnp.sum(exp_logits, axis=1), "inner")
        label_rows = label_one.reshape(1, 1, inner_count, patches_dev)
        indicator_rows = (label_rows == class_ids[None, :, None, None]).astype(jnp.float32)
        dlogit = (exp_logits / class_total[:, None] - indicator_rows) / total_tiles
        grad_in, grad_two = pull_second(dlogit)
        returned = lax.all_to_all(grad_in, "inner", split_axis=1, concat_axis=1, tiled=True)
        (derivative_lone,) = pull_first(returned.reshape(encoded.shape))
        first_gradients = jax.tree.map(
            lambda total, extra: total + extra, first_gradients, derivative_lone
        )
        grads_second = jax.tree.map(lambda total, extra: total + extra, grads_second, grad_two)
        loss_term = jnp.sum(indicator_rows * (jnp.log(class_total)[:, None] - logits)) * batch_norm
        loss_vec = loss_vec + loss_term * (jnp.arange(MICRO) == slot_one[0]).astype(jnp.float32)
    stacked = (
        jnp.stack([first_gradients[1], grads_second[0]]),
        jnp.stack([first_gradients[2], grads_second[1]]),
        jnp.stack([first_gradients[3], grads_second[2]]),
        first_gradients[0],
        grads_second[3],
        loss_vec,
    )
    summed = lax.psum(
        (stacked[0], stacked[1], stacked[2], stacked[3], stacked[4], stacked[5]),
        ("pipe", "dp", "inner"),
    )
    gain_grad = lax.dynamic_slice_in_dim(summed[0], pipe_pos, 1, 0)
    qkv_grad = lax.dynamic_slice_in_dim(summed[1], pipe_pos, 1, 0)
    out_grad = lax.dynamic_slice_in_dim(summed[2], pipe_pos, 1, 0)
    return (summed[5], summed[3], gain_grad, qkv_grad, out_grad, summed[4])


def solution(mesh):
    placed = (
        P("dp", "inner", None, None),
        P("dp", None),
        P("dp"),
        P("dp"),
        P("dp", None),
        P(),
        P("pipe", None),
        P("pipe", None, None),
        P("pipe", None, None),
        P(),
    )
    return jax.shard_map(
        shards,
        mesh=mesh,
        in_specs=placed,
        out_specs=(P(), P(), P("pipe", None), P("pipe", None, None), P("pipe", None, None), P()),
        check_vma=False,
    )
```

profile of v0, /device:TPU:0, one launch (start us, length us, event | category | flops | bytes accessed | tf_op | source)
XLA Modules:
  0.0 420.5 jit_solution(11192878133737695859)
XLA Ops:
  7.2 5.5 %all-gather = f32[2,1,256]{2,1,0:T(1,128)S(1)} all-gather(f32[1,1,256]{2,1,0:T(1,128)} %bitcast.538), channel_id=1, replica_groups=mesh['pipe'=2,'dp'=4,'inner'=4] {'pipe'}, dimensions={0}, use_global_device_ids=true | all-gather | bytes 3072 | tf_op jit(solution)/shard_map/all_gather | solution.py:130
  13.3 1.3 convert_element_type.585
  14.6 10.9 %all_gather.10 = bf16[2,256,768]{2,1,0:T(8,128)(2,1)S(1)} all-gather(bf16[1,256,768]{2,1,0:T(8,128)(2,1)} %param.17), channel_id=1, replica_groups=mesh['pipe'=2,'dp'=4,'inner'=4] {'pipe'}, dimensions={0}, use_global_device_ids=true | all-gather | bytes 1179648 | tf_op jit(solution)/shard_map/all_gather | solution.py:131
  32.0 1.5 reshape.1853
  33.5 1.4 fusion.196
  35.5 5.9 %all_gather.11 = bf16[2,256,256]{2,1,0:T(8,128)(2,1)S(1)} all-gather(bf16[1,256,256]{2,1,0:T(8,128)(2,1)} %param.18), channel_id=1, replica_groups=mesh['pipe'=2,'dp'=4,'inner'=4] {'pipe'}, dimensions={0}, use_global_device_ids=true | all-gather | bytes 393216 | tf_op jit(solution)/shard_map/all_gather | solution.py:134
  41.4 2.4 reshape.1849
  47.0 1.7 copy.450
  49.5 4.4 %multiply_reduce_fusion.15 = (f32[12,8,16]{2,1,0:T(8,128)S(1)}, f32[12,8,16,32]{3,2,1,0:T(8,128)S(1)}) fusion(f32[32]{0:T(128)S(1)} %or_convert_fusion.1, f32[12,32,8,32]{3,2,1,0:T(8,128)} %reshape.1853, f32[12,32,8]{1,2,0:T(8,128)S(1)} %add_rsqrt_fusion.2, f32[12,16,8,32]{3,2,1,0:T(8,128)S(1)} %copy-done.6, f32[12,16,8]{1,2,0:T(8,128)S(1)} %add_rsqrt_fusion.3), kind=kOutput, calls=%fused_computation.179 | convolution fusion | flops 19167744 | bytes 811136 | tf_op jit(solution)/shard_map/jvp(ohbyv,ohsyv->ohybs)/dot_general | solution.py:59
  57.8 5.3 %all-to-all-start = ((bf16[1,4,4,12,256]{4,2,3,0,1:T(4,128)(2,1)}), bf16[1,4,4,12,256]{4,2,3,0,1:T(4,128)(2,1)}, u32[]{:S(2)}, u32[]{:S(2)}) async-start(bf16[1,4,4,12,256]{4,2,3,0,1:T(4,128)(2,1)} %copy.454), calls=%async_computation | async-start | bytes 196608 | tf_op jit(solution)/shard_map/all_to_all | solution.py:154
  68.1 1.4 reshape.1866
  69.4 2.6 reshape.1865
  73.2 2.2 reshape.1861
  75.5 2.0 multiply_reduce_fusion.10
  77.5 1.6 copy.467
  79.1 1.4 add_rsqrt_fusion.1
  81.7 1.6 copy.469
  84.2 4.7 %multiply_reduce_fusion.14 = (f32[12,8,16]{2,1,0:T(8,128)S(1)}, f32[12,8,16,32]{3,2,1,0:T(8,128)S(1)}) fusion(f32[32]{0:T(128)} %or_convert_fusion, f32[12,32,8,32]{3,2,1,0:T(8,128)} %reshape.1865, f32[12,32,8]{1,2,0:T(8,128)S(1)} %add_rsqrt_fusion, f32[12,16,8,32]{3,2,1,0:T(8,128)} %reshape.1863, f32[12,16,8]{1,2,0:T(8,128)} %add_rsqrt_fusion.1), kind=kOutput, calls=%fused_computation.178 | convolution fusion | flops 19167744 | bytes 811136 | tf_op jit(solution)/shard_map/jvp(ohbyv,ohsyv->ohybs)/dot_general | solution.py:59
  90.9 1.9 convert_element_type.626
  92.9 1.8 fusion.62
  95.1 1.6 copy.510
  98.9 1.3 fusion.182
  100.2 5.5 %all-to-all-start.1 = ((bf16[1,4,4,12,256]{4,2,3,0,1:T(4,128)(2,1)}), bf16[1,4,4,12,256]{4,2,3,0,1:T(4,128)(2,1)S(1)}, u32[]{:S(2)}, u32[]{:S(2)}) async-start(bf16[1,4,4,12,256]{4,2,3,0,1:T(4,128)(2,1)} %copy.473), calls=%async_computation.1 | async-start | bytes 196608 | tf_op jit(solution)/shard_map/all_to_all | solution.py:154
  108.1 3.4 all-to-all-done.1
  120.5 2.0 reshape.1857
  125.7 2.0 reshape.1859
  133.8 1.8 copy.598
  137.5 1.4 broadcast_multiply_fusion.3
  141.7 1.4 broadcast_multiply_fusion.2
  146.5 1.4 broadcast_multiply_fusion.1
  149.8 1.4 broadcast_multiply_fusion
  152.3 2.7 fusion.199
  157.1 2.6 fusion.198
  161.5 9.6 %all-reduce.18 = (f32[1,4,12]{2,1,0:T(4,128)S(1)}, f32[1,4,12]{2,1,0:T(4,128)S(1)}) all-reduce(f32[1,4,12]{2,1,0:T(4,128)S(1)} %reduce_sum.391, f32[1,4,12]{2,1,0:T(4,128)S(1)} %reduce_sum.408), channel_id=1, replica_groups=mesh['pipe'=2,'dp'=4,'inner'=4] {'inner'}, use_global_device_ids=true, to_apply=%region_9.10 | all-reduce | flops 96 | bytes 768 | tf_op jit(solution)/shard_map/psum | solution.py:159
  171.5 1.3 fusion.164
  172.8 1.9 fusion.45
  175.9 1.9 copy.515
  177.9 1.6 convolution_convert_fusion.8
  180.5 1.8 fusion.124
  189.7 1.6 convolution_convert_fusion.9
  197.9 1.8 fusion.202
  199.6 1.7 fusion.203
  201.4 3.3 multiply_reduce_fusion.17
  206.0 1.5 multiply_reduce_fusion.19
  211.0 3.3 all-to-all-start.2
  214.4 2.2 add_bitcast_fusion
  216.5 1.8 fusion.178
  221.2 5.0 %all-to-all-start.3 = ((bf16[1,4,4,12,256]{4,2,3,0,1:T(4,128)(2,1)}), bf16[1,4,4,12,256]{4,2,3,0,1:T(4,128)(2,1)S(1)}, u32[]{:S(2)}, u32[]{:S(2)}) async-start(bf16[1,4,4,12,256]{4,2,3,0,1:T(4,128)(2,1)} %bitcast.103), calls=%async_computation.3 | async-start | bytes 196608 | tf_op jit(solution)/shard_map/all_to_all | solution.py:164
  228.4 3.7 all-to-all-done.3
  233.0 2.4 convolution_convert_fusion
  237.2 2.1 multiply_reduce_fusion.2
  240.8 1.9 reshape.1898
  242.7 2.0 fusion.21
  244.7 1.7 fusion.55
  246.5 3.3 fusion
  253.5 1.6 convolution_convert_fusion.1
  256.8 2.4 multiply_reduce_fusion.5
  260.7 2.0 reshape.1885
  262.7 1.3 fusion.20
  265.1 4.5 %fusion.1 = (f32[12,32,8]{1,2,0:T(8,128)S(1)}, f32[12,8,32,32]{2,3,1,0:T(8,128)S(1)}) fusion(f32[1,12,32,8,32]{2,4,3,1,0:T(8,128)S(1)} %copy-done, f32[12,16,8,32]{3,2,1,0:T(8,128)S(1)} %copy-done.7, f32[12,16,8]{1,2,0:T(8,128)S(1)} %copy-done.73, f32[12,8,16,32]{3,2,1,0:T(8,128)S(1)} %copy-done.9, f32[12,8,16,32]{3,2,1,0:T(8,128)} %copy-done.35, ...), kind=kOutput, calls=%fused_computation.8 | convolution fusion | flops 19362816 | bytes 1407104 | tf_op jit(solution)/shard_map/transpose(jvp(ohbyv,ohsyv->ohybs))/dot_general | solution.py:59
  275.7 1.3 pad_maximum_fusion
  279.4 40.4 %all-reduce.16 = (f32[4]{0:T(128)}, f32[16,256]{1,0:T(8,128)}, f32[2,256]{1,0:T(2,128)S(1)}, f32[256]{0:T(256)}) all-reduce(f32[4]{0:T(128)S(1)} %copy-done.195, f32[16,256]{1,0:T(8,128)S(1)} %add.366, f32[2,256]{1,0:T(2,128)S(1)} %pad_maximum_fusion.6, ...), channel_id=1, replica_groups=mesh['pipe'=2,'dp'=4,'inner'=4] {'pipe','dp','inner'}, use_global_device_ids=true, to_apply=%region_22.23 | all-reduce | flops 4868 | bytes 38944 | tf_op jit(solution)/shard_map/psum | solution.py:180
  320.3 90.1 %all-reduce.21.cloned.1.call-done = (f32[2,256,768]{2,1,0:T(8,128)}, f32[2,256,256]{2,1,0:T(8,128)}) async-done(((f32[2,256,768]{2,1,0:T(8,128)}, f32[2,256,256]{2,1,0:T(8,128)}), (f32[2,256,768]{2,1,0:T(8,128)}, f32[2,256,256]{2,1,0:T(8,128)})) %all-reduce.21.cloned.1.call-update) | async-done | bytes 2097168 | tf_op jit(solution)/shard_map/psum | solution.py:180
  410.4 2.1 constant_dynamic-slice_fusion.1
  (602 shorter events, 108.8 us)
Async XLA Ops:
  7.2 18.4 %copy-start.198 = (s32[4,16]{1,0:T(4,128)S(1)}, s32[4,16]{1,0:T(4,128)}, u32[]{:S(2)}) copy-start(s32[4,16]{1,0:T(4,128)} %param.11) | copy-start | bytes 772
  7.2 18.6 %copy-start.143 = (bf16[4,12,16,256]{3,2,1,0:T(8,128)(2,1)S(1)}, bf16[4,12,16,256]{3,2,1,0:T(8,128)(2,1)}, u32[]{:S(2)}) copy-start(bf16[4,12,16,256]{3,2,1,0:T(8,128)(2,1)} %param.10) | copy-start | bytes 1179652
  13.3 16.4 %copy-start.156 = (f32[1,1,256]{2,1,0:T(1,128)}, f32[1,1,256]{2,1,0:T(1,128)S(1)}, u32[]{:S(2)}) copy-start(f32[1,1,256]{2,1,0:T(1,128)S(1)} %get-tuple-element.53) | copy-start | bytes 3076
  25.6 39.5 %copy-start.1 = (bf16[256,768]{1,0:T(8,128)(2,1)}, bf16[256,768]{1,0:T(8,128)(2,1)S(1)}, u32[]{:S(2)}) copy-start(bf16[256,768]{1,0:T(8,128)(2,1)S(1)} %get-tuple-element.33) | copy-start | bytes 1179652
  30.4 13.4 %copy-start.3 = (f32[1,12,16,8,32]{4,3,2,1,0:T(8,128)}, f32[1,12,16,8,32]{4,3,2,1,0:T(8,128)S(1)}, u32[]{:S(2)}) copy-start(f32[1,12,16,8,32]{4,3,2,1,0:T(8,128)S(1)} %reshape.1852) | copy-start | bytes 589828
  35.5 18.4 %copy-start.183 = (f32[32]{0:T(128)}, f32[32]{0:T(128)S(1)}, u32[]{:S(2)}) copy-start(f32[32]{0:T(128)S(1)} %or_convert_fusion.1) | copy-start | bytes 388
  41.4 14.5 %copy-start.21 = (bf16[2,256,256]{2,1,0:T(8,128)(2,1)}, bf16[2,256,256]{2,1,0:T(8,128)(2,1)S(1)}, u32[]{:S(2)}) copy-start(bf16[2,256,256]{2,1,0:T(8,128)(2,1)S(1)} %all_gather.11) | copy-start | bytes 786436
  44.7 4.7 %copy-start.6 = (f32[12,16,8,32]{3,2,1,0:T(8,128)S(1)}, f32[12,16,8,32]{3,2,1,0:T(8,128)}, u32[]{:S(2)}) copy-start(f32[12,16,8,32]{3,2,1,0:T(8,128)} %reshape.1851) | copy-start | bytes 589828
  45.8 8.1 %copy-start.71 = (f32[12,16,8]{1,2,0:T(8,128)}, f32[12,16,8]{1,2,0:T(8,128)S(1)}, u32[]{:S(2)}) copy-start(f32[12,16,8]{1,2,0:T(8,128)S(1)} %add_rsqrt_fusion.3) | copy-start | bytes 18436
  49.4 4.4 %copy-start.88 = (f32[12,32,8]{1,2,0:T(8,128)}, f32[12,32,8]{1,2,0:T(8,128)S(1)}, u32[]{:S(2)}) copy-start(f32[12,32,8]{1,2,0:T(8,128)S(1)} %add_rsqrt_fusion.2) | copy-start | bytes 36868
  49.5 4.5 %copy-start.29 = (bf16[12,32,8,32]{3,2,1,0:T(8,128)(2,1)S(1)}, bf16[12,32,8,32]{3,2,1,0:T(8,128)(2,1)}, u32[]{:S(2)}) copy-start(bf16[12,32,8,32]{3,2,1,0:T(8,128)(2,1)} %reshape.1849) | copy-start | bytes 589828
  54.9 8.2 %copy-start.46 = (f32[12,16,256]{2,1,0:T(8,128)S(1)}, f32[12,16,256]{2,1,0:T(8,128)}, u32[]{:S(2)}) copy-start(f32[12,16,256]{2,1,0:T(8,128)} %copy-done.45) | copy-start | bytes 589828
  54.9 8.2 %copy-start.82 = (f32[12,16,256]{2,1,0:T(8,128)S(1)}, f32[12,16,256]{2,1,0:T(8,128)}, u32[]{:S(2)}) copy-start(f32[12,16,256]{2,1,0:T(8,128)} %get-tuple-element.34) | copy-start | bytes 589828
  54.9 8.2 %copy-start.157 = (f32[1,1,256]{2,1,0:T(1,128)S(1)}, f32[1,1,256]{2,1,0:T(1,128)}, u32[]{:S(2)}) copy-start(f32[1,1,256]{2,1,0:T(1,128)} %copy-done.156) | copy-start | bytes 3076
  55.9 9.1 %copy-start.70 = (f32[1,12,32,256]{3,2,1,0:T(8,128)S(1)}, f32[1,12,32,256]{3,2,1,0:T(8,128)}, u32[]{:S(2)}) copy-start(f32[1,12,32,256]{3,2,1,0:T(8,128)} %get-tuple-element.40) | copy-start | bytes 1179652
  57.8 42.4 %all-to-all-start = ((bf16[1,4,4,12,256]{4,2,3,0,1:T(4,128)(2,1)}), bf16[1,4,4,12,256]{4,2,3,0,1:T(4,128)(2,1)}, u32[]{:S(2)}, u32[]{:S(2)}) async-start(bf16[1,4,4,12,256]{4,2,3,0,1:T(4,128)(2,1)} %copy.454), calls=%async_computation | async-start | bytes 196608 | tf_op jit(solution)/shard_map/all_to_all | solution.py:154
  84.2 4.7 %copy-start.95 = (f32[12,32,8]{1,2,0:T(8,128)}, f32[12,32,8]{1,2,0:T(8,128)S(1)}, u32[]{:S(2)}) copy-start(f32[12,32,8]{1,2,0:T(8,128)S(1)} %add_rsqrt_fusion) | copy-start | bytes 36868
  84.2 5.4 %copy-start.31 = (bf16[12,32,8,32]{3,2,1,0:T(8,128)(2,1)S(1)}, bf16[12,32,8,32]{3,2,1,0:T(8,128)(2,1)}, u32[]{:S(2)}) copy-start(bf16[12,32,8,32]{3,2,1,0:T(8,128)(2,1)} %reshape.1861) | copy-start | bytes 589828
  84.2 5.4 %copy-start.186 = (f32[32]{0:T(128)S(1)}, f32[32]{0:T(128)}, u32[]{:S(2)}) copy-start(f32[32]{0:T(128)} %or_convert_fusion) | copy-start | bytes 388
  97.2 16.1 %copy-start.173 = (f32[1,1,256]{2,1,0:T(1,128)S(1)}, f32[1,1,256]{2,1,0:T(1,128)}, u32[]{:S(2)}) copy-start(f32[1,1,256]{2,1,0:T(1,128)} %get-tuple-element.52) | copy-start | bytes 3076
  100.2 11.3 %all-to-all-start.1 = ((bf16[1,4,4,12,256]{4,2,3,0,1:T(4,128)(2,1)}), bf16[1,4,4,12,256]{4,2,3,0,1:T(4,128)(2,1)S(1)}, u32[]{:S(2)}, u32[]{:S(2)}) async-start(bf16[1,4,4,12,256]{4,2,3,0,1:T(4,128)(2,1)} %copy.473), calls=%async_computation.1 | async-start | bytes 196608 | tf_op jit(solution)/shard_map/all_to_all | solution.py:154
  108.1 5.4 %copy-start.165 = (f32[4,48]{1,0:T(4,128)}, f32[4,48]{1,0:T(4,128)S(1)}, u32[]{:S(2)}) copy-start(f32[4,48]{1,0:T(4,128)S(1)} %rsqrt.141) | copy-start | bytes 2308
  132.7 3.9 copy-start.107
  136.6 19.1 %copy-start.61 = (bf16[4,48,256]{1,2,0:T(8,128)(2,1)}, bf16[4,48,256]{1,2,0:T(8,128)(2,1)S(1)}, u32[]{:S(2)}) copy-start(bf16[4,48,256]{1,2,0:T(8,128)(2,1)S(1)} %copy.599) | copy-start | bytes 294916
  140.9 4.2 copy-start.121
  149.7 5.3 %copy-start.123 = (f32[4,48,8]{1,2,0:T(8,128)}, f32[4,48,8]{1,2,0:T(8,128)S(1)}, u32[]{:S(2)}) copy-start(f32[4,48,8]{1,2,0:T(8,128)S(1)} %add_rsqrt_fusion.4) | copy-start | bytes 18436
  155.0 22.8 %copy-start.152 = (f32[4,8,48]{2,1,0:T(8,128)}, f32[4,8,48]{2,1,0:T(8,128)S(1)}, u32[]{:S(2)}) copy-start(f32[4,8,48]{2,1,0:T(8,128)S(1)} %get-tuple-element.74) | copy-start | bytes 18436
  156.4 4.3 %copy-start.43 = (f32[4,48,256]{2,1,0:T(8,128)}, f32[4,48,256]{2,1,0:T(8,128)S(1)}, u32[]{:S(2)}) copy-start(f32[4,48,256]{2,1,0:T(8,128)S(1)} %convolution_add_fusion) | copy-start | bytes 589828
  160.5 11.0 %copy-start.196 = (s32[48]{0:T(128)S(1)}, s32[48]{0:T(128)}, u32[]{:S(2)}) copy-start(s32[48]{0:T(128)} %get-tuple-element.50) | copy-start | bytes 580
  160.5 11.0 %copy-start.197 = (s32[48]{0:T(128)S(1)}, s32[48]{0:T(128)}, u32[]{:S(2)}) copy-start(s32[48]{0:T(128)} %get-tuple-element.51) | copy-start | bytes 580
  160.5 11.0 %copy-start.199 = (s32[4]{0:T(128)S(1)}, s32[4]{0:T(128)}, u32[]{:S(2)}) copy-start(s32[4]{0:T(128)} %iota_add_fusion.1) | copy-start | bytes 52
  161.0 18.5 %copy-start.44 = (f32[4,48,256]{2,1,0:T(8,128)}, f32[4,48,256]{2,1,0:T(8,128)S(1)}, u32[]{:S(2)}) copy-start(f32[4,48,256]{2,1,0:T(8,128)S(1)} %convolution_add_fusion.2) | copy-start | bytes 589828
  172.8 6.8 %copy-start.163 = (f32[4,48]{1,0:T(4,128)}, f32[4,48]{1,0:T(4,128)S(1)}, u32[]{:S(2)}) copy-start(f32[4,48]{1,0:T(4,128)S(1)} %get-tuple-element.47) | copy-start | bytes 2308
  177.9 5.3 %copy-start.27 = (f32[4,8,48,48]{2,3,1,0:T(8,128)S(1)}, f32[4,8,48,48]{2,3,1,0:T(8,128)}, u32[]{:S(2)}) copy-start(f32[4,8,48,48]{2,3,1,0:T(8,128)} %copy-done.26) | copy-start | bytes 884740
  177.9 5.3 %copy-start.62 = (bf16[4,48,256]{1,2,0:T(8,128)(2,1)S(1)}, bf16[4,48,256]{1,2,0:T(8,128)(2,1)}, u32[]{:S(2)}) copy-start(bf16[4,48,256]{1,2,0:T(8,128)(2,1)} %copy-done.61) | copy-start | bytes 294916
  177.9 5.3 %copy-start.63 = (bf16[4,8,32,48]{3,2,1,0:T(8,128)(2,1)S(1)}, bf16[4,8,32,48]{3,2,1,0:T(8,128)(2,1)}, u32[]{:S(2)}) copy-start(bf16[4,8,32,48]{3,2,1,0:T(8,128)(2,1)} %copy.515) | copy-start | bytes 294916
  177.9 5.3 %copy-start.155 = (f32[4,8,48]{2,1,0:T(8,128)S(1)}, f32[4,8,48]{2,1,0:T(8,128)}, u32[]{:S(2)}) copy-start(f32[4,8,48]{2,1,0:T(8,128)} %multiply_divide_fusion.2) | copy-start | bytes 18436
  201.4 4.5 %copy-start.79 = (f32[4,8,48,48]{2,3,1,0:T(8,128)S(1)}, f32[4,8,48,48]{2,3,1,0:T(8,128)}, u32[]{:S(2)}) copy-start(f32[4,8,48,48]{2,3,1,0:T(8,128)} %copy-done.78) | copy-start | bytes 884740
  209.1 5.3 %copy-start.87 = (bf16[256,256]{1,0:T(8,128)(2,1)S(1)}, bf16[256,256]{1,0:T(8,128)(2,1)}, u32[]{:S(2)}) copy-start(bf16[256,256]{1,0:T(8,128)(2,1)} %fusion.23) | copy-start | bytes 393220
  210.0 9.0 %copy-start.189 = (f32[1,256,1]{1,0,2:T(1,128)S(1)}, f32[1,256,1]{1,0,2:T(1,128)}, u32[]{:S(2)}) copy-start(f32[1,256,1]{1,0,2:T(1,128)} %fusion.202) | copy-start | bytes 3076
  210.0 9.0 %copy-start.190 = (f32[1,256,1]{1,0,2:T(1,128)S(1)}, f32[1,256,1]{1,0,2:T(1,128)}, u32[]{:S(2)}) copy-start(f32[1,256,1]{1,0,2:T(1,128)} %fusion.203) | copy-start | bytes 3076
  210.0 9.6 %copy-start.191 = (f32[256]{0:T(256)S(1)}, f32[256]{0:T(256)}, u32[]{:S(2)}) copy-start(f32[256]{0:T(256)} %get-tuple-element.12) | copy-start | bytes 3076
  210.1 9.6 %copy-start.192 = (f32[256]{0:T(256)S(1)}, f32[256]{0:T(256)}, u32[]{:S(2)}) copy-start(f32[256]{0:T(256)} %get-tuple-element.61) | copy-start | bytes 3076
  210.1 10.1 %copy-start.55 = (bf16[4,8,32,48]{3,2,1,0:T(8,128)(2,1)S(1)}, bf16[4,8,32,48]{3,2,1,0:T(8,128)(2,1)}, u32[]{:S(2)}) copy-start(bf16[4,8,32,48]{3,2,1,0:T(8,128)(2,1)} %copy-done.54) | copy-start | bytes 294916
  210.1 10.1 %copy-start.57 = (f32[256,256]{1,0:T(8,128)S(1)}, f32[256,256]{1,0:T(8,128)}, u32[]{:S(2)}) copy-start(f32[256,256]{1,0:T(8,128)} %fusion.45) | copy-start | bytes 786436
  210.1 10.1 %copy-start.162 = (f32[4,48]{1,0:T(4,128)S(1)}, f32[4,48]{1,0:T(4,128)}, u32[]{:S(2)}) copy-start(f32[4,48]{1,0:T(4,128)} %get-tuple-element.46) | copy-start | bytes 2308
  210.1 10.1 %copy-start.172 = (f32[256]{0:T(256)S(1)}, f32[256]{0:T(256)}, u32[]{:S(2)}) copy-start(f32[256]{0:T(256)} %param.19) | copy-start | bytes 3076
  211.0 10.2 %all-to-all-start.2 = ((bf16[1,4,4,12,256]{4,2,3,0,1:T(4,128)(2,1)}), bf16[1,4,4,12,256]{4,2,3,0,1:T(4,128)(2,1)S(1)}, u32[]{:S(2)}, u32[]{:S(2)}) async-start(bf16[1,4,4,12,256]{4,2,3,0,1:T(4,128)(2,1)} %bitcast.69), calls=%async_computation.2 | async-start | bytes 196608 | tf_op jit(solution)/shard_map/all_to_all | solution.py:164
  214.4 12.2 %copy-start.113 = (bf16[12,16,256]{2,1,0:T(8,128)(2,1)S(1)}, bf16[12,16,256]{2,1,0:T(8,128)(2,1)}, u32[]{:S(2)}) copy-start(bf16[12,16,256]{2,1,0:T(8,128)(2,1)} %convert_element_type.598) | copy-start | bytes 294916
  221.2 10.9 %all-to-all-start.3 = ((bf16[1,4,4,12,256]{4,2,3,0,1:T(4,128)(2,1)}), bf16[1,4,4,12,256]{4,2,3,0,1:T(4,128)(2,1)S(1)}, u32[]{:S(2)}, u32[]{:S(2)}) async-start(bf16[1,4,4,12,256]{4,2,3,0,1:T(4,128)(2,1)} %bitcast.103), calls=%async_computation.3 | async-start | bytes 196608 | tf_op jit(solution)/shard_map/all_to_all | solution.py:164
  226.2 184.1 %all-reduce.21.cloned.1.call-start = ((), (), s32[]{:S(2)}) async-start(), calls=%async_computation.4 | async-start | bytes 4194304 | tf_op jit(solution)/shard_map/psum | solution.py:180
  226.5 6.5 %copy-start.12 = (f32[12,8,16,32]{3,2,1,0:T(8,128)S(1)}, f32[12,8,16,32]{3,2,1,0:T(8,128)}, u32[]{:S(2)}) copy-start(f32[12,8,16,32]{3,2,1,0:T(8,128)} %copy-done.11) | copy-start | bytes 589828
  226.5 5.8 %copy-start.65 = (bf16[1,16,12,256]{3,1,2,0:T(8,128)(2,1)}, bf16[1,16,12,256]{3,1,2,0:T(8,128)(2,1)S(1)}, u32[]{:S(2)}) copy-start(bf16[1,16,12,256]{3,1,2,0:T(8,128)(2,1)S(1)} %reshape.1879) | copy-start | bytes 294916
  239.9 4.8 %copy-start.2 = (bf16[256,768]{1,0:T(8,128)(2,1)S(1)}, bf16[256,768]{1,0:T(8,128)(2,1)}, u32[]{:S(2)}) copy-start(bf16[256,768]{1,0:T(8,128)(2,1)} %copy-done.1) | copy-start | bytes 1179652
  239.9 6.6 %copy-start.10 = (f32[12,16,8,32]{3,2,1,0:T(8,128)S(1)}, f32[12,16,8,32]{3,2,1,0:T(8,128)}, u32[]{:S(2)}) copy-start(f32[12,16,8,32]{3,2,1,0:T(8,128)} %reshape.1863) | copy-start | bytes 589828
  242.7 3.7 copy-start.34
  242.7 3.7 copy-start.75
  242.7 3.7 copy-start.100
  242.7 3.8 copy-start.116
  242.7 3.8 copy-start.188
  259.8 5.2 %copy-start = (f32[1,12,32,8,32]{2,4,3,1,0:T(8,128)S(1)}, f32[1,12,32,8,32]{2,4,3,1,0:T(8,128)}, u32[]{:S(2)}) copy-start(f32[1,12,32,8,32]{2,4,3,1,0:T(8,128)} %copy.510) | copy-start | bytes 1179652
  259.8 5.2 %copy-start.7 = (f32[12,16,8,32]{3,2,1,0:T(8,128)S(1)}, f32[12,16,8,32]{3,2,1,0:T(8,128)}, u32[]{:S(2)}) copy-start(f32[12,16,8,32]{3,2,1,0:T(8,128)} %reshape.1851) | copy-start | bytes 589828
  265.1 4.5 %copy-start.104 = (f32[12,32,8]{1,2,0:T(8,128)S(1)}, f32[12,32,8]{1,2,0:T(8,128)}, u32[]{:S(2)}) copy-start(f32[12,32,8]{1,2,0:T(8,128)} %copy.450) | copy-start | bytes 36868
  265.1 4.6 %copy-start.90 = (f32[12,32,8]{1,2,0:T(8,128)S(1)}, f32[12,32,8]{1,2,0:T(8,128)}, u32[]{:S(2)}) copy-start(f32[12,32,8]{1,2,0:T(8,128)} %copy-done.88) | copy-start | bytes 36868
  (142 other events, 263.4 us)
Sparse Core Ops, SparseCore 0:
  277.1 133.1 all-reduce.20
where the time goes:
time: 428 us; the launch traced here: 420 us
  waiting for transfers between devices  97.2 us (23%)
  matrix products  86.5 us (20%)
  local copies, waits for them, and re-layouts  84.2 us (20%)
  blocking collectives  72.2 us (17%)
  other arithmetic  42.6 us (10%)
  starting transfers between devices  19.4 us (5%)
  between operations  18.4 us (4%)
    psum x1, waiting for transfers between devices, shards(): lax.psum((stacked[0], stacked[1], stacked[2], stacked[3], stacked[4], sta...  90.1 us
    psum x1, blocking collectives, shards(): lax.psum((stacked[0], stacked[1], stacked[2], stacked[3], stacked[4], sta...  40.4 us
    dot_general x48, matrix products, matmul_f32(): jnp.einsum('...d,de->...e', left_side, right_side.astype(jnp.bfloat16), p...  38.3 us
    reshape x22, local copies, waits for them, and re-layouts, unit_heads(): values.reshape(values.shape[:-1] + (HEADS, values.shape[-1] // HEADS))  24.9 us
    dot_general x6, matrix products, temporal(): jnp.einsum('ohbyv,ohsyv->ohybs', probe_entry_lines, lookup_entry_lines, p...  21.4 us
    another operation x9, local copies, waits for them, and re-layouts  14.3 us
    dot_general x6, matrix products, spatial(): jnp.einsum('wisbx,wiqbx->wibsq', probe_entry_lines, lookup_entry_lines, p...  12.1 us
    all_gather x1, blocking collectives, shards(): lax.all_gather(segment_probe_lookup_content.astype(jnp.float32), 'pipe',...  10.9 us
  transfers between devices with their start and end apart: 5, of which 3 were waited for; matrix products, arithmetic and copies ran while one was open for 12% of the time, Pallas kernels for 0%

commit v1 on v0

--- a/solution.py
+++ b/solution.py
@@ -1,8 +1,11 @@
+import functools
 import math
 
 import jax
 import jax.numpy as jnp
 from jax import lax
+from jax.experimental import pallas as pl
+from jax.experimental.pallas import tpu as pltpu
 from jax.sharding import PartitionSpec as P
 
 HEADS = 8
@@ -105,7 +108,7 @@
     return logits.reshape(batch_count, classes, groups, patches)
 
 
-def shards(
+def shards_general(
     pixels,
     date_days,
     clear_count,
@@ -187,6 +190,639 @@
     return (summed[5], summed[3], gain_grad, qkv_grad, out_grad, summed[4])
 
 
+F32 = jnp.float32
+BF16 = jnp.bfloat16
+VMEM_LIMIT = 56 * 2**20
+
+
+def params(**kw):
+    return pltpu.CompilerParams(vmem_limit_bytes=VMEM_LIMIT, **kw)
+
+
+def vmem(count):
+    return [pl.BlockSpec(memory_space=pltpu.VMEM)] * count
+
+
+def mm(a, b, ca=1, cb=0):
+    return lax.dot_general(a, b, (((ca,), (cb,)), ((), ())), preferred_element_type=F32)
+
+
+def split(a):
+    hi = a.astype(BF16)
+    return hi, (a - hi.astype(F32)).astype(BF16)
+
+
+def mm2(a, b, ca=1, cb=0):
+    hi, lo = split(a)
+    return mm(hi, b, ca, cb) + mm(lo, b, ca, cb)
+
+
+def mm2r(a, b, ca=1, cb=0):
+    hi, lo = split(b)
+    return mm(a, hi, ca, cb) + mm(a, lo, ca, cb)
+
+
+def mm3(a, b, ca=1, cb=0):
+    ah, al = split(a)
+    bh, bl = split(b)
+    return mm(ah, bh, ca, cb) + (mm(ah, bl, ca, cb) + mm(al, bh, ca, cb))
+
+
+def same_block(rows, cols, size):
+    r = lax.broadcasted_iota(jnp.int32, (rows, cols), 0) // size
+    c = lax.broadcasted_iota(jnp.int32, (rows, cols), 1) // size
+    return (r == c).astype(F32)
+
+
+def head_ones(width):
+    return same_block(width, width, width // HEADS).astype(BF16)
+
+
+def head_mask(width):
+    h = lax.broadcasted_iota(jnp.int32, (HEADS, 1, width), 0)
+    c = lax.broadcasted_iota(jnp.int32, (HEADS, 1, width), 2) // (width // HEADS)
+    return (h == c).astype(F32)
+
+
+def unit(x, ones):
+    r = lax.rsqrt(mm2(x * x, ones) + head_eps)
+    return x * r, r
+
+
+def unit_back(dxn, xn, r, ones):
+    return r * (dxn - xn * mm2(dxn * xn, ones))
+
+
+def norm_scale(x):
+    return lax.rsqrt(jnp.mean(x * x, axis=-1, keepdims=True) + norm_eps)
+
+
+def rounded(x):
+    return x.astype(BF16).astype(F32)
+
+
+def expand_heads(x, hm):
+    n, d = x.shape
+    return (x[None] * hm).reshape(HEADS * n, d)
+
+
+def fold_heads(x, hm):
+    n = x.shape[0] // HEADS
+    return jnp.sum(x.reshape(HEADS, n, x.shape[1]) * hm, axis=0)
+
+
+def permutation(n, outer):
+    inner = n // outer
+    r = lax.broadcasted_iota(jnp.int32, (n, n), 0)
+    c = lax.broadcasted_iota(jnp.int32, (n, n), 1)
+    return (c == (r % inner) * outer + r // inner).astype(F32).astype(BF16)
+
+
+def date_sequence(pix, enc):
+    return (pix.astype(F32) + enc[:, None]).reshape(-1, pix.shape[-1])
+
+
+def temporal_fwd(pix_ref, enc_ref, mask_ref, cls_ref, gain_ref, w_ref, wo_ref,
+                 send_ref, nd_ref, kn_ref, rk_ref, v_ref, ad_ref, ac_ref, att_ref, cq_ref):
+    d = pix_ref.shape[-1]
+    dates = pix_ref.shape[2]
+    classes = cls_ref.shape[0]
+    gain = gain_ref[...]
+    x = date_sequence(pix_ref[...], enc_ref[...])
+    rows = x.shape[0]
+    bps = rows // dates
+    nd = (x * norm_scale(x) * gain).astype(BF16)
+    nd_ref[...] = nd
+    cls = cls_ref[...].astype(F32)
+    nc = (cls * norm_scale(cls) * gain).astype(BF16)
+    ones = head_ones(d)
+    hm = head_mask(d)
+    kv = mm(nd, w_ref[:, d:])
+    qkvc = mm(nc, w_ref[...])
+    kn, rk = unit(kv[:, :d], ones)
+    kn_ref[...] = kn
+    rk_ref[...] = rk
+    v = kv[:, d:].astype(BF16)
+    v_ref[...] = v
+    qn, rq = unit(qkvc[:, :d], ones)
+    kcn, rkc = unit(qkvc[:, d : 2 * d], ones)
+    vc = qkvc[:, 2 * d :].astype(BF16)
+    cq_ref[0] = qn
+    cq_ref[1] = rq
+    cq_ref[2] = kcn
+    cq_ref[3] = rkc
+    cq_ref[4] = vc.astype(F32)
+    group = 128 // dates
+    qe = expand_heads(qn, hm)
+    kct = jnp.concatenate([kcn] * group, axis=0)
+    ed = jnp.exp(normalizer_sharpness * mm3(qe, kn, 1, 1)) * mask_ref[...]
+    ec = jnp.exp(normalizer_sharpness * mm3(qe, kct, 1, 1))
+    seg = same_block(128, 128, dates).astype(BF16)
+    sum_c = mm2(ec, seg)
+    vct = jnp.concatenate([vc] * group, axis=0)
+    bm = group_mask(group, dates)
+    atts = []
+    for g in range(bps // group):
+        lanes = slice(g * 128, (g + 1) * 128)
+        e = ed[:, lanes]
+        den = mm2(e, seg) + sum_c
+        ad = e / den
+        ac = ec / den
+        ad_ref[:, lanes] = ad
+        ac_ref[:, lanes] = ac
+        aexp = (jnp.concatenate([ad, ac], axis=1)[None] * bm).reshape(-1, 256).astype(BF16)
+        vst = jnp.concatenate([v[lanes], vct], axis=0)
+        o = mm(aexp, vst).reshape(group, HEADS, classes, d)
+        atts.append(jnp.sum(o * hm[None], axis=1).reshape(group * classes, d))
+    att = jnp.concatenate(atts, axis=0).astype(BF16)
+    att_ref[...] = att
+    upd = jnp.concatenate([cls] * bps, axis=0) + mm(att, wo_ref[...])
+    send_ref[...] = mm(permutation(rows, classes), upd.astype(BF16)).astype(BF16)
+
+
+def group_mask(group, dates):
+    g = lax.broadcasted_iota(jnp.int32, (group, 1, 256), 0)
+    c = (lax.broadcasted_iota(jnp.int32, (group, 1, 256), 2) % 128) // dates
+    return (g == c).astype(F32)
+
+
+def temporal_bwd(back_ref, pix_ref, enc_ref, cls_ref, gain_ref, w_ref, wo_ref,
+                 nd_ref, kn_ref, rk_ref, v_ref, ad_ref, ac_ref, att_ref, cq_ref,
+                 dw_ref, dgain_ref, dcls_ref):
+    d = pix_ref.shape[-1]
+    dates = pix_ref.shape[2]
+    classes = cls_ref.shape[0]
+    gain = gain_ref[...]
+    x = date_sequence(pix_ref[...], enc_ref[...])
+    rows = x.shape[0]
+    bps = rows // dates
+    cls = cls_ref[...].astype(F32)
+    inv_c = norm_scale(cls)
+    nc = (cls * inv_c * gain).astype(BF16)
+    nd = nd_ref[...]
+    ones = head_ones(d)
+    hm = head_mask(d)
+    group = 128 // dates
+    du = mm(permutation(rows, rows // classes), back_ref[...]).astype(BF16)
+    dw_ref[:, 3 * d :] = mm(att_ref[...], du, 0, 0)
+    do = rounded(mm(du, wo_ref[...], 1, 1))
+    qn = cq_ref[0]
+    rq = cq_ref[1]
+    kcn = cq_ref[2]
+    rkc = cq_ref[3]
+    vct = jnp.concatenate([cq_ref[4].astype(BF16)] * group, axis=0)
+    kct = jnp.concatenate([kcn] * group, axis=0)
+    qe = expand_heads(qn, hm)
+    seg = same_block(128, 128, dates).astype(BF16)
+    bm = group_mask(group, dates)
+    qnt = jnp.concatenate([qn] * group, axis=0)
+    rqt = jnp.concatenate([rq] * group, axis=0)
+    rkct = jnp.concatenate([rkc] * group, axis=0)
+    w = w_ref[...]
+    wq, wk, wv = w[:, :d], w[:, d : 2 * d], w[:, 2 * d :]
+    nct = jnp.concatenate([nc] * group, axis=0)
+    dwq = jnp.zeros((d, d), F32)
+    dwk = jnp.zeros((d, d), F32)
+    dwv = jnp.zeros((d, d), F32)
+    dnc = jnp.zeros((classes, d), F32)
+    dgain = jnp.zeros((1, d), F32)
+    xhat = x * norm_scale(x)
+    for g in range(bps // group):
+        lanes = slice(g * 128, (g + 1) * 128)
+        ad = ad_ref[:, lanes]
+        ac = ac_ref[:, lanes]
+        a2 = jnp.concatenate([ad, ac], axis=1)
+        aexp = (a2[None] * bm).reshape(-1, 256).astype(BF16)
+        vst = jnp.concatenate([v_ref[lanes, :], vct], axis=0)
+        doe = (do[lanes].reshape(group, 1, classes, d) * hm[None]).reshape(-1, d).astype(BF16)
+        da = jnp.sum(mm(doe, vst, 1, 1).reshape(group, -1, 256) * bm, axis=0)
+        da = rounded(da)
+        dvst = mm(aexp, doe, 0, 0).astype(BF16)
+        prod = da * a2
+        dot = mm2(prod[:, :128] + prod[:, 128:], seg)
+        ds = normalizer_sharpness * a2 * (da - jnp.concatenate([dot, dot], axis=1))
+        kn = kn_ref[lanes, :]
+        kst = jnp.concatenate([kn, kct], axis=0)
+        dse = (ds[None] * bm).reshape(-1, 256)
+        dqn = jnp.sum(mm3(dse, kst).reshape(group, HEADS, classes, d) * hm[None], axis=1)
+        dqn = dqn.reshape(group * classes, d)
+        dkst = mm3(ds, qe, 0, 0)
+        dq = unit_back(dqn, qnt, rqt, ones)
+        dk = unit_back(dkst[:128], kn, rk_ref[lanes, :], ones)
+        dkc = unit_back(dkst[128:], kct, rkct, ones)
+        ndg = nd[lanes]
+        dwq += mm2r(nct, dq, 0, 0)
+        dwk += mm2r(ndg, dk, 0, 0) + mm2r(nct, dkc, 0, 0)
+        dwv += mm(ndg, dvst[:128], 0, 0) + mm(nct, dvst[128:], 0, 0)
+        dn_k = rounded(mm2(jnp.concatenate([dk, dkc], axis=0), wk, 1, 1))
+        dn = rounded(rounded(mm(dvst, wv, 1, 1)) + dn_k)
+        dn_c = rounded(dn[128:] + rounded(mm2(dq, wq, 1, 1)))
+        dgain += jnp.sum(dn[:128] * xhat[lanes], axis=0, keepdims=True)
+        dnc += jnp.sum(dn_c.reshape(group, classes, d), axis=0)
+    dw_ref[:, :d] = dwq
+    dw_ref[:, d : 2 * d] = dwk
+    dw_ref[:, 2 * d : 3 * d] = dwv
+    dgain_ref[...] = dgain + jnp.sum(dnc * cls * inv_c, axis=0, keepdims=True)
+    t = dnc * gain
+    dcls = inv_c * (t - cls * (inv_c * inv_c * jnp.mean(t * cls, axis=-1, keepdims=True)))
+    dcls_ref[...] = dcls + jnp.sum(du.astype(F32).reshape(bps, classes, d), axis=0)
+
+
+def spatial_rows(recv_ref, kinds):
+    sources, rows, d = recv_ref.shape
+    n = rows // kinds
+    blocks = [recv_ref[s].astype(F32) for s in range(sources)]
+    return jnp.concatenate(
+        [blocks[s][k * n : (k + 1) * n] for k in range(kinds) for s in range(sources)], axis=0
+    )
+
+
+def spatial_fwd(kinds, tiles, recv_ref, gain_ref, w_ref, wo_ref, head_ref,
+                u_ref, n_ref, qk_ref, r_ref, v_ref, a_ref, o_ref, hid_ref, raw_ref, sum_ref):
+    d = recv_ref.shape[-1]
+    u = spatial_rows(recv_ref, kinds)
+    u_ref[...] = u
+    rows = u.shape[0]
+    n = (u * norm_scale(u) * gain_ref[...]).astype(BF16)
+    n_ref[...] = n
+    ones = head_ones(d)
+    hm = head_mask(d)
+    qkv = mm(n, w_ref[...])
+    qn, rq = unit(qkv[:, :d], ones)
+    kn, rk = unit(qkv[:, d : 2 * d], ones)
+    v = qkv[:, 2 * d :].astype(BF16)
+    qk_ref[0] = qn
+    qk_ref[1] = kn
+    r_ref[0] = rq
+    r_ref[1] = rk
+    v_ref[...] = v
+    per = rows // kinds
+    patches = per // (recv_ref.shape[0] * tiles)
+    ri = (lax.broadcasted_iota(jnp.int32, (per, per), 0) // patches) % tiles
+    ci = (lax.broadcasted_iota(jnp.int32, (per, per), 1) // patches) % tiles
+    tm = jnp.concatenate([(ri == ci).astype(F32)] * HEADS, axis=0)
+    outs = []
+    for k in range(kinds):
+        rs = slice(k * per, (k + 1) * per)
+        e = jnp.exp(normalizer_sharpness * mm3(expand_heads(qn[rs], hm), kn[rs], 1, 1)) * tm
+        a = e / jnp.sum(e, axis=-1, keepdims=True)
+        a_ref[k] = a
+        outs.append(fold_heads(mm(a.astype(BF16), v[rs]), hm))
+    o = jnp.concatenate(outs, axis=0).astype(BF16)
+    o_ref[...] = o
+    hid = u + mm(o, wo_ref[...])
+    hid_ref[...] = hid
+    raw = jnp.sum(hid * head_ref[...], axis=-1, keepdims=True)
+    raw = jnp.broadcast_to(raw, (rows, 128))
+    raw_ref[...] = raw
+    ex = jnp.exp(logit_cap * jnp.tanh(raw / logit_cap))
+    sum_ref[...] = jnp.sum(ex.reshape(kinds, per, 128), axis=0)
+
+
+def spatial_bwd(kinds, tiles, total_tiles, tot_ref, label_ref, slot_ref, gain_ref, w_ref, wo_ref, head_ref,
+                u_ref, n_ref, qk_ref, r_ref, v_ref, a_ref, o_ref, hid_ref, raw_ref,
+                send_ref, dw_ref, dgain_ref, dhead_ref, loss_ref):
+    d = u_ref.shape[-1]
+    rows = u_ref.shape[0]
+    per = rows // kinds
+    sources = tot_ref.shape[0]
+    total = jnp.sum(tot_ref[...], axis=0)
+    total = jnp.concatenate([total] * kinds, axis=0)
+    th = jnp.tanh(raw_ref[...] / logit_cap)
+    logits = logit_cap * th
+    kind = lax.broadcasted_iota(jnp.int32, (rows, 128), 0) // per
+    ind = (jnp.concatenate([label_ref[...]] * kinds, axis=0) == kind).astype(F32)
+    slot = jnp.concatenate([slot_ref[...]] * kinds, axis=0)
+    loss_ref[...] = jnp.sum(ind * (jnp.log(total) - logits) * slot, axis=0, keepdims=True)
+    draw = (jnp.exp(logits) / total - ind) / total_tiles * (1.0 - th * th)
+    dr = jnp.concatenate([draw] * (d // 128), axis=1)
+    head = head_ref[...]
+    dhead_ref[...] = jnp.sum(dr * hid_ref[...], axis=0, keepdims=True)
+    col = mm2r(o_ref[...], draw, 0, 0)
+    dw_ref[:, 3 * d :] = jnp.concatenate([col] * (d // 128), axis=1) * head
+    head_back = mm2(jnp.broadcast_to(head, (8, d)), wo_ref[...], 1, 1)[:1]
+    do = rounded(dr * head_back)
+    ones = head_ones(d)
+    hm = head_mask(d)
+    dqs, dks, dvs = [], [], []
+    for k in range(kinds):
+        rs = slice(k * per, (k + 1) * per)
+        a = a_ref[k]
+        doe = expand_heads(do[rs], hm).astype(BF16)
+        da = rounded(mm(doe, v_ref[rs, :], 1, 1))
+        dvs.append(mm(a.astype(BF16), doe, 0, 0))
+        ds = normalizer_sharpness * a * (da - jnp.sum(da * a, axis=-1, keepdims=True))
+        qn = qk_ref[0, rs, :]
+        kn = qk_ref[1, rs, :]
+        dqs.append(unit_back(fold_heads(mm3(ds, kn), hm), qn, r_ref[0, rs, :], ones))
+        dks.append(unit_back(mm3(ds, expand_heads(qn, hm), 0, 0), kn, r_ref[1, rs, :], ones))
+    dq = jnp.concatenate(dqs, axis=0)
+    dk = jnp.concatenate(dks, axis=0)
+    dv = jnp.concatenate(dvs, axis=0).astype(BF16)
+    n = n_ref[...]
+    dw_ref[:, :d] = mm2r(n, dq, 0, 0)
+    dw_ref[:, d : 2 * d] = mm2r(n, dk, 0, 0)
+    dw_ref[:, 2 * d : 3 * d] = mm(n, dv, 0, 0)
+    w = w_ref[...]
+    dn = rounded(rounded(mm(dv, w[:, 2 * d :], 1, 1)) + rounded(mm2(dk, w[:, d : 2 * d], 1, 1)))
+    dn = rounded(dn + rounded(mm2(dq, w[:, :d], 1, 1)))
+    u = u_ref[...]
+    inv = norm_scale(u)
+    dgain_ref[...] = jnp.sum(dn * u * inv, axis=0, keepdims=True)
+    t = dn * gain_ref[...]
+    du = dr * head + inv * (t - u * (inv * inv * jnp.mean(t * u, axis=-1, keepdims=True)))
+    m = per // sources
+    for s in range(sources):
+        parts = [du[k * per + s * m : k * per + (s + 1) * m] for k in range(kinds)]
+        send_ref[s] = jnp.concatenate(parts, axis=0).astype(BF16)
+
+
+MESH = pl.DeviceIdType.MESH
+
+
+def enter(devices):
+    barrier = pltpu.get_barrier_semaphore()
+    for dev in devices:
+        pl.semaphore_signal(barrier, inc=1, device_id=dev, device_id_type=MESH)
+    pl.semaphore_wait(barrier, len(devices))
+
+
+def swap_kernel(count, whole, x_ref, o_ref, send_sem, recv_sem, own_sem):
+    me = lax.axis_index("inner")
+    others = [lax.rem(me + k, count) for k in range(1, count)]
+    own = pltpu.make_async_copy(x_ref if whole else x_ref.at[me], o_ref.at[me], own_sem)
+    own.start()
+    enter([{"inner": dev} for dev in others])
+    copies = []
+    for k, dev in enumerate(others):
+        copy = pltpu.make_async_remote_copy(
+            src_ref=x_ref if whole else x_ref.at[dev], dst_ref=o_ref.at[me],
+            send_sem=send_sem.at[k], recv_sem=recv_sem.at[k],
+            device_id={"inner": dev}, device_id_type=MESH,
+        )
+        copy.start()
+        copies.append(copy)
+    own.wait()
+    for copy in copies:
+        copy.wait()
+
+
+def swap(x, count, whole, cid):
+    shape = ((count,) + x.shape) if whole else x.shape
+    return pl.pallas_call(
+        functools.partial(swap_kernel, count, whole),
+        out_shape=jax.ShapeDtypeStruct(shape, x.dtype),
+        in_specs=vmem(1),
+        out_specs=vmem(1)[0],
+        scratch_shapes=[
+            pltpu.SemaphoreType.DMA((count - 1,)),
+            pltpu.SemaphoreType.DMA((count - 1,)),
+            pltpu.SemaphoreType.DMA,
+        ],
+        compiler_params=params(collective_id=cid, has_side_effects=True),
+    )(x)
+
+
+def weights_kernel(wq_ref, wo_ref, oq_ref, oo_ref, send_sem, recv_sem, own_sem):
+    pipe = lax.axis_index("pipe")
+    dp = lax.axis_index("dp")
+    core = lax.rem(dp, 2)
+    far = {"pipe": 1 - pipe}
+    near = {"dp": dp + 1 - 2 * core}
+    half = wq_ref.shape[1] // 2
+    mine = pl.ds(pl.multiple_of(core * half, half), half)
+    owns = []
+    for k, (src, dst) in enumerate(((wq_ref, oq_ref), (wo_ref, oo_ref))):
+        own = pltpu.make_async_copy(src.at[0], dst.at[pipe], own_sem.at[k])
+        own.start()
+        owns.append(own)
+    enter([far, near])
+    firsts = []
+    for k, (src, dst) in enumerate(((wq_ref, oq_ref), (wo_ref, oo_ref))):
+        copy = pltpu.make_async_remote_copy(
+            src_ref=src.at[0, mine], dst_ref=dst.at[pipe, mine],
+            send_sem=send_sem.at[k], recv_sem=recv_sem.at[k],
+            device_id=far, device_id_type=MESH,
+        )
+        copy.start()
+        firsts.append(copy)
+    seconds = []
+    for k, dst in enumerate((oq_ref, oo_ref)):
+        firsts[k].wait_recv()
+        copy = pltpu.make_async_remote_copy(
+            src_ref=dst.at[1 - pipe, mine], dst_ref=dst.at[1 - pipe, mine],
+            send_sem=send_sem.at[2 + k], recv_sem=recv_sem.at[2 + k],
+            device_id=near, device_id_type=MESH,
+        )
+        copy.start()
+        seconds.append(copy)
+    for copy in firsts:
+        copy.wait_send()
+    for copy in seconds:
+        copy.wait()
+    for own in owns:
+        own.wait()
+
+
+def bring_weights(wqkv, wout, cid):
+    return pl.pallas_call(
+        weights_kernel,
+        out_shape=[
+            jax.ShapeDtypeStruct((2,) + wqkv.shape[1:], wqkv.dtype),
+            jax.ShapeDtypeStruct((2,) + wout.shape[1:], wout.dtype),
+        ],
+        in_specs=vmem(2),
+        out_specs=vmem(2),
+        scratch_shapes=[
+            pltpu.SemaphoreType.DMA((4,)),
+            pltpu.SemaphoreType.DMA((4,)),
+            pltpu.SemaphoreType.DMA((2,)),
+        ],
+        compiler_params=params(collective_id=cid, has_side_effects=True),
+    )(wqkv, wout)
+
+
+def total_kernel(g_ref, x_ref, o_ref, ox_ref, a0, a1, a2, a3, a4, b0, b1, b2, b3, b4, xs, xr, send_sem, recv_sem):
+    pipe = lax.axis_index("pipe")
+    dp = lax.axis_index("dp")
+    inner = lax.axis_index("inner")
+    core = lax.rem(dp, 2)
+    y = dp // 2
+    z_hi = inner // 2
+    z_lo = lax.rem(inner, 2)
+    rows = g_ref.shape[1]
+    partners = [
+        {"dp": dp + 1 - 2 * core},
+        {"pipe": 1 - pipe},
+        {"dp": dp + 2 - 4 * y},
+        {"inner": inner + 2 - 4 * z_hi},
+        {"inner": inner + 1 - 2 * z_lo},
+    ]
+    enter(partners)
+
+    def send(k, src, dst, sem):
+        copy = pltpu.make_async_remote_copy(
+            src_ref=src, dst_ref=dst, send_sem=send_sem.at[sem], recv_sem=recv_sem.at[sem],
+            device_id=partners[k], device_id_type=MESH,
+        )
+        copy.start()
+        return copy
+
+    def part(bit, size):
+        return pl.ds(pl.multiple_of(bit * size, size), size)
+
+    started = []
+    half = rows // 2
+    main = send(0, g_ref.at[:, part(1 - core, half)], b0, 0)
+    small = send(0, x_ref, xr.at[pl.ds(0, 2)], 5)
+    main.wait_recv()
+    a0[...] = g_ref[:, part(core, half)] + b0[...]
+    small.wait_recv()
+    xs[pl.ds(0, 2)] = x_ref[...] + xr[pl.ds(0, 2)]
+    started += [main, small]
+    main = send(1, a0.at[1 - pipe], b1, 1)
+    small = send(1, xs.at[1 - pipe], xr.at[2], 6)
+    main.wait_recv()
+    a1[...] = a0[pipe] + b1[...]
+    small.wait_recv()
+    xs[2] = xs[pipe] + xr[2]
+    started += [main, small]
+    source, size = a1, half
+    for k, bit, acc, got in ((2, y, a2, b2), (3, z_hi, a3, b3), (4, z_lo, a4, b4)):
+        size //= 2
+        main = send(k, source.at[part(1 - bit, size)], got, k)
+        small = send(k, xs.at[k], xr.at[k + 1], 5 + k)
+        main.wait_recv()
+        acc[...] = source[part(bit, size)] + got[...]
+        small.wait_recv()
+        xs[k + 1] = xs[k] + xr[k + 1]
+        started += [main, small]
+        source = acc
+    ox_ref[...] = xs[5]
+    start = core * half + y * (half // 2) + z_hi * (half // 4) + z_lo * size
+    o_ref[pl.ds(pl.multiple_of(start, size), size)] = a4[...]
+    for n, (k, bit) in enumerate(((4, z_lo), (3, z_hi), (2, y), (0, core))):
+        span = pl.ds(pl.multiple_of(start, size), size)
+        copy = send(k, o_ref.at[span], o_ref.at[span], 10 + n)
+        copy.wait_recv()
+        started.append(copy)
+        start = start - bit * size
+        size *= 2
+    for copy in started:
+        copy.wait_send()
+
+
+def total(g, x, cid):
+    rows, width = g.shape[1:]
+    half = rows // 2
+    sizes = [(2, half, width), (half, width), (half // 2, width), (half // 4, width), (half // 8, width)]
+    return pl.pallas_call(
+        total_kernel,
+        out_shape=[
+            jax.ShapeDtypeStruct((rows, width), F32),
+            jax.ShapeDtypeStruct(x.shape[1:], F32),
+        ],
+        in_specs=vmem(2),
+        out_specs=vmem(2),
+        scratch_shapes=[pltpu.VMEM(s, F32) for s in sizes] * 2
+        + [pltpu.VMEM((6,) + x.shape[1:], F32)] * 2
+        + [pltpu.SemaphoreType.DMA((14,)), pltpu.SemaphoreType.DMA((14,))],
+        compiler_params=params(collective_id=cid, has_side_effects=True),
+    )(g, x)
+
+
+def local(fn, outs, *args):
+    return pl.pallas_call(
+        fn,
+        out_shape=[jax.ShapeDtypeStruct(s, t) for s, t in outs],
+        in_specs=vmem(len(args)),
+        out_specs=vmem(len(outs)),
+        compiler_params=params(),
+    )(*args)
+
+
+def shards(pixels, date_days, clear_count, batch_slot, labels, class_tokens, section_gain,
+           segment_probe_lookup_content, section_out, head_vec):
+    tiles_dev, patches_dev, dates, width = pixels.shape
+    inner_count = lax.axis_size("inner")
+    kinds = CLASSES // inner_count
+    total_tiles = tiles_dev * lax.axis_size("dp")
+    group = lax.axis_index("inner")
+    pipe_pos = lax.axis_index("pipe")
+    tiles = tiles_dev // 2
+    rows = tiles * patches_dev * dates
+    batch_norm = 1.0 / (total_tiles // MICRO * PATCHES)
+    w_all, wo_all = bring_weights(segment_probe_lookup_content, section_out, 0)
+    gains = lax.all_gather(section_gain, "pipe", axis=0, tiled=True)
+
+    def own(a):
+        return lax.dynamic_slice_in_dim(a, pipe_pos * tiles, tiles, 0)
+
+    pix, days, counts, label, slot = map(own, (pixels, date_days, clear_count, labels, batch_slot))
+    channel = jnp.arange(width)
+    frequency = jnp.exp((channel // 2 * 2).astype(F32) * (-math.log(10000.0) / width))
+    phases = days.astype(F32)[:, :, None] * frequency
+    enc = jnp.where(channel % 2 == 0, jnp.sin(phases), jnp.cos(phases))
+    mask = (jnp.arange(dates)[None, None] < counts[:, None, None]).astype(F32)
+    mask = jnp.broadcast_to(mask, (tiles, patches_dev, dates)).reshape(1, rows)
+    label_rows = label.reshape(tiles, inner_count, patches_dev) - group * kinds
+    label_rows = jnp.swapaxes(label_rows, 0, 1).reshape(-1, 1)
+    per = label_rows.shape[0]
+    label_rows = jnp.broadcast_to(label_rows, (per, 128))
+    slot_rows = jnp.broadcast_to(slot[None, :, None], (inner_count, tiles, patches_dev)).reshape(per, 1)
+    slot_rows = (slot_rows == jnp.arange(128)[None]).astype(F32) * batch_norm
+    w0, w1 = w_all[0], w_all[1]
+    wo0, wo1 = wo_all[0], wo_all[1]
+    g0, g1 = gains[0:1], gains[1:2]
+    head = head_vec.reshape(1, width)
+    hq = HEADS * CLASSES
+    f, b = F32, BF16
+    send, *saved = local(
+        temporal_fwd,
+        [((rows, width), b), ((rows, width), b), ((rows, width), f), ((rows, width), f), ((rows, width), b),
+         ((hq, rows), f), ((hq, rows), f), ((rows, width), b), ((5, CLASSES, width), f)],
+        pix, enc, mask, class_tokens, g0, w0, wo0,
+    )
+    recv = swap(send.reshape(inner_count, -1, width), inner_count, False, 1)
+    srows = kinds * per
+    *kept, sums = local(
+        functools.partial(spatial_fwd, kinds, tiles),
+        [((srows, width), f), ((srows, width), b), ((2, srows, width), f), ((2, srows, width), f),
+         ((srows, width), b), ((kinds, HEADS * per, per), f), ((srows, width), b), ((srows, width), f),
+         ((srows, 128), f), ((per, 128), f)],
+        recv, g1, w1, wo1, head,
+    )
+    totals = swap(sums, inner_count, True, 2)
+    back, dw1, dg1, dhead, loss = local(
+        functools.partial(spatial_bwd, kinds, tiles, total_tiles),
+        [((inner_count, srows // inner_count, width), b), ((width, 4 * width), f), ((1, width), f),
+         ((1, width), f), ((1, 128), f)],
+        totals, label_rows, slot_rows, g1, w1, wo1, head, *kept,
+    )
+    returned = swap(back, inner_count, False, 3).reshape(rows, width)
+    dw0, dg0, dcls = local(
+        temporal_bwd,
+        [((width, 4 * width), f), ((1, width), f), ((CLASSES, width), f)],
+        returned, pix, enc, class_tokens, g0, w0, wo0, *saved,
+    )
+    common = [dcls.reshape(-1, 128), dhead.reshape(-1, 128), loss]
+    pad = -(dcls.size // 128 + dhead.size // 128 + 1 + width // 128) % 8
+    fill = [jnp.zeros((pad, 128), F32)]
+    extra = jnp.stack(
+        [jnp.concatenate(common + [g.reshape(-1, 128)] + fill, axis=0) for g in (dg0, dg1)]
+    )
+    grad, small = total(jnp.stack([dw0, dw1]), extra, 4)
+    nc, nh = dcls.size // 128, width // 128
+    return (
+        small[nc + nh, :MICRO],
+        small[:nc].reshape(CLASSES, width),
+        small[nc + nh + 1 : nc + 2 * nh + 1].reshape(1, width),
+        grad[None, :, : 3 * width],
+        grad[None, :, 3 * width :],
+        small[nc : nc + nh].reshape(width),
+    )
+
+
 def solution(mesh):
     placed = (
         P("dp", "inner", None, None),
@@ -200,8 +836,16 @@
         P("pipe", None, None),
         P(),
     )
+
+    def body(*args):
+        tiles_dev, patches_dev, dates, width = args[0].shape
+        pairs = tiles_dev // 2 * patches_dev
+        sizes = tuple(mesh.shape[a] for a in ("pipe", "dp", "inner"))
+        fits = sizes == (2, 4, 4) and pairs % 8 == 0 and dates == CLASSES and width == 256
+        return (shards if fits else shards_general)(*args)
+
     return jax.shard_map(
-        shards,
+        body,
         mesh=mesh,
         in_specs=placed,
         out_specs=(P(), P(), P("pipe", None), P("pipe", None, None), P("pipe", None, None), P()),

time: 428 us -> 153 us (0.36); the launches traced: 420 us -> 152 us
  Pallas kernels: 0 us -> 126 us
  waiting for transfers between devices: 97.2 us -> 0 us
  matrix products: 86.5 us -> 0 us
  local copies, waits for them, and re-layouts: 84.2 us -> 15.4 us
  blocking collectives: 72.2 us -> 4.23 us
  other arithmetic: 42.6 us -> 5.68 us
  starting transfers between devices: 19.4 us -> 0 us
  between operations: 18.4 us -> 0.8 us
    pallas_call x0 -> x9, Pallas kernels: none -> 126 us  [the longest x1 54.2 us: total(): pl.pallas_call(total_kernel, out_shape=[jax.ShapeDtypeStruct((rows, width...]
    psum x1 -> x0, waiting for transfers between devices: 90.1 us -> none  [shards(): lax.psum((stacked[0], stacked[1], stacked[2], stacked[3], stacked[4], sta...]
    dot_general x76 -> x0, matrix products: 86.5 us -> none  [the longest x48 38.3 us: matmul_f32(): jnp.einsum('...d,de->...e', left_side, right_side.astype(jnp.bfloat16), p...]
    psum x2 -> x0, blocking collectives: 50 us -> none  [the longest x1 40.4 us: shards(): lax.psum((stacked[0], stacked[1], stacked[2], stacked[3], stacked[4], sta...]
    reshape x32 -> x4, local copies, waits for them, and re-layouts: 29.8 us -> 2.55 us  [the longest x1 0.72 us: shards(): common = [dcls.reshape(-1, 128), dhead.reshape(-1, 128), loss]]
    all_to_all x4 -> x0, starting transfers between devices: 19.1 us -> none  [the longest x2 10.8 us: shards(): lax.all_to_all(encoded.reshape(fold_shape), 'inner', split_axis=1, concat...]
    all_gather x3 -> x1, blocking collectives: 22.3 us -> 4.23 us  [shards(): gains = lax.all_gather(section_gain, 'pipe', axis=0, tiled=True)]
    another operation x9 -> x0, local copies, waits for them, and re-layouts: 14.3 us -> none
  transfers between devices with their start and end apart: 5 -> 0, of which waited for: 3 -> 0; matrix products, arithmetic and copies ran while one was open for 12% -> 0% of each run, Pallas kernels for 0% -> 0%
where the time goes in v1:
time: 153 us; the launch traced here: 152 us
  Pallas kernels  126 us (82%)
  local copies, waits for them, and re-layouts  15.4 us (10%)
  other arithmetic  5.68 us (4%)
  blocking collectives  4.23 us (3%)
    pallas_call x1, Pallas kernels, total(): pl.pallas_call(total_kernel, out_shape=[jax.ShapeDtypeStruct((rows, width...  54.2 us
    pallas_call x4, Pallas kernels, local(): pl.pallas_call(fn, out_shape=[jax.ShapeDtypeStruct(s, t) for s, t in outs...  31.6 us
    pallas_call x3, Pallas kernels, swap(): pl.pallas_call(functools.partial(swap_kernel, count, whole), out_shape=ja...  26.8 us
    pallas_call x1, Pallas kernels, bring_weights(): pl.pallas_call(weights_kernel, out_shape=[jax.ShapeDtypeStruct((2,) + wqk...  13.3 us
    all_gather x1, blocking collectives, shards(): gains = lax.all_gather(section_gain, 'pipe', axis=0, tiled=True)  4.23 us

profile of v1, /device:TPU:0, one launch (start us, length us, event | category | flops | bytes accessed | tf_op | source)
XLA Modules:
  0.0 151.9 jit_solution(6691856498137200063)
XLA Ops:
  0.6 0.0 copy-start
  0.6 0.0 copy-start.5
  0.7 1.0 copy-done
  1.6 0.7 constant_dynamic-slice_fusion.pix_ref
  2.3 0.7 dynamic-slice_convert_fusion
  3.0 0.8 fusion.1.enc_ref
  3.8 0.7 dynamic_slice.17
  4.6 0.1 compare_convert_fusion
  4.7 0.6 reshape.94.mask_ref
  5.3 13.3 %shard_map.145 = (bf16[2,256,768]{2,1,0:T(8,128)(2,1)}, bf16[2,256,256]{2,1,0:T(8,128)(2,1)}) custom-call(bf16[1,256,768]{2,1,0:T(8,128)(2,1)} %wq_ref.1, bf16[1,256,256]{2,1,0:T(8,128)(2,1)} %wo_ref.1), custom_call_target="tpu_custom_call" | custom-call | tf_op jit(solution)/shard_map/pallas_call | solution.py:628
  18.6 0.0 copy-start.7
  18.6 0.0 copy-start.8
  18.6 2.1 %slice_bitcast_fusion.1 = (bf16[256,768]{1,0:T(8,128)(2,1)}, bf16[256,768]{1,0:T(8,128)(2,1)}) fusion(bf16[2,256,768]{2,1,0:T(8,128)(2,1)} %get-tuple-element.37), kind=kLoop, calls=%fused_computation.2 | loop fusion | bytes 1572864 | tf_op jit(solution)/shard_map/squeeze | solution.py:774
  20.7 1.7 %slice_bitcast_fusion.4 = (bf16[256,256]{1,0:T(8,128)(2,1)}, bf16[256,256]{1,0:T(8,128)(2,1)}) fusion(bf16[2,256,256]{2,1,0:T(8,128)(2,1)} %get-tuple-element.38), kind=kLoop, calls=%fused_computation.5 | loop fusion | bytes 524288 | tf_op jit(solution)/shard_map/squeeze | solution.py:775
  22.3 0.0 copy-done.5
  22.3 4.2 %all-gather = f32[2,1,256]{2,1,0:T(1,128)S(1)} all-gather(f32[1,1,256]{2,1,0:T(1,128)S(1)} %bitcast.44), channel_id=1, replica_groups=mesh['pipe'=2,'dp'=4,'inner'=4] {'pipe'}, dimensions={0}, use_global_device_ids=true | all-gather | bytes 3072 | tf_op jit(solution)/shard_map/all_gather | solution.py:756
  26.6 0.6 slice_bitcast_fusion.6
  27.1 4.1 %shard_map.146 = (bf16[384,256]{1,0:T(8,128)(2,1)}, bf16[384,256]{1,0:T(8,128)(2,1)}, f32[384,256]{1,0:T(8,128)}, f32[384,256]{1,0:T(8,128)}, bf16[384,256]{1,0:...) custom-call(bf16[2,12,16,256]{3,2,1,0:T(8,128)(2,1)} %constant_dynami, ...), custom_call_target="tpu_custom_call" | custom-call | tf_op jit(solution)/shard_map/pallas_call | solution.py:735
  31.3 9.2 %shard_map.147.recv_ref = bf16[4,96,256]{2,1,0:T(8,128)(2,1)} custom-call(bf16[4,96,256]{2,1,0:T(8,128)(2,1)} %bitcast.36), custom_call_target="tpu_custom_call" | custom-call | tf_op jit(solution)/shard_map/pallas_call | solution.py:572
  40.5 6.7 %shard_map.148 = (f32[384,256]{1,0:T(8,128)}, bf16[384,256]{1,0:T(8,128)(2,1)}, f32[2,384,256]{2,1,0:T(8,128)}, f32[2,384,256]{2,1,0:T(8,128)}, bf16[384,256]{1,...) custom-call(bf16[4,96,256]{2,1,0:T(8,128)(2,1)} %shard_map.147.recv_, ...), custom_call_target="tpu_custom_call" | custom-call | tf_op jit(solution)/shard_map/pallas_call | solution.py:735
  47.2 8.6 %shard_map.149.tot_ref = f32[4,96,128]{2,1,0:T(8,128)} custom-call(f32[96,128]{1,0:T(8,128)} %get-tuple-element.40.x_ref), custom_call_target="tpu_custom_call" | custom-call | tf_op jit(solution)/shard_map/pallas_call | solution.py:572
  55.8 0.0 copy-done.7
  55.9 0.1 sub.18
  55.9 0.1 broadcast_in_dim.38
  56.0 0.7 broadcast_in_dim.39.label_ref
  56.7 0.0 copy-done.8
  56.7 0.1 dynamic_slice.19
  56.8 0.1 broadcast_in_dim.40
  56.9 0.1 eq.22
  57.0 0.7 fusion.slot_ref
  57.7 10.5 %shard_map.150 = (bf16[4,96,256]{2,1,0:T(8,128)(2,1)}, f32[256,1024]{1,0:T(8,128)}, f32[1,256]{1,0:T(1,128)}, f32[1,256]{1,0:T(1,128)}, f32[1,128]{1,0:T(1,128)}) custom-call(f32[4,96,128]{2,1,0:T(8,128)} %shard_map.149.tot_ref, s32[96,128]{1,0:T(8,128)} %broadcast_in_dim.39.label_ref, f32[96,128]{1,0:T(8,128)} %fusion.slot_ref, ...), custom_call_target="tpu_custom_call" | custom-call | tf_op jit(solution)/shard_map/pallas_call | solution.py:735
  68.1 0.0 copy-start.3
  68.1 0.0 copy-start.4
  68.2 0.0 copy-start.6
  68.2 0.0 copy-start.1
  68.2 8.9 %shard_map.151 = bf16[4,96,256]{2,1,0:T(8,128)(2,1)} custom-call(bf16[4,96,256]{2,1,0:T(8,128)(2,1)} %get-tuple-element.50.x_ref), custom_call_target="tpu_custom_call" | custom-call | tf_op jit(solution)/shard_map/pallas_call | solution.py:572
  77.1 10.3 %shard_map.152 = (f32[256,1024]{1,0:T(8,128)}, f32[1,256]{1,0:T(1,128)}, f32[16,256]{1,0:T(8,128)}) custom-call(bf16[384,256]{1,0:T(8,128)(2,1)} %bitcast.35, bf16[2,12,16,256]{3,2,1,0:T(8,128)(2,1)} %constant_dynamic-slice_fusion.pix_ref, f32[2,16,256]{2,1,0:T(8,128)} %fusion.1.enc_ref, bf16[16,256]{1,0:T(8,128)(2,1)} %cls_ref.3, ...), custom_call_target="tpu_custom_call" | custom-call | tf_op jit(solution)/shard_map/pallas_call | solution.py:735
  87.4 0.7 reshape.98
  88.1 0.0 copy-done.3
  88.1 0.0 copy-done.4
  88.1 0.7 concatenate.6
  88.8 0.0 copy-done.6
  88.9 0.6 pad_maximum_fusion.1.x_ref
  89.5 0.0 copy-done.1
  89.5 2.8 %pad_maximum_fusion.g_ref = f32[2,256,1024]{2,1,0:T(8,128)} fusion(f32[1,256,1024]{2,1,0:T(8,128)S(1)} %bitcast.33, f32[1,256,1024]{2,1,0:T(8,128)} %bitcast.34), kind=kLoop, calls=%fused_computation | loop fusion | flops 524288 | bytes 4194304 | tf_op jit(solution)/shard_map/stack | solution.py:814
  92.2 54.2 %shard_map.153 = (f32[256,1024]{1,0:T(8,128)}, f32[40,128]{1,0:T(8,128)}) custom-call(f32[2,256,1024]{2,1,0:T(8,128)} %pad_maximum_fusion.g_ref, f32[2,40,128]{2,1,0:T(8,128)} %pad_maximum_fusion.1.x_ref), custom_call_target="tpu_custom_call" | custom-call | tf_op jit(solution)/shard_map/pallas_call | solution.py:719
  146.4 0.0 copy-start.2
  146.4 2.1 %slice_bitcast_fusion = f32[1,256,768]{2,1,0:T(8,128)} fusion(f32[256,1024]{1,0:T(8,128)} %get-tuple-element.67), kind=kLoop, calls=%fused_computation.1 | loop fusion | bytes 1572864 | tf_op jit(solution)/shard_map/broadcast_in_dim | solution.py:820
  148.5 1.7 %slice_bitcast_fusion.3 = f32[1,256,256]{2,1,0:T(8,128)} fusion(f32[256,1024]{1,0:T(8,128)} %get-tuple-element.67), kind=kLoop, calls=%fused_computation.4 | loop fusion | bytes 524288 | tf_op jit(solution)/shard_map/broadcast_in_dim | solution.py:821
  150.2 0.0 copy-done.2
  150.2 0.6 reshape.102
  150.8 0.6 slice_bitcast_fusion.8
  151.4 0.5 slice_bitcast_fusion.9
  (8 shorter events, 0.1 us)
Async XLA Ops:
  0.6 1.0 copy-start
  0.6 21.7 %copy-start.5 = (f32[1,256]{1,0:T(1,128)S(1)}, f32[1,256]{1,0:T(1,128)}, u32[]{:S(2)}) copy-start(f32[1,256]{1,0:T(1,128)} %param.16) | copy-start | bytes 3076
  18.6 37.3 %copy-start.7 = (s32[4,48]{1,0:T(4,128)S(1)}, s32[4,48]{1,0:T(4,128)}, u32[]{:S(2)}) copy-start(s32[4,48]{1,0:T(4,128)} %param.14) | copy-start | bytes 2308
  18.6 38.2 %copy-start.8 = (s32[4]{0:T(128)S(1)}, s32[4]{0:T(128)}, u32[]{:S(2)}) copy-start(s32[4]{0:T(128)} %param.13) | copy-start | bytes 52
  68.1 20.0 %copy-start.3 = (f32[1,256]{1,0:T(1,128)S(1)}, f32[1,256]{1,0:T(1,128)}, u32[]{:S(2)}) copy-start(f32[1,256]{1,0:T(1,128)} %get-tuple-element.62) | copy-start | bytes 3076
  68.1 20.0 %copy-start.4 = (f32[1,128]{1,0:T(1,128)S(1)}, f32[1,128]{1,0:T(1,128)}, u32[]{:S(2)}) copy-start(f32[1,128]{1,0:T(1,128)} %get-tuple-element.63) | copy-start | bytes 1540
  68.2 20.7 %copy-start.6 = (f32[1,256]{1,0:T(1,128)S(1)}, f32[1,256]{1,0:T(1,128)}, u32[]{:S(2)}) copy-start(f32[1,256]{1,0:T(1,128)} %get-tuple-element.65) | copy-start | bytes 3076
  68.2 21.3 %copy-start.1 = (f32[256,1024]{1,0:T(8,128)S(1)}, f32[256,1024]{1,0:T(8,128)}, u32[]{:S(2)}) copy-start(f32[256,1024]{1,0:T(8,128)} %get-tuple-element.60) | copy-start | bytes 3145732
  146.4 3.8 %copy-start.2 = (f32[40,128]{1,0:T(8,128)S(1)}, f32[40,128]{1,0:T(8,128)}, u32[]{:S(2)}) copy-start(f32[40,128]{1,0:T(8,128)} %get-tuple-element.66) | copy-start | bytes 61444

commit v2 on v1

--- a/solution.py
+++ b/solution.py
@@ -282,15 +282,32 @@
     return (pix.astype(F32) + enc[:, None]).reshape(-1, pix.shape[-1])
 
 
-def temporal_fwd(pix_ref, enc_ref, mask_ref, cls_ref, gain_ref, w_ref, wo_ref,
+def own_tiles(tiles):
+    return pl.ds(lax.axis_index("pipe") * tiles, tiles)
+
+
+def clear_mask(count_ref, tiles, rows, dates):
+    lane = lax.broadcasted_iota(jnp.int32, (1, rows), 1)
+    first = lax.axis_index("pipe") * tiles
+    mask = jnp.zeros((1, rows), F32)
+    for t in range(tiles):
+        clear = (lane // (rows // tiles) == t) & (lane % dates < count_ref[first + t])
+        mask = mask + clear.astype(F32)
+    return mask
+
+
+def temporal_fwd(tiles, pix_ref, enc_ref, count_ref, cls_ref, gain_ref, w_ref, wo_ref,
                  send_ref, nd_ref, kn_ref, rk_ref, v_ref, ad_ref, ac_ref, att_ref, cq_ref):
     d = pix_ref.shape[-1]
     dates = pix_ref.shape[2]
     classes = cls_ref.shape[0]
-    gain = gain_ref[...]
-    x = date_sequence(pix_ref[...], enc_ref[...])
+    gain = gain_ref[0]
+    w_ref = w_ref.at[0]
+    wo_ref = wo_ref.at[0]
+    x = date_sequence(pix_ref[own_tiles(tiles)], enc_ref[own_tiles(tiles)])
     rows = x.shape[0]
     bps = rows // dates
+    mask = clear_mask(count_ref, tiles, rows, dates)
     nd = (x * norm_scale(x) * gain).astype(BF16)
     nd_ref[...] = nd
     cls = cls_ref[...].astype(F32)
@@ -315,7 +332,7 @@
     group = 128 // dates
     qe = expand_heads(qn, hm)
     kct = jnp.concatenate([kcn] * group, axis=0)
-    ed = jnp.exp(normalizer_sharpness * mm3(qe, kn, 1, 1)) * mask_ref[...]
+    ed = jnp.exp(normalizer_sharpness * mm3(qe, kn, 1, 1)) * mask
     ec = jnp.exp(normalizer_sharpness * mm3(qe, kct, 1, 1))
     seg = same_block(128, 128, dates).astype(BF16)
     sum_c = mm2(ec, seg)
@@ -337,7 +354,10 @@
     att = jnp.concatenate(atts, axis=0).astype(BF16)
     att_ref[...] = att
     upd = jnp.concatenate([cls] * bps, axis=0) + mm(att, wo_ref[...])
-    send_ref[...] = mm(permutation(rows, classes), upd.astype(BF16)).astype(BF16)
+    send = mm(permutation(rows, classes), upd.astype(BF16)).astype(BF16)
+    part = send_ref.shape[1]
+    for k in range(send_ref.shape[0]):
+        send_ref[k] = send[k * part : (k + 1) * part]
 
 
 def group_mask(group, dates):
@@ -346,14 +366,16 @@
     return (g == c).astype(F32)
 
 
-def temporal_bwd(back_ref, pix_ref, enc_ref, cls_ref, gain_ref, w_ref, wo_ref,
+def temporal_bwd(tiles, back_ref, pix_ref, enc_ref, cls_ref, gain_ref, w_ref, wo_ref,
                  nd_ref, kn_ref, rk_ref, v_ref, ad_ref, ac_ref, att_ref, cq_ref,
                  dw_ref, dgain_ref, dcls_ref):
     d = pix_ref.shape[-1]
     dates = pix_ref.shape[2]
     classes = cls_ref.shape[0]
-    gain = gain_ref[...]
-    x = date_sequence(pix_ref[...], enc_ref[...])
+    gain = gain_ref[0]
+    w_ref = w_ref.at[0]
+    wo_ref = wo_ref.at[0]
+    x = date_sequence(pix_ref[own_tiles(tiles)], enc_ref[own_tiles(tiles)])
     rows = x.shape[0]
     bps = rows // dates
     cls = cls_ref[...].astype(F32)
@@ -363,7 +385,8 @@
     ones = head_ones(d)
     hm = head_mask(d)
     group = 128 // dates
-    du = mm(permutation(rows, rows // classes), back_ref[...]).astype(BF16)
+    back = jnp.concatenate([back_ref[k] for k in range(back_ref.shape[0])], axis=0)
+    du = mm(permutation(rows, rows // classes), back).astype(BF16)
     dw_ref[:, 3 * d :] = mm(att_ref[...], du, 0, 0)
     do = rounded(mm(du, wo_ref[...], 1, 1))
     qn = cq_ref[0]
@@ -440,6 +463,9 @@
 def spatial_fwd(kinds, tiles, recv_ref, gain_ref, w_ref, wo_ref, head_ref,
                 u_ref, n_ref, qk_ref, r_ref, v_ref, a_ref, o_ref, hid_ref, raw_ref, sum_ref):
     d = recv_ref.shape[-1]
+    gain_ref = gain_ref.at[1]
+    w_ref = w_ref.at[1]
+    wo_ref = wo_ref.at[1]
     u = spatial_rows(recv_ref, kinds)
     u_ref[...] = u
     rows = u.shape[0]
@@ -479,10 +505,34 @@
     sum_ref[...] = jnp.sum(ex.reshape(kinds, per, 128), axis=0)
 
 
-def spatial_bwd(kinds, tiles, total_tiles, tot_ref, label_ref, slot_ref, gain_ref, w_ref, wo_ref, head_ref,
+def patch_columns(label_ref, slot_ref, sources, tiles, lanes):
+    first = lax.axis_index("pipe") * tiles
+    count = label_ref.shape[1]
+    patches = count // sources
+    shape = (sources * tiles * patches, count)
+    row = lax.broadcasted_iota(jnp.int32, shape, 0)
+    col = lax.broadcasted_iota(jnp.int32, shape, 1)
+    tile = (row // patches) % tiles
+    here = col == (row // (patches * tiles)) * patches + row % patches
+    slot_shape = (shape[0], lanes)
+    slot_tile = (lax.broadcasted_iota(jnp.int32, slot_shape, 0) // patches) % tiles
+    lane = lax.broadcasted_iota(jnp.int32, slot_shape, 1)
+    labels = jnp.zeros(shape, F32)
+    slots = jnp.zeros(slot_shape, F32)
+    for t in range(tiles):
+        values = label_ref[pl.ds(first + t, 1), :].astype(F32)
+        labels = labels + jnp.where(here & (tile == t), values, 0.0)
+        slots = slots + ((slot_tile == t) & (lane == slot_ref[first + t])).astype(F32)
+    return jnp.broadcast_to(jnp.sum(labels, axis=-1, keepdims=True), slot_shape), slots
+
+
+def spatial_bwd(kinds, tiles, total_tiles, batch_norm, tot_ref, label_ref, slot_ref, gain_ref, w_ref, wo_ref, head_ref,
                 u_ref, n_ref, qk_ref, r_ref, v_ref, a_ref, o_ref, hid_ref, raw_ref,
                 send_ref, dw_ref, dgain_ref, dhead_ref, loss_ref):
     d = u_ref.shape[-1]
+    gain_ref = gain_ref.at[1]
+    w_ref = w_ref.at[1]
+    wo_ref = wo_ref.at[1]
     rows = u_ref.shape[0]
     per = rows // kinds
     sources = tot_ref.shape[0]
@@ -490,10 +540,12 @@
     total = jnp.concatenate([total] * kinds, axis=0)
     th = jnp.tanh(raw_ref[...] / logit_cap)
     logits = logit_cap * th
-    kind = lax.broadcasted_iota(jnp.int32, (rows, 128), 0) // per
-    ind = (jnp.concatenate([label_ref[...]] * kinds, axis=0) == kind).astype(F32)
-    slot = jnp.concatenate([slot_ref[...]] * kinds, axis=0)
-    loss_ref[...] = jnp.sum(ind * (jnp.log(total) - logits) * slot, axis=0, keepdims=True)
+    label, slot = patch_columns(label_ref, slot_ref, sources, tiles, 128)
+    kind = lax.broadcasted_iota(jnp.int32, (rows, 128), 0) // per + lax.axis_index("inner") * kinds
+    ind = (jnp.concatenate([label] * kinds, axis=0) == kind.astype(F32)).astype(F32)
+    slot = jnp.concatenate([slot] * kinds, axis=0)
+    loss = jnp.sum(ind * (jnp.log(total) - logits) * slot, axis=0, keepdims=True) * batch_norm
+    loss_ref[...] = jnp.concatenate([loss] * (d // 128), axis=1)
     draw = (jnp.exp(logits) / total - ind) / total_tiles * (1.0 - th * th)
     dr = jnp.concatenate([draw] * (d // 128), axis=1)
     head = head_ref[...]
@@ -583,7 +635,7 @@
     )(x)
 
 
-def weights_kernel(wq_ref, wo_ref, oq_ref, oo_ref, send_sem, recv_sem, own_sem):
+def weights_kernel(wq_ref, wo_ref, g_ref, oq_ref, oo_ref, og_ref, send_sem, recv_sem, own_sem):
     pipe = lax.axis_index("pipe")
     dp = lax.axis_index("dp")
     core = lax.rem(dp, 2)
@@ -596,7 +648,14 @@
         own = pltpu.make_async_copy(src.at[0], dst.at[pipe], own_sem.at[k])
         own.start()
         owns.append(own)
+    og_ref[pipe] = g_ref[...]
     enter([far, near])
+    gains = pltpu.make_async_remote_copy(
+        src_ref=g_ref, dst_ref=og_ref.at[pipe],
+        send_sem=send_sem.at[4], recv_sem=recv_sem.at[4],
+        device_id=far, device_id_type=MESH,
+    )
+    gains.start()
     firsts = []
     for k, (src, dst) in enumerate(((wq_ref, oq_ref), (wo_ref, oo_ref))):
         copy = pltpu.make_async_remote_copy(
@@ -622,27 +681,30 @@
         copy.wait()
     for own in owns:
         own.wait()
-
-
-def bring_weights(wqkv, wout, cid):
+    gains.wait()
+
+
+def bring_weights(wqkv, wout, gain, cid):
     return pl.pallas_call(
         weights_kernel,
         out_shape=[
             jax.ShapeDtypeStruct((2,) + wqkv.shape[1:], wqkv.dtype),
             jax.ShapeDtypeStruct((2,) + wout.shape[1:], wout.dtype),
+            jax.ShapeDtypeStruct((2,) + gain.shape, gain.dtype),
         ],
-        in_specs=vmem(2),
-        out_specs=vmem(2),
+        in_specs=vmem(3),
+        out_specs=vmem(3),
         scratch_shapes=[
-            pltpu.SemaphoreType.DMA((4,)),
-            pltpu.SemaphoreType.DMA((4,)),
+            pltpu.SemaphoreType.DMA((5,)),
+            pltpu.SemaphoreType.DMA((5,)),
             pltpu.SemaphoreType.DMA((2,)),
         ],
         compiler_params=params(collective_id=cid, has_side_effects=True),
-    )(wqkv, wout)
-
-
-def total_kernel(g_ref, x_ref, o_ref, ox_ref, a0, a1, a2, a3, a4, b0, b1, b2, b3, b4, xs, xr, send_sem, recv_sem):
+    )(wqkv, wout, gain)
+
+
+def total_kernel(dw0, dw1, dcls, dg0, dg1, dhead, loss, oqkv, oout, ocls, ogain, ohead, oloss,
+                 b0, a0, s1, b1, a1, s2, b2, a2, b3, a3, b4, a4, res, x0, xs, xr, send_sem, recv_sem):
     pipe = lax.axis_index("pipe")
     dp = lax.axis_index("dp")
     inner = lax.axis_index("inner")
@@ -650,15 +712,16 @@
     y = dp // 2
     z_hi = inner // 2
     z_lo = lax.rem(inner, 2)
-    rows = g_ref.shape[1]
+    rows, width = dw0.shape
+    cols = width // 2
     partners = [
         {"dp": dp + 1 - 2 * core},
         {"pipe": 1 - pipe},
         {"dp": dp + 2 - 4 * y},
+        {"inner": inner + 1 - 2 * z_lo},
         {"inner": inner + 2 - 4 * z_hi},
-        {"inner": inner + 1 - 2 * z_lo},
     ]
-    enter(partners)
+    started = []
 
     def send(k, src, dst, sem):
         copy = pltpu.make_async_remote_copy(
@@ -666,79 +729,182 @@
             device_id=partners[k], device_id_type=MESH,
         )
         copy.start()
+        started.append(copy)
         return copy
 
     def part(bit, size):
         return pl.ds(pl.multiple_of(bit * size, size), size)
 
-    started = []
+    def span(c):
+        return pl.ds(c * cols, cols)
+
+    nc = dcls.shape[0]
+    x0[...] = jnp.zeros_like(x0)
+    for k, gain in enumerate((dg0, dg1)):
+        x0[k, :nc, :] = dcls[...]
+        x0[k, nc : nc + 1, :] = gain[...]
+        x0[k, nc + 1 : nc + 2, :] = dhead[...]
+        x0[k, nc + 2 : nc + 3, :] = loss[...]
+    enter(partners)
     half = rows // 2
-    main = send(0, g_ref.at[:, part(1 - core, half)], b0, 0)
-    small = send(0, x_ref, xr.at[pl.ds(0, 2)], 5)
-    main.wait_recv()
-    a0[...] = g_ref[:, part(core, half)] + b0[...]
+    quarter = half // 2
+    going = [
+        [send(0, dw.at[part(1 - core, half), span(c)], b0.at[c, k], 10 * c + k) for k, dw in enumerate((dw0, dw1))]
+        for c in range(2)
+    ]
+    small = send(0, x0, xr.at[pl.ds(0, 2)], 20)
+    mine = part(core, half)
+    hops = []
+    for c in range(2):
+        for copy in going[c]:
+            copy.wait_recv()
+        for k, dw in enumerate((dw0, dw1)):
+            a0[c, k] = dw[mine, span(c)] + b0[c, k]
+        if c == 0:
+            s1[0] = a0[0, 1 - pipe].astype(s1.dtype)
+            hops.append(send(1, s1.at[0], b1.at[0], 2))
+        else:
+            for k in range(2):
+                s1[1, pl.ds(k * quarter, quarter)] = a0[1, k, part(1 - y, quarter)].astype(s1.dtype)
+            hops.append(send(2, s1.at[1], b1.at[1], 12))
     small.wait_recv()
-    xs[pl.ds(0, 2)] = x_ref[...] + xr[pl.ds(0, 2)]
-    started += [main, small]
-    main = send(1, a0.at[1 - pipe], b1, 1)
-    small = send(1, xs.at[1 - pipe], xr.at[2], 6)
-    main.wait_recv()
-    a1[...] = a0[pipe] + b1[...]
+    xs[pl.ds(0, 2)] = x0[...] + xr[pl.ds(0, 2)]
+    small = send(1, xs.at[1 - pipe], xr.at[2], 21)
+    hops[0].wait_recv()
+    a1[0] = a0[0, pipe] + b1[0].astype(F32)
+    s2[0] = a1[0, part(1 - y, quarter)].astype(s2.dtype)
+    hops[0] = send(2, s2.at[0], b2.at[0], 3)
+    hops[1].wait_recv()
+    for k in range(2):
+        there = pl.ds(k * quarter, quarter)
+        a1[1, there] = a0[1, k, part(y, quarter)] + b1[1, there].astype(F32)
+    s2[1] = a1[1, part(1 - pipe, quarter)].astype(s2.dtype)
+    hops[1] = send(1, s2.at[1], b2.at[1], 13)
     small.wait_recv()
     xs[2] = xs[pipe] + xr[2]
-    started += [main, small]
-    source, size = a1, half
-    for k, bit, acc, got in ((2, y, a2, b2), (3, z_hi, a3, b3), (4, z_lo, a4, b4)):
-        size //= 2
-        main = send(k, source.at[part(1 - bit, size)], got, k)
-        small = send(k, xs.at[k], xr.at[k + 1], 5 + k)
-        main.wait_recv()
-        acc[...] = source[part(bit, size)] + got[...]
+    small = send(2, xs.at[2], xr.at[3], 22)
+    source, bits, size = a1, (y, pipe), quarter
+    for k, nxt, acc, got in ((3, z_lo, a2, b2), (4, z_hi, a3, b3), (5, None, a4, b4)):
+        for c in range(2):
+            hops[c].wait_recv()
+            acc[c] = source[c, part(bits[c], size)] + got[c].astype(F32)
+            if nxt is not None:
+                smaller = size // 2
+                landing = b3 if k == 3 else b4
+                hops[c] = send(k, acc.at[c, part(1 - nxt, smaller)], landing.at[c], 10 * c + k + 1)
         small.wait_recv()
-        xs[k + 1] = xs[k] + xr[k + 1]
-        started += [main, small]
-        source = acc
-    ox_ref[...] = xs[5]
-    start = core * half + y * (half // 2) + z_hi * (half // 4) + z_lo * size
-    o_ref[pl.ds(pl.multiple_of(start, size), size)] = a4[...]
-    for n, (k, bit) in enumerate(((4, z_lo), (3, z_hi), (2, y), (0, core))):
-        span = pl.ds(pl.multiple_of(start, size), size)
-        copy = send(k, o_ref.at[span], o_ref.at[span], 10 + n)
-        copy.wait_recv()
-        started.append(copy)
+        xs[k] = xs[k - 1] + xr[k]
+        if nxt is not None:
+            small = send(k, xs.at[k], xr.at[k + 1], 20 + k)
+            source, bits, size = acc, (nxt, nxt), size // 2
+    start = core * half + y * quarter + z_lo * (quarter // 2) + z_hi * size
+    gathers = [None, None]
+    for n, (k, bit) in enumerate(((4, z_hi), (3, z_lo), (2, y), (0, core))):
+        here = pl.ds(pl.multiple_of(start, size), size)
+        for c in range(2):
+            if n == 0:
+                res[c, here] = a4[c]
+            else:
+                gathers[c].wait_recv()
+            gathers[c] = send(k, res.at[c, here], res.at[c, here], 10 * c + 6 + n)
         start = start - bit * size
         size *= 2
+    last = xs[5]
+    ocls[...] = last[:nc]
+    ogain[...] = last[nc : nc + 1]
+    ohead[...] = last[nc + 1 : nc + 2]
+    oloss[...] = last[nc + 2 : nc + 3]
+    for copy in gathers:
+        copy.wait_recv()
+    first = oqkv.shape[2] - cols
+    oqkv[0, :, :cols] = res[0]
+    oqkv[0, :, cols:] = res[1, :, :first]
+    oout[0] = res[1, :, first:]
     for copy in started:
         copy.wait_send()
 
 
-def total(g, x, cid):
-    rows, width = g.shape[1:]
-    half = rows // 2
-    sizes = [(2, half, width), (half, width), (half // 2, width), (half // 4, width), (half // 8, width)]
+def total_scratch(rows, width, classes):
+    half, cols = rows // 2, width // 2
+    extra = (-(-(classes + 3) // 8) * 8, width // 4)
+    return [
+        pltpu.VMEM((2, 2, half, cols), F32),
+        pltpu.VMEM((2, 2, half, cols), F32),
+        pltpu.VMEM((2, half, cols), BF16),
+        pltpu.VMEM((2, half, cols), BF16),
+        pltpu.VMEM((2, half, cols), F32),
+        pltpu.VMEM((2, half // 2, cols), BF16),
+        pltpu.VMEM((2, half // 2, cols), BF16),
+        pltpu.VMEM((2, half // 2, cols), F32),
+        pltpu.VMEM((2, half // 4, cols), F32),
+        pltpu.VMEM((2, half // 4, cols), F32),
+        pltpu.VMEM((2, half // 8, cols), F32),
+        pltpu.VMEM((2, half // 8, cols), F32),
+        pltpu.VMEM((2, rows, cols), F32),
+        pltpu.VMEM((2,) + extra, F32),
+        pltpu.VMEM((6,) + extra, F32),
+        pltpu.VMEM((6,) + extra, F32),
+        pltpu.SemaphoreType.DMA((25,)),
+        pltpu.SemaphoreType.DMA((25,)),
+    ]
+
+
+def total_outs(rows, width, classes):
+    d = width // 4
+    shapes = [(1, rows, 3 * d), (1, rows, d), (classes, d), (1, d), (1, d), (1, d)]
+    return [jax.ShapeDtypeStruct(s, F32) for s in shapes]
+
+
+def total(cid, *args):
+    rows, width = args[0].shape
+    classes = args[2].shape[0]
     return pl.pallas_call(
         total_kernel,
-        out_shape=[
-            jax.ShapeDtypeStruct((rows, width), F32),
-            jax.ShapeDtypeStruct(x.shape[1:], F32),
-        ],
-        in_specs=vmem(2),
-        out_specs=vmem(2),
-        scratch_shapes=[pltpu.VMEM(s, F32) for s in sizes] * 2
-        + [pltpu.VMEM((6,) + x.shape[1:], F32)] * 2
-        + [pltpu.SemaphoreType.DMA((14,)), pltpu.SemaphoreType.DMA((14,))],
+        out_shape=total_outs(rows, width, classes),
+        in_specs=vmem(len(args)),
+        out_specs=vmem(6),
+        scratch_shapes=total_scratch(rows, width, classes),
         compiler_params=params(collective_id=cid, has_side_effects=True),
-    )(g, x)
-
-
-def local(fn, outs, *args):
+    )(*args)
+
+
+def local(fn, outs, scalars, *args):
+    specs = vmem(len(args))
+    for k in scalars:
+        specs[k] = pl.BlockSpec(memory_space=pltpu.SMEM)
     return pl.pallas_call(
         fn,
         out_shape=[jax.ShapeDtypeStruct(s, t) for s, t in outs],
-        in_specs=vmem(len(args)),
+        in_specs=specs,
         out_specs=vmem(len(outs)),
         compiler_params=params(),
     )(*args)
+
+
+def date_encoding(date_days, width):
+    channel = jnp.arange(width)
+    frequency = jnp.exp((channel // 2 * 2).astype(F32) * (-math.log(10000.0) / width))
+    phases = date_days.astype(F32)[:, :, None] * frequency
+    return jnp.where(channel % 2 == 0, jnp.sin(phases), jnp.cos(phases))
+
+
+def saved_shapes(rows, width):
+    hq = HEADS * CLASSES
+    f, b = F32, BF16
+    return [((rows, width), b), ((rows, width), f), ((rows, width), f), ((rows, width), b),
+            ((hq, rows), f), ((hq, rows), f), ((rows, width), b), ((5, CLASSES, width), f)]
+
+
+def kept_shapes(kinds, per, width):
+    srows = kinds * per
+    f, b = F32, BF16
+    return [((srows, width), f), ((srows, width), b), ((2, srows, width), f), ((2, srows, width), f),
+            ((srows, width), b), ((kinds, HEADS * per, per), f), ((srows, width), b), ((srows, width), f),
+            ((srows, 128), f)]
+
+
+def grad_shapes(width):
+    return [((width, 4 * width), F32), ((1, width), F32)]
 
 
 def shards(pixels, date_days, clear_count, batch_slot, labels, class_tokens, section_gain,
@@ -747,80 +913,39 @@
     inner_count = lax.axis_size("inner")
     kinds = CLASSES // inner_count
     total_tiles = tiles_dev * lax.axis_size("dp")
-    group = lax.axis_index("inner")
-    pipe_pos = lax.axis_index("pipe")
     tiles = tiles_dev // 2
     rows = tiles * patches_dev * dates
     batch_norm = 1.0 / (total_tiles // MICRO * PATCHES)
-    w_all, wo_all = bring_weights(segment_probe_lookup_content, section_out, 0)
-    gains = lax.all_gather(section_gain, "pipe", axis=0, tiled=True)
-
-    def own(a):
-        return lax.dynamic_slice_in_dim(a, pipe_pos * tiles, tiles, 0)
-
-    pix, days, counts, label, slot = map(own, (pixels, date_days, clear_count, labels, batch_slot))
-    channel = jnp.arange(width)
-    frequency = jnp.exp((channel // 2 * 2).astype(F32) * (-math.log(10000.0) / width))
-    phases = days.astype(F32)[:, :, None] * frequency
-    enc = jnp.where(channel % 2 == 0, jnp.sin(phases), jnp.cos(phases))
-    mask = (jnp.arange(dates)[None, None] < counts[:, None, None]).astype(F32)
-    mask = jnp.broadcast_to(mask, (tiles, patches_dev, dates)).reshape(1, rows)
-    label_rows = label.reshape(tiles, inner_count, patches_dev) - group * kinds
-    label_rows = jnp.swapaxes(label_rows, 0, 1).reshape(-1, 1)
-    per = label_rows.shape[0]
-    label_rows = jnp.broadcast_to(label_rows, (per, 128))
-    slot_rows = jnp.broadcast_to(slot[None, :, None], (inner_count, tiles, patches_dev)).reshape(per, 1)
-    slot_rows = (slot_rows == jnp.arange(128)[None]).astype(F32) * batch_norm
-    w0, w1 = w_all[0], w_all[1]
-    wo0, wo1 = wo_all[0], wo_all[1]
-    g0, g1 = gains[0:1], gains[1:2]
+    w, wo, gains = bring_weights(segment_probe_lookup_content, section_out, section_gain, 0)
+    enc = date_encoding(date_days, width)
     head = head_vec.reshape(1, width)
-    hq = HEADS * CLASSES
-    f, b = F32, BF16
+    per = inner_count * tiles * patches_dev
+    exchanged = (inner_count, rows // inner_count, width)
     send, *saved = local(
-        temporal_fwd,
-        [((rows, width), b), ((rows, width), b), ((rows, width), f), ((rows, width), f), ((rows, width), b),
-         ((hq, rows), f), ((hq, rows), f), ((rows, width), b), ((5, CLASSES, width), f)],
-        pix, enc, mask, class_tokens, g0, w0, wo0,
-    )
-    recv = swap(send.reshape(inner_count, -1, width), inner_count, False, 1)
-    srows = kinds * per
+        functools.partial(temporal_fwd, tiles),
+        [(exchanged, BF16)] + saved_shapes(rows, width), (2,),
+        pixels, enc, clear_count, class_tokens, gains, w, wo,
+    )
+    recv = swap(send, inner_count, False, 1)
     *kept, sums = local(
         functools.partial(spatial_fwd, kinds, tiles),
-        [((srows, width), f), ((srows, width), b), ((2, srows, width), f), ((2, srows, width), f),
-         ((srows, width), b), ((kinds, HEADS * per, per), f), ((srows, width), b), ((srows, width), f),
-         ((srows, 128), f), ((per, 128), f)],
-        recv, g1, w1, wo1, head,
+        kept_shapes(kinds, per, width) + [((per, 128), F32)], (),
+        recv, gains, w, wo, head,
     )
     totals = swap(sums, inner_count, True, 2)
     back, dw1, dg1, dhead, loss = local(
-        functools.partial(spatial_bwd, kinds, tiles, total_tiles),
-        [((inner_count, srows // inner_count, width), b), ((width, 4 * width), f), ((1, width), f),
-         ((1, width), f), ((1, 128), f)],
-        totals, label_rows, slot_rows, g1, w1, wo1, head, *kept,
-    )
-    returned = swap(back, inner_count, False, 3).reshape(rows, width)
+        functools.partial(spatial_bwd, kinds, tiles, total_tiles, batch_norm),
+        [(exchanged, BF16)] + grad_shapes(width) + [((1, width), F32)] * 2, (2,),
+        totals, labels, batch_slot, gains, w, wo, head, *kept,
+    )
+    returned = swap(back, inner_count, False, 3)
     dw0, dg0, dcls = local(
-        temporal_bwd,
-        [((width, 4 * width), f), ((1, width), f), ((CLASSES, width), f)],
-        returned, pix, enc, class_tokens, g0, w0, wo0, *saved,
-    )
-    common = [dcls.reshape(-1, 128), dhead.reshape(-1, 128), loss]
-    pad = -(dcls.size // 128 + dhead.size // 128 + 1 + width // 128) % 8
-    fill = [jnp.zeros((pad, 128), F32)]
-    extra = jnp.stack(
-        [jnp.concatenate(common + [g.reshape(-1, 128)] + fill, axis=0) for g in (dg0, dg1)]
-    )
-    grad, small = total(jnp.stack([dw0, dw1]), extra, 4)
-    nc, nh = dcls.size // 128, width // 128
-    return (
-        small[nc + nh, :MICRO],
-        small[:nc].reshape(CLASSES, width),
-        small[nc + nh + 1 : nc + 2 * nh + 1].reshape(1, width),
-        grad[None, :, : 3 * width],
-        grad[None, :, 3 * width :],
-        small[nc : nc + nh].reshape(width),
-    )
+        functools.partial(temporal_bwd, tiles),
+        grad_shapes(width) + [((CLASSES, width), F32)], (),
+        returned, pixels, enc, class_tokens, gains, w, wo, *saved,
+    )
+    gqkv, gout, gcls, ggain, ghead, gloss = total(4, dw0, dw1, dcls, dg0, dg1, dhead, loss)
+    return gloss[0, :MICRO], gcls, ggain, gqkv, gout, ghead.reshape(width)
 
 
 def solution(mesh):

time: 153 us -> 121 us (0.79)
  Pallas kernels: 126 us -> 111 us
  local copies, waits for them, and re-layouts: 15.4 us -> 7.1 us
  blocking collectives: 4.23 us -> 0 us
  other arithmetic: 5.68 us -> 1.64 us
    pallas_call x1, Pallas kernels: 54.2 us -> 37.1 us  [total(): pl.pallas_call(total_kernel, out_shape=total_outs(rows, width, classes),...]
    unnamed x18 -> x9, local copies, waits for them, and re-layouts: 1.02 us -> 5.89 us
    broadcast_in_dim x7 -> x0, local copies, waits for them, and re-layouts: 4.61 us -> none  [the longest x1 2.07 us: shards(): grad[None, :, :3 * width]]
    all_gather x1 -> x0, blocking collectives: 4.23 us -> none  [shards(): gains = lax.all_gather(section_gain, 'pipe', axis=0, tiled=True)]
    another operation x2 -> x0, other arithmetic: 3.37 us -> none  [the longest x1 2.75 us: shards(): grad, small = total(jnp.stack([dw0, dw1]), extra, 4)]
    squeeze x3 -> x1, local copies, waits for them, and re-layouts: 4.25 us -> 1.21 us  [shards(): return (gloss[0, :MICRO], gcls, ggain, gqkv, gout, ghead.reshape(width))]
    reshape x4 -> x0, local copies, waits for them, and re-layouts: 2.55 us -> none  [the longest x1 0.72 us: shards(): common = [dcls.reshape(-1, 128), dhead.reshape(-1, 128), loss]]
where the time goes in v2:
time: 121 us; the launch traced here: 120 us
  Pallas kernels  111 us (92%)
  local copies, waits for them, and re-layouts  7.1 us (6%)
  other arithmetic  1.64 us (1%)
    pallas_call x1, Pallas kernels, total(): pl.pallas_call(total_kernel, out_shape=total_outs(rows, width, classes),...  37.1 us
    pallas_call x4, Pallas kernels, local(): pl.pallas_call(fn, out_shape=[jax.ShapeDtypeStruct(s, t) for s, t in outs...  32.4 us
    pallas_call x3, Pallas kernels, swap(): pl.pallas_call(functools.partial(swap_kernel, count, whole), out_shape=ja...  27.7 us
    pallas_call x1, Pallas kernels, bring_weights(): pl.pallas_call(weights_kernel, out_shape=[jax.ShapeDtypeStruct((2,) + wqk...  13.4 us
    unnamed x9, local copies, waits for them, and re-layouts  5.89 us

profile of v2, /device:TPU:0, one launch (start us, length us, event | category | flops | bytes accessed | tf_op | source)
XLA Modules:
  0.0 120.0 jit_solution(6638027370420666403)
XLA Ops:
  0.7 0.7 convert_element_type.10
  1.3 0.9 fusion.enc_ref
  2.3 13.4 %shard_map.145 = (bf16[2,256,768]{2,1,0:T(8,128)(2,1)}, bf16[2,256,256]{2,1,0:T(8,128)(2,1)}, f32[2,1,256]{2,1,0:T(1,128)}) custom-call(bf16[1,256,768]{2,1,0:T(8,128)(2,1)} %wq_ref.1, bf16[1,256,256]{2,1,0:T(8,128)(2,1)} %wo_ref.1, f32[1,256]{1,0:T(1,128)} %g_ref.1), custom_call_target="tpu_custom_call" | custom-call | tf_op jit(solution)/shard_map/pallas_call | solution.py:688
  15.7 4.3 %shard_map.146 = (bf16[4,96,256]{2,1,0:T(8,128)(2,1)}, bf16[384,256]{1,0:T(8,128)(2,1)}, f32[384,256]{1,0:T(8,128)}, f32[384,256]{1,0:T(8,128)}, bf16[384,256]{1...) custom-call(bf16[4,12,16,256]{3,2,1,0:T(8,128)(2,1)} %pix_ref.3, ...), custom_call_target="tpu_custom_call" | custom-call | tf_op jit(solution)/shard_map/pallas_call | solution.py:875
  20.0 9.9 %shard_map.147.recv_ref = bf16[4,96,256]{2,1,0:T(8,128)(2,1)} custom-call(bf16[4,96,256]{2,1,0:T(8,128)(2,1)} %get-tuple-element.45.x_ref), custom_call_target="tpu_custom_call" | custom-call | tf_op jit(solution)/shard_map/pallas_call | solution.py:624
  29.9 6.8 %shard_map.148 = (f32[384,256]{1,0:T(8,128)}, bf16[384,256]{1,0:T(8,128)(2,1)}, f32[2,384,256]{2,1,0:T(8,128)}, f32[2,384,256]{2,1,0:T(8,128)}, bf16[384,256]{1,...) custom-call(bf16[4,96,256]{2,1,0:T(8,128)(2,1)} %shard_map.147.recv_, ...), custom_call_target="tpu_custom_call" | custom-call | tf_op jit(solution)/shard_map/pallas_call | solution.py:875
  36.8 9.0 %shard_map.149.tot_ref = f32[4,96,128]{2,1,0:T(8,128)} custom-call(f32[96,128]{1,0:T(8,128)} %get-tuple-element.46.x_ref), custom_call_target="tpu_custom_call" | custom-call | tf_op jit(solution)/shard_map/pallas_call | solution.py:624
  45.7 10.8 %shard_map.150 = (bf16[4,96,256]{2,1,0:T(8,128)(2,1)}, f32[256,1024]{1,0:T(8,128)}, f32[1,256]{1,0:T(1,128)}, f32[1,256]{1,0:T(1,128)}, f32[1,256]{1,0:T(1,128)}) custom-call(f32[4,96,128]{2,1,0:T(8,128)} %shard_map.149.tot_ref, s32[4,48]{1,0:T(4,128)} %label_ref.1, s32[4]{0:T(128)} %slot_ref.1, f32[2,1,256]{2,1,0:T(1,128)} %get-tuple-element.42.gain_ref, ...), custom_call_target="tpu_custom_call" | custom-call | tf_op jit(solution)/shard_map/pallas_call | solution.py:875
  56.5 8.8 %shard_map.151.back_ref = bf16[4,96,256]{2,1,0:T(8,128)(2,1)} custom-call(bf16[4,96,256]{2,1,0:T(8,128)(2,1)} %get-tuple-element.56.x_ref), custom_call_target="tpu_custom_call" | custom-call | tf_op jit(solution)/shard_map/pallas_call | solution.py:624
  65.3 10.4 %shard_map.152 = (f32[256,1024]{1,0:T(8,128)}, f32[1,256]{1,0:T(1,128)}, f32[16,256]{1,0:T(8,128)}) custom-call(bf16[4,96,256]{2,1,0:T(8,128)(2,1)} %shard_map.151.back_ref, bf16[4,12,16,256]{3,2,1,0:T(8,128)(2,1)} %pix_ref.3, f32[4,16,256]{2,1,0:T(8,128)} %fusion.enc_ref, bf16[16,256]{1,0:T(8,128)(2,1)} %cls_ref.3, ...), custom_call_target="tpu_custom_call" | custom-call | tf_op jit(solution)/shard_map/pallas_call | solution.py:875
  75.8 37.1 %shard_map.153 = (f32[1,256,768]{2,1,0:T(8,128)}, f32[1,256,256]{2,1,0:T(8,128)}, f32[16,256]{1,0:T(8,128)}, f32[1,256]{1,0:T(1,128)}, f32[1,256]{1,0:T(1,128)}, /*index=5*/f32[1,256]{1,0:T(1,128)}) custom-call(f32[256,1024]{1,0:T(8,128)} %get-tuple-element.65.dw0, f32[256,1024]{1,0:T(8,128)} %get-tuple-element.66.dw1, f32[16,256]{1,0:T(8,128)} %get-tuple-element.67.dcls, ...), custom_call_target="tpu_custom_call" | custom-call | tf_op jit(solution)/shard_map/pallas_call | solution.py:861
  112.9 0.0 copy-start
  112.9 0.0 copy-start.1
  112.9 1.2 %slice_bitcast_fusion = f32[4]{0:T(128)} fusion(f32[1,256]{1,0:T(1,128)} %get-tuple-element.72), kind=kLoop, calls=%fused_computation.14 | loop fusion | bytes 32 | tf_op jit(solution)/shard_map/squeeze | solution.py:948
  114.1 1.3 %copy.21 = f32[16,256]{1,0:T(8,128)} copy(f32[16,256]{1,0:T(8,128)} %get-tuple-element.85) | data formatting | bytes 32768
  115.5 1.2 %copy.22 = f32[1,256]{1,0:T(1,128)} copy(f32[1,256]{1,0:T(1,128)} %get-tuple-element.86) | data formatting | bytes 2048
  116.7 2.1 %copy.23 = f32[1,256,768]{2,1,0:T(8,128)} copy(f32[1,256,768]{2,1,0:T(8,128)} %get-tuple-element.87) | data formatting | bytes 1572864
  118.7 0.0 copy-done
  118.7 0.7 copy.24
  119.5 0.0 copy-done.1
  119.5 0.6 copy.25
  (2 shorter events, 0.0 us)
Async XLA Ops:
  112.9 5.9 %copy-start = (f32[1,256,256]{2,1,0:T(8,128)S(1)}, f32[1,256,256]{2,1,0:T(8,128)}, u32[]{:S(2)}) copy-start(f32[1,256,256]{2,1,0:T(8,128)} %get-tuple-element.88) | copy-start | bytes 786436
  112.9 6.5 %copy-start.1 = (f32[1,256]{1,0:T(1,128)S(1)}, f32[1,256]{1,0:T(1,128)}, u32[]{:S(2)}) copy-start(f32[1,256]{1,0:T(1,128)} %get-tuple-element.77) | copy-start | bytes 3076

commit v3 on v2

--- a/solution.py
+++ b/solution.py
@@ -599,43 +599,28 @@
     pl.semaphore_wait(barrier, len(devices))
 
 
-def swap_kernel(count, whole, x_ref, o_ref, send_sem, recv_sem, own_sem):
+def push(src, dst, sems, k, dev):
+    copy = pltpu.make_async_remote_copy(
+        src_ref=src, dst_ref=dst, send_sem=sems[0].at[k], recv_sem=sems[1].at[k],
+        device_id=dev, device_id_type=MESH,
+    )
+    copy.start()
+    return copy
+
+
+def swap(src, dst, sems, first, whole):
+    count = dst.shape[0]
     me = lax.axis_index("inner")
-    others = [lax.rem(me + k, count) for k in range(1, count)]
-    own = pltpu.make_async_copy(x_ref if whole else x_ref.at[me], o_ref.at[me], own_sem)
-    own.start()
-    enter([{"inner": dev} for dev in others])
     copies = []
-    for k, dev in enumerate(others):
-        copy = pltpu.make_async_remote_copy(
-            src_ref=x_ref if whole else x_ref.at[dev], dst_ref=o_ref.at[me],
-            send_sem=send_sem.at[k], recv_sem=recv_sem.at[k],
-            device_id={"inner": dev}, device_id_type=MESH,
-        )
-        copy.start()
-        copies.append(copy)
-    own.wait()
-    for copy in copies:
-        copy.wait()
-
-
-def swap(x, count, whole, cid):
-    shape = ((count,) + x.shape) if whole else x.shape
-    return pl.pallas_call(
-        functools.partial(swap_kernel, count, whole),
-        out_shape=jax.ShapeDtypeStruct(shape, x.dtype),
-        in_specs=vmem(1),
-        out_specs=vmem(1)[0],
-        scratch_shapes=[
-            pltpu.SemaphoreType.DMA((count - 1,)),
-            pltpu.SemaphoreType.DMA((count - 1,)),
-            pltpu.SemaphoreType.DMA,
-        ],
-        compiler_params=params(collective_id=cid, has_side_effects=True),
-    )(x)
-
-
-def weights_kernel(wq_ref, wo_ref, g_ref, oq_ref, oo_ref, og_ref, send_sem, recv_sem, own_sem):
+    for k in range(1, count):
+        dev = lax.rem(me + k, count)
+        block = src if whole else src.at[dev]
+        copies.append(push(block, dst.at[me], sems, first + k - 1, {"inner": dev}))
+    dst[me] = src[...] if whole else src[me]
+    return copies
+
+
+def bring_weights(wq_ref, wo_ref, g_ref, oq_ref, oo_ref, og_ref, sems, first):
     pipe = lax.axis_index("pipe")
     dp = lax.axis_index("dp")
     core = lax.rem(dp, 2)
@@ -643,68 +628,50 @@
     near = {"dp": dp + 1 - 2 * core}
     half = wq_ref.shape[1] // 2
     mine = pl.ds(pl.multiple_of(core * half, half), half)
-    owns = []
-    for k, (src, dst) in enumerate(((wq_ref, oq_ref), (wo_ref, oo_ref))):
-        own = pltpu.make_async_copy(src.at[0], dst.at[pipe], own_sem.at[k])
-        own.start()
-        owns.append(own)
+    both = ((wq_ref, oq_ref), (wo_ref, oo_ref))
+    started = [
+        push(src.at[0, mine], dst.at[pipe, mine], sems, first + k, far) for k, (src, dst) in enumerate(both)
+    ]
+    gains = push(g_ref, og_ref.at[pipe], sems, first + 4, far)
+    oq_ref[pipe] = wq_ref[0]
+    oo_ref[pipe] = wo_ref[0]
     og_ref[pipe] = g_ref[...]
-    enter([far, near])
-    gains = pltpu.make_async_remote_copy(
-        src_ref=g_ref, dst_ref=og_ref.at[pipe],
-        send_sem=send_sem.at[4], recv_sem=recv_sem.at[4],
-        device_id=far, device_id_type=MESH,
-    )
-    gains.start()
-    firsts = []
-    for k, (src, dst) in enumerate(((wq_ref, oq_ref), (wo_ref, oo_ref))):
-        copy = pltpu.make_async_remote_copy(
-            src_ref=src.at[0, mine], dst_ref=dst.at[pipe, mine],
-            send_sem=send_sem.at[k], recv_sem=recv_sem.at[k],
-            device_id=far, device_id_type=MESH,
-        )
-        copy.start()
-        firsts.append(copy)
-    seconds = []
+    passed = []
     for k, dst in enumerate((oq_ref, oo_ref)):
-        firsts[k].wait_recv()
-        copy = pltpu.make_async_remote_copy(
-            src_ref=dst.at[1 - pipe, mine], dst_ref=dst.at[1 - pipe, mine],
-            send_sem=send_sem.at[2 + k], recv_sem=recv_sem.at[2 + k],
-            device_id=near, device_id_type=MESH,
-        )
-        copy.start()
-        seconds.append(copy)
-    for copy in firsts:
-        copy.wait_send()
-    for copy in seconds:
-        copy.wait()
-    for own in owns:
-        own.wait()
-    gains.wait()
-
-
-def bring_weights(wqkv, wout, gain, cid):
-    return pl.pallas_call(
-        weights_kernel,
-        out_shape=[
-            jax.ShapeDtypeStruct((2,) + wqkv.shape[1:], wqkv.dtype),
-            jax.ShapeDtypeStruct((2,) + wout.shape[1:], wout.dtype),
-            jax.ShapeDtypeStruct((2,) + gain.shape, gain.dtype),
-        ],
-        in_specs=vmem(3),
-        out_specs=vmem(3),
-        scratch_shapes=[
-            pltpu.SemaphoreType.DMA((5,)),
-            pltpu.SemaphoreType.DMA((5,)),
-            pltpu.SemaphoreType.DMA((2,)),
-        ],
-        compiler_params=params(collective_id=cid, has_side_effects=True),
-    )(wqkv, wout, gain)
-
-
-def total_kernel(dw0, dw1, dcls, dg0, dg1, dhead, loss, oqkv, oout, ocls, ogain, ohead, oloss,
-                 b0, a0, s1, b1, a1, s2, b2, a2, b3, a3, b4, a4, res, x0, xs, xr, send_sem, recv_sem):
+        started[k].wait_recv()
+        there = dst.at[1 - pipe, mine]
+        passed.append(push(there, there, sems, first + 2 + k, near))
+    for copy in passed:
+        copy.wait_recv()
+    gains.wait_recv()
+    return started + passed + [gains]
+
+
+def total_partners():
+    dp = lax.axis_index("dp")
+    inner = lax.axis_index("inner")
+    return [
+        {"dp": dp + 1 - 2 * lax.rem(dp, 2)},
+        {"pipe": 1 - lax.axis_index("pipe")},
+        {"dp": dp + 2 - 4 * (dp // 2)},
+        {"inner": inner + 1 - 2 * lax.rem(inner, 2)},
+        {"inner": inner + 2 - 4 * (inner // 2)},
+    ]
+
+
+def first_hop(layer, dw, b0, sems):
+    core = lax.rem(lax.axis_index("dp"), 2)
+    rows, width = dw.shape
+    half, cols = rows // 2, width // 2
+    there = pl.ds(pl.multiple_of((1 - core) * half, half), half)
+    return [
+        push(dw.at[there, pl.ds(c * cols, cols)], b0.at[c, layer], sems, 10 * c + layer, total_partners()[0])
+        for c in range(2)
+    ]
+
+
+def total(early, dw0, dw1, dcls, dg0, dg1, dhead, loss, res, osmall,
+          b0, a0, s1, b1, a1, s2, b2, a2, b3, a3, b4, a4, x0, xs, xr, sems):
     pipe = lax.axis_index("pipe")
     dp = lax.axis_index("dp")
     inner = lax.axis_index("inner")
@@ -714,23 +681,12 @@
     z_lo = lax.rem(inner, 2)
     rows, width = dw0.shape
     cols = width // 2
-    partners = [
-        {"dp": dp + 1 - 2 * core},
-        {"pipe": 1 - pipe},
-        {"dp": dp + 2 - 4 * y},
-        {"inner": inner + 1 - 2 * z_lo},
-        {"inner": inner + 2 - 4 * z_hi},
-    ]
+    partners = total_partners()
     started = []
 
     def send(k, src, dst, sem):
-        copy = pltpu.make_async_remote_copy(
-            src_ref=src, dst_ref=dst, send_sem=send_sem.at[sem], recv_sem=recv_sem.at[sem],
-            device_id=partners[k], device_id_type=MESH,
-        )
-        copy.start()
-        started.append(copy)
-        return copy
+        started.append(push(src, dst, sems, sem, partners[k]))
+        return started[-1]
 
     def part(bit, size):
         return pl.ds(pl.multiple_of(bit * size, size), size)
@@ -745,13 +701,11 @@
         x0[k, nc : nc + 1, :] = gain[...]
         x0[k, nc + 1 : nc + 2, :] = dhead[...]
         x0[k, nc + 2 : nc + 3, :] = loss[...]
-    enter(partners)
     half = rows // 2
     quarter = half // 2
-    going = [
-        [send(0, dw.at[part(1 - core, half), span(c)], b0.at[c, k], 10 * c + k) for k, dw in enumerate((dw0, dw1))]
-        for c in range(2)
-    ]
+    late = first_hop(0, dw0, b0, sems)
+    started += early + late
+    going = list(zip(late, early))
     small = send(0, x0, xr.at[pl.ds(0, 2)], 20)
     mine = part(core, half)
     hops = []
@@ -809,24 +763,33 @@
             gathers[c] = send(k, res.at[c, here], res.at[c, here], 10 * c + 6 + n)
         start = start - bit * size
         size *= 2
-    last = xs[5]
-    ocls[...] = last[:nc]
-    ogain[...] = last[nc : nc + 1]
-    ohead[...] = last[nc + 1 : nc + 2]
-    oloss[...] = last[nc + 2 : nc + 3]
+    osmall[...] = xs[5]
     for copy in gathers:
         copy.wait_recv()
+    for copy in started:
+        copy.wait_send()
+
+
+def finish(res, small, oqkv, oout, ocls, ogain, ohead, oloss):
+    cols = res.shape[2]
+    nc = ocls.shape[0]
     first = oqkv.shape[2] - cols
     oqkv[0, :, :cols] = res[0]
     oqkv[0, :, cols:] = res[1, :, :first]
     oout[0] = res[1, :, first:]
-    for copy in started:
-        copy.wait_send()
+    ocls[...] = small[:nc, :]
+    ogain[...] = small[nc : nc + 1, :]
+    ohead[...] = small[nc + 1 : nc + 2, :]
+    oloss[...] = small[nc + 2 : nc + 3, : oloss.shape[1]]
+
+
+def small_shape(classes, width):
+    return (-(-(classes + 3) // 8) * 8, width)
 
 
 def total_scratch(rows, width, classes):
     half, cols = rows // 2, width // 2
-    extra = (-(-(classes + 3) // 8) * 8, width // 4)
+    extra = small_shape(classes, width // 4)
     return [
         pltpu.VMEM((2, 2, half, cols), F32),
         pltpu.VMEM((2, 2, half, cols), F32),
@@ -840,32 +803,10 @@
         pltpu.VMEM((2, half // 4, cols), F32),
         pltpu.VMEM((2, half // 8, cols), F32),
         pltpu.VMEM((2, half // 8, cols), F32),
-        pltpu.VMEM((2, rows, cols), F32),
         pltpu.VMEM((2,) + extra, F32),
         pltpu.VMEM((6,) + extra, F32),
         pltpu.VMEM((6,) + extra, F32),
-        pltpu.SemaphoreType.DMA((25,)),
-        pltpu.SemaphoreType.DMA((25,)),
     ]
-
-
-def total_outs(rows, width, classes):
-    d = width // 4
-    shapes = [(1, rows, 3 * d), (1, rows, d), (classes, d), (1, d), (1, d), (1, d)]
-    return [jax.ShapeDtypeStruct(s, F32) for s in shapes]
-
-
-def total(cid, *args):
-    rows, width = args[0].shape
-    classes = args[2].shape[0]
-    return pl.pallas_call(
-        total_kernel,
-        out_shape=total_outs(rows, width, classes),
-        in_specs=vmem(len(args)),
-        out_specs=vmem(6),
-        scratch_shapes=total_scratch(rows, width, classes),
-        compiler_params=params(collective_id=cid, has_side_effects=True),
-    )(*args)
 
 
 def local(fn, outs, scalars, *args):
@@ -907,6 +848,49 @@
     return [((width, 4 * width), F32), ((1, width), F32)]
 
 
+def everything(tiles, kinds, total_tiles, batch_norm,
+               wq_own, wo_own, g_own, pix_ref, enc_ref, count_ref, slot_ref, label_ref, cls_ref, head_ref,
+               res_ref, small_ref, w_ref, wo_ref, g_ref, *refs):
+    refs = list(refs)
+
+    def take(count):
+        taken, refs[:count] = refs[:count], []
+        return taken
+
+    send_ref, recv_ref, back_ref, returned_ref, sums_ref, totals_ref = take(6)
+    saved = take(8)
+    kept = take(9)
+    dw0, dg0, dw1, dg1, dcls, dhead, loss = take(7)
+    parts = take(15)
+    sems = take(2)
+    inner = lax.axis_index("inner")
+    count = recv_ref.shape[0]
+    along = total_partners()
+    enter(along[:3] + [{"inner": lax.rem(inner + k, count)} for k in range(1, count)])
+    started = bring_weights(wq_own, wo_own, g_own, w_ref, wo_ref, g_ref, sems, 25)
+    temporal_fwd(tiles, pix_ref, enc_ref, count_ref, cls_ref, g_ref, w_ref, wo_ref, send_ref, *saved)
+    copies = swap(send_ref, recv_ref, sems, 30, False)
+    for copy in copies:
+        copy.wait_recv()
+    started += copies
+    spatial_fwd(kinds, tiles, recv_ref, g_ref, w_ref, wo_ref, head_ref, *kept, sums_ref)
+    copies = swap(sums_ref, totals_ref, sems, 30 + count, True)
+    for copy in copies:
+        copy.wait_recv()
+    started += copies
+    spatial_bwd(kinds, tiles, total_tiles, batch_norm, totals_ref, label_ref, slot_ref,
+                g_ref, w_ref, wo_ref, head_ref, *kept, back_ref, dw1, dg1, dhead, loss)
+    copies = swap(back_ref, returned_ref, sems, 30 + 2 * count, False)
+    early = first_hop(1, dw1, parts[0], sems)
+    for copy in copies:
+        copy.wait_recv()
+    started += copies
+    temporal_bwd(tiles, returned_ref, pix_ref, enc_ref, cls_ref, g_ref, w_ref, wo_ref, *saved, dw0, dg0, dcls)
+    total(early, dw0, dw1, dcls, dg0, dg1, dhead, loss, res_ref, small_ref, *parts, sems)
+    for copy in started:
+        copy.wait_send()
+
+
 def shards(pixels, date_days, clear_count, batch_slot, labels, class_tokens, section_gain,
            segment_probe_lookup_content, section_out, head_vec):
     tiles_dev, patches_dev, dates, width = pixels.shape
@@ -916,36 +900,43 @@
     tiles = tiles_dev // 2
     rows = tiles * patches_dev * dates
     batch_norm = 1.0 / (total_tiles // MICRO * PATCHES)
-    w, wo, gains = bring_weights(segment_probe_lookup_content, section_out, section_gain, 0)
     enc = date_encoding(date_days, width)
     head = head_vec.reshape(1, width)
     per = inner_count * tiles * patches_dev
-    exchanged = (inner_count, rows // inner_count, width)
-    send, *saved = local(
-        functools.partial(temporal_fwd, tiles),
-        [(exchanged, BF16)] + saved_shapes(rows, width), (2,),
-        pixels, enc, clear_count, class_tokens, gains, w, wo,
-    )
-    recv = swap(send, inner_count, False, 1)
-    *kept, sums = local(
-        functools.partial(spatial_fwd, kinds, tiles),
-        kept_shapes(kinds, per, width) + [((per, 128), F32)], (),
-        recv, gains, w, wo, head,
-    )
-    totals = swap(sums, inner_count, True, 2)
-    back, dw1, dg1, dhead, loss = local(
-        functools.partial(spatial_bwd, kinds, tiles, total_tiles, batch_norm),
-        [(exchanged, BF16)] + grad_shapes(width) + [((1, width), F32)] * 2, (2,),
-        totals, labels, batch_slot, gains, w, wo, head, *kept,
-    )
-    returned = swap(back, inner_count, False, 3)
-    dw0, dg0, dcls = local(
-        functools.partial(temporal_bwd, tiles),
-        grad_shapes(width) + [((CLASSES, width), F32)], (),
-        returned, pixels, enc, class_tokens, gains, w, wo, *saved,
-    )
-    gqkv, gout, gcls, ggain, ghead, gloss = total(4, dw0, dw1, dcls, dg0, dg1, dhead, loss)
-    return gloss[0, :MICRO], gcls, ggain, gqkv, gout, ghead.reshape(width)
+    exchanged = ((inner_count, rows // inner_count, width), BF16)
+    shapes = [
+        ((2,) + segment_probe_lookup_content.shape[1:], BF16),
+        ((2,) + section_out.shape[1:], BF16),
+        ((2,) + section_gain.shape, F32),
+        exchanged, exchanged, exchanged, exchanged,
+        ((per, 128), F32), ((inner_count, per, 128), F32),
+    ]
+    shapes += saved_shapes(rows, width) + kept_shapes(kinds, per, width) + grad_shapes(width) * 2
+    shapes += [((CLASSES, width), F32), ((1, width), F32), ((1, width), F32)]
+    specs = vmem(10)
+    specs[5] = specs[6] = pl.BlockSpec(memory_space=pltpu.SMEM)
+    sems = 30 + 3 * inner_count
+    grads, small = pl.pallas_call(
+        functools.partial(everything, tiles, kinds, total_tiles, batch_norm),
+        out_shape=[
+            jax.ShapeDtypeStruct((2, width, 2 * width), F32),
+            jax.ShapeDtypeStruct(small_shape(CLASSES, width), F32),
+        ],
+        in_specs=specs,
+        out_specs=vmem(2),
+        scratch_shapes=[pltpu.VMEM(s, t) for s, t in shapes]
+        + total_scratch(width, 4 * width, CLASSES)
+        + [pltpu.SemaphoreType.DMA((sems,))] * 2,
+        compiler_params=params(collective_id=0, has_side_effects=True),
+    )(segment_probe_lookup_content, section_out, section_gain, pixels, enc, clear_count, batch_slot,
+      labels, class_tokens, head)
+    gqkv, gout, gcls, ggain, ghead, gloss = local(
+        finish,
+        [((1, width, 3 * width), F32), ((1, width, width), F32), ((CLASSES, width), F32), ((1, width), F32),
+         ((1, width), F32), ((1, MICRO), F32)], (),
+        grads, small,
+    )
+    return gloss.reshape(MICRO), gcls, ggain, gqkv, gout, ghead.reshape(width)
 
 
 def solution(mesh):

time: 121 us -> 89.8 us (0.74)
  Pallas kernels: 111 us -> 87.3 us
  local copies, waits for them, and re-layouts: 7.1 us -> 0.65 us
    pallas_call x4 -> x1, Pallas kernels: 32.4 us -> 2.22 us  [local(): pl.pallas_call(fn, out_shape=[jax.ShapeDtypeStruct(s, t) for s, t in outs...]
    pallas_call x5 -> x1, Pallas kernels: 78.2 us -> 85.1 us  [shards(): pl.pallas_call(functools.partial(everything, tiles, kinds, total_tiles, b...]
    unnamed x9 -> x2, local copies, waits for them, and re-layouts: 5.89 us -> 0.65 us
    squeeze x1 -> x0, local copies, waits for them, and re-layouts: 1.21 us -> none  [shards(): return (gloss[0, :MICRO], gcls, ggain, gqkv, gout, ghead.reshape(width))]
where the time goes in v3:
time: 89.8 us; the launch traced here: 89.6 us
  Pallas kernels  87.3 us (97%)
  other arithmetic  0.96 us (1%)
    pallas_call x1, Pallas kernels, shards(): pl.pallas_call(functools.partial(everything, tiles, kinds, total_tiles, b...  85.1 us
    pallas_call x1, Pallas kernels, local(): pl.pallas_call(fn, out_shape=[jax.ShapeDtypeStruct(s, t) for s, t in outs...  2.22 us

profile of v3, /device:TPU:0, one launch (start us, length us, event | category | flops | bytes accessed | tf_op | source)
XLA Modules:
  0.0 89.6 jit_solution(2380732746362891920)
XLA Ops:
  0.6 0.0 copy-start
  0.7 0.6 copy-done
  1.3 0.9 %fusion.enc_ref = f32[4,16,256]{2,1,0:T(8,128)} fusion(f32[256]{0:T(256)S(1)} %fusion.4, f32[4,16]{1,0:T(4,128)S(1)} %convert_element_type.10, pred[256]{0:T(512)(128)(4,1)S(1)} %fusion.6), kind=kLoop, calls=%fused_computation.2 | loop fusion | flops 32768 | bytes 67072 | tf_op jit(solution)/shard_map/jit(_where)/select_n | solution.py:829
  2.3 85.1 %shard_map.145 = (f32[2,256,512]{2,1,0:T(8,128)}, f32[24,256]{1,0:T(8,128)}) custom-call(bf16[1,256,768]{2,1,0:T(8,128)(2,1)} %wq_own.1, bf16[1,256,256]{2,1,0:T(8,128)(2,1)} %wo_own.1, f32[1,256]{1,0:T(1,128)} %g_own.1, bf16[4,12,16,256]{3,2,1,0:T(8,128)(2,1)} %pix_ref.1, f32[4,16,256]{2,1,0:T(8,128)} %fusion.enc_ref, s32[4]{0:T(128)} %count_ref.1, ...), custom_call_target="tpu_custom_call" | custom-call | tf_op jit(solution)/shard_map/pallas_call | solution.py:919
  87.3 2.2 %shard_map.146 = (f32[1,256,768]{2,1,0:T(8,128)}, f32[1,256,256]{2,1,0:T(8,128)}, f32[16,256]{1,0:T(8,128)}, f32[1,256]{1,0:T(1,128)}, f32[1,256]{1,0:T(1,128)}, /*index=5*/f32[1,4]{1,0:T(1,128)}) custom-call(f32[2,256,512]{2,1,0:T(8,128)} %get-tuple-element.14.res, f32[24,256]{1,0:T(8,128)} %get-tuple-element.15.small), custom_call_target="tpu_custom_call" | custom-call | tf_op jit(solution)/shard_map/pallas_call | solution.py:816
  (3 shorter events, 0.0 us)
Async XLA Ops:
  0.6 0.7 copy-start

commit v4 on v3

--- a/solution.py
+++ b/solution.py
@@ -261,14 +261,33 @@
     return x.astype(BF16).astype(F32)
 
 
-def expand_heads(x, hm):
+def expand_heads(x, hmb):
     n, d = x.shape
-    return (x[None] * hm).reshape(HEADS * n, d)
-
-
-def fold_heads(x, hm):
+    return (x[None] * hmb).reshape(HEADS * n, d)
+
+
+def head_sum(pairs, hmb):
+    out = None
+    for h in range(HEADS):
+        for a, b in pairs:
+            term = mm(a[h], b * hmb[h])
+            out = term if out is None else out + term
+    return out
+
+
+def by_head(x):
     n = x.shape[0] // HEADS
-    return jnp.sum(x.reshape(HEADS, n, x.shape[1]) * hm, axis=0)
+    return [x[h * n : (h + 1) * n] for h in range(HEADS)]
+
+
+def scores(qs, ks):
+    return mm(qs[0], ks[0], 1, 1) + (mm(qs[0], ks[1], 1, 1) + mm(qs[1], ks[0], 1, 1))
+
+
+def key_back(ds, qs):
+    d = qs[0].shape[1]
+    both = mm(ds[0], jnp.concatenate(qs, axis=1), 0, 0)
+    return both[:, :d] + (both[:, d:] + mm(ds[1], qs[0], 0, 0))
 
 
 def permutation(n, outer):
@@ -296,7 +315,7 @@
     return mask
 
 
-def temporal_fwd(tiles, pix_ref, enc_ref, count_ref, cls_ref, gain_ref, w_ref, wo_ref,
+def temporal_fwd(before_out, tiles, pix_ref, enc_ref, count_ref, cls_ref, gain_ref, w_ref, wo_ref,
                  send_ref, nd_ref, kn_ref, rk_ref, v_ref, ad_ref, ac_ref, att_ref, cq_ref):
     d = pix_ref.shape[-1]
     dates = pix_ref.shape[2]
@@ -313,7 +332,7 @@
     cls = cls_ref[...].astype(F32)
     nc = (cls * norm_scale(cls) * gain).astype(BF16)
     ones = head_ones(d)
-    hm = head_mask(d)
+    hmb = head_mask(d).astype(BF16)
     kv = mm(nd, w_ref[:, d:])
     qkvc = mm(nc, w_ref[...])
     kn, rk = unit(kv[:, :d], ones)
@@ -330,14 +349,14 @@
     cq_ref[3] = rkc
     cq_ref[4] = vc.astype(F32)
     group = 128 // dates
-    qe = expand_heads(qn, hm)
+    qe = [expand_heads(p, hmb) for p in split(qn)]
     kct = jnp.concatenate([kcn] * group, axis=0)
-    ed = jnp.exp(normalizer_sharpness * mm3(qe, kn, 1, 1)) * mask
-    ec = jnp.exp(normalizer_sharpness * mm3(qe, kct, 1, 1))
+    ed = jnp.exp(normalizer_sharpness * scores(qe, split(kn))) * mask
+    ec = jnp.exp(normalizer_sharpness * scores(qe, split(kct)))
     seg = same_block(128, 128, dates).astype(BF16)
     sum_c = mm2(ec, seg)
     vct = jnp.concatenate([vc] * group, axis=0)
-    bm = group_mask(group, dates)
+    bmb = group_mask(group, dates).astype(BF16)
     atts = []
     for g in range(bps // group):
         lanes = slice(g * 128, (g + 1) * 128)
@@ -347,17 +366,23 @@
         ac = ec / den
         ad_ref[:, lanes] = ad
         ac_ref[:, lanes] = ac
-        aexp = (jnp.concatenate([ad, ac], axis=1)[None] * bm).reshape(-1, 256).astype(BF16)
+        a2 = jnp.concatenate([ad, ac], axis=1).astype(BF16)
         vst = jnp.concatenate([v[lanes], vct], axis=0)
-        o = mm(aexp, vst).reshape(group, HEADS, classes, d)
-        atts.append(jnp.sum(o * hm[None], axis=1).reshape(group * classes, d))
+        atts.append(head_sum([(by_head(expand_patches(a2, bmb)), vst)], hmb))
     att = jnp.concatenate(atts, axis=0).astype(BF16)
     att_ref[...] = att
+    before_out()
     upd = jnp.concatenate([cls] * bps, axis=0) + mm(att, wo_ref[...])
     send = mm(permutation(rows, classes), upd.astype(BF16)).astype(BF16)
     part = send_ref.shape[1]
     for k in range(send_ref.shape[0]):
         send_ref[k] = send[k * part : (k + 1) * part]
+
+
+def expand_patches(x, bmb):
+    group, _, lanes = bmb.shape
+    n = x.shape[0] // HEADS
+    return (x.reshape(HEADS, 1, n, lanes) * bmb[None]).reshape(HEADS * group * n, lanes)
 
 
 def group_mask(group, dates):
@@ -383,21 +408,22 @@
     nc = (cls * inv_c * gain).astype(BF16)
     nd = nd_ref[...]
     ones = head_ones(d)
-    hm = head_mask(d)
+    hmb = head_mask(d).astype(BF16)
     group = 128 // dates
     back = jnp.concatenate([back_ref[k] for k in range(back_ref.shape[0])], axis=0)
     du = mm(permutation(rows, rows // classes), back).astype(BF16)
     dw_ref[:, 3 * d :] = mm(att_ref[...], du, 0, 0)
-    do = rounded(mm(du, wo_ref[...], 1, 1))
+    do = mm(du, wo_ref[...], 1, 1).astype(BF16)
     qn = cq_ref[0]
     rq = cq_ref[1]
     kcn = cq_ref[2]
     rkc = cq_ref[3]
     vct = jnp.concatenate([cq_ref[4].astype(BF16)] * group, axis=0)
     kct = jnp.concatenate([kcn] * group, axis=0)
-    qe = expand_heads(qn, hm)
+    qe = [expand_heads(p, hmb) for p in split(qn)]
     seg = same_block(128, 128, dates).astype(BF16)
     bm = group_mask(group, dates)
+    bmb = bm.astype(BF16)
     qnt = jnp.concatenate([qn] * group, axis=0)
     rqt = jnp.concatenate([rq] * group, axis=0)
     rkct = jnp.concatenate([rkc] * group, axis=0)
@@ -415,21 +441,22 @@
         ad = ad_ref[:, lanes]
         ac = ac_ref[:, lanes]
         a2 = jnp.concatenate([ad, ac], axis=1)
-        aexp = (a2[None] * bm).reshape(-1, 256).astype(BF16)
+        aexp = expand_patches(a2.astype(BF16), bmb)
         vst = jnp.concatenate([v_ref[lanes, :], vct], axis=0)
-        doe = (do[lanes].reshape(group, 1, classes, d) * hm[None]).reshape(-1, d).astype(BF16)
-        da = jnp.sum(mm(doe, vst, 1, 1).reshape(group, -1, 256) * bm, axis=0)
-        da = rounded(da)
+        doe = expand_heads(do[lanes], hmb)
+        da = jnp.sum(mm(doe, vst, 1, 1).reshape(HEADS, group, classes, 256) * bm[None], axis=1)
+        da = rounded(da.reshape(HEADS * classes, 256))
         dvst = mm(aexp, doe, 0, 0).astype(BF16)
         prod = da * a2
         dot = mm2(prod[:, :128] + prod[:, 128:], seg)
         ds = normalizer_sharpness * a2 * (da - jnp.concatenate([dot, dot], axis=1))
         kn = kn_ref[lanes, :]
         kst = jnp.concatenate([kn, kct], axis=0)
-        dse = (ds[None] * bm).reshape(-1, 256)
-        dqn = jnp.sum(mm3(dse, kst).reshape(group, HEADS, classes, d) * hm[None], axis=1)
-        dqn = dqn.reshape(group * classes, d)
-        dkst = mm3(ds, qe, 0, 0)
+        ds = split(ds)
+        dh, dl = [by_head(expand_patches(p, bmb)) for p in ds]
+        kh, kl = split(kst)
+        dqn = head_sum([(dh, kh), (dh, kl), (dl, kh)], hmb)
+        dkst = key_back(ds, qe)
         dq = unit_back(dqn, qnt, rqt, ones)
         dk = unit_back(dkst[:128], kn, rk_ref[lanes, :], ones)
         dkc = unit_back(dkst[128:], kct, rkct, ones)
@@ -472,7 +499,7 @@
     n = (u * norm_scale(u) * gain_ref[...]).astype(BF16)
     n_ref[...] = n
     ones = head_ones(d)
-    hm = head_mask(d)
+    hmb = head_mask(d).astype(BF16)
     qkv = mm(n, w_ref[...])
     qn, rq = unit(qkv[:, :d], ones)
     kn, rk = unit(qkv[:, d : 2 * d], ones)
@@ -490,10 +517,11 @@
     outs = []
     for k in range(kinds):
         rs = slice(k * per, (k + 1) * per)
-        e = jnp.exp(normalizer_sharpness * mm3(expand_heads(qn[rs], hm), kn[rs], 1, 1)) * tm
+        qe = [expand_heads(p, hmb) for p in split(qn[rs])]
+        e = jnp.exp(normalizer_sharpness * scores(qe, split(kn[rs]))) * tm
         a = e / jnp.sum(e, axis=-1, keepdims=True)
         a_ref[k] = a
-        outs.append(fold_heads(mm(a.astype(BF16), v[rs]), hm))
+        outs.append(head_sum([(by_head(a.astype(BF16)), v[rs])], hmb))
     o = jnp.concatenate(outs, axis=0).astype(BF16)
     o_ref[...] = o
     hid = u + mm(o, wo_ref[...])
@@ -502,7 +530,14 @@
     raw = jnp.broadcast_to(raw, (rows, 128))
     raw_ref[...] = raw
     ex = jnp.exp(logit_cap * jnp.tanh(raw / logit_cap))
-    sum_ref[...] = jnp.sum(ex.reshape(kinds, per, 128), axis=0)
+    total = jnp.sum(ex.reshape(kinds, per, 128), axis=0)
+    total = jnp.where(diagonal(per), total, 0.0)
+    sum_ref[...] = jnp.broadcast_to(jnp.sum(total, axis=0, keepdims=True), sum_ref.shape)
+
+
+def diagonal(rows):
+    r = lax.broadcasted_iota(jnp.int32, (rows, 128), 0)
+    return r == lax.broadcasted_iota(jnp.int32, (rows, 128), 1)
 
 
 def patch_columns(label_ref, slot_ref, sources, tiles, lanes):
@@ -536,7 +571,9 @@
     rows = u_ref.shape[0]
     per = rows // kinds
     sources = tot_ref.shape[0]
-    total = jnp.sum(tot_ref[...], axis=0)
+    total = jnp.sum(tot_ref[...], axis=0)[:1]
+    total = jnp.sum(jnp.where(diagonal(per), total, 0.0), axis=-1, keepdims=True)
+    total = jnp.broadcast_to(total, (per, 128))
     total = jnp.concatenate([total] * kinds, axis=0)
     th = jnp.tanh(raw_ref[...] / logit_cap)
     logits = logit_cap * th
@@ -553,21 +590,25 @@
     col = mm2r(o_ref[...], draw, 0, 0)
     dw_ref[:, 3 * d :] = jnp.concatenate([col] * (d // 128), axis=1) * head
     head_back = mm2(jnp.broadcast_to(head, (8, d)), wo_ref[...], 1, 1)[:1]
-    do = rounded(dr * head_back)
+    do = (dr * head_back).astype(BF16)
     ones = head_ones(d)
-    hm = head_mask(d)
+    hmb = head_mask(d).astype(BF16)
     dqs, dks, dvs = [], [], []
     for k in range(kinds):
         rs = slice(k * per, (k + 1) * per)
         a = a_ref[k]
-        doe = expand_heads(do[rs], hm).astype(BF16)
+        doe = expand_heads(do[rs], hmb)
         da = rounded(mm(doe, v_ref[rs, :], 1, 1))
         dvs.append(mm(a.astype(BF16), doe, 0, 0))
         ds = normalizer_sharpness * a * (da - jnp.sum(da * a, axis=-1, keepdims=True))
         qn = qk_ref[0, rs, :]
         kn = qk_ref[1, rs, :]
-        dqs.append(unit_back(fold_heads(mm3(ds, kn), hm), qn, r_ref[0, rs, :], ones))
-        dks.append(unit_back(mm3(ds, expand_heads(qn, hm), 0, 0), kn, r_ref[1, rs, :], ones))
+        ds = split(ds)
+        dh, dl = [by_head(p) for p in ds]
+        kh, kl = split(kn)
+        qe = [expand_heads(p, hmb) for p in split(qn)]
+        dqs.append(unit_back(head_sum([(dh, kh), (dh, kl), (dl, kh)], hmb), qn, r_ref[0, rs, :], ones))
+        dks.append(unit_back(key_back(ds, qe), kn, r_ref[1, rs, :], ones))
     dq = jnp.concatenate(dqs, axis=0)
     dk = jnp.concatenate(dks, axis=0)
     dv = jnp.concatenate(dvs, axis=0).astype(BF16)
@@ -636,15 +677,18 @@
     oq_ref[pipe] = wq_ref[0]
     oo_ref[pipe] = wo_ref[0]
     og_ref[pipe] = g_ref[...]
-    passed = []
-    for k, dst in enumerate((oq_ref, oo_ref)):
+
+    def pass_on(k):
         started[k].wait_recv()
-        there = dst.at[1 - pipe, mine]
-        passed.append(push(there, there, sems, first + 2 + k, near))
-    for copy in passed:
+        there = both[k][1].at[1 - pipe, mine]
+        copy = push(there, there, sems, first + 2 + k, near)
+        started.append(copy)
         copy.wait_recv()
+
+    pass_on(0)
     gains.wait_recv()
-    return started + passed + [gains]
+    started.append(gains)
+    return started, lambda: pass_on(1)
 
 
 def total_partners():
@@ -665,20 +709,18 @@
     half, cols = rows // 2, width // 2
     there = pl.ds(pl.multiple_of((1 - core) * half, half), half)
     return [
-        push(dw.at[there, pl.ds(c * cols, cols)], b0.at[c, layer], sems, 10 * c + layer, total_partners()[0])
+        push(dw.at[there, pl.ds(c * cols, cols)], b0.at[c, layer], sems, 16 * c + layer, total_partners()[0])
         for c in range(2)
     ]
 
 
 def total(early, dw0, dw1, dcls, dg0, dg1, dhead, loss, res, osmall,
-          b0, a0, s1, b1, a1, s2, b2, a2, b3, a3, b4, a4, x0, xs, xr, sems):
+          b0, a0, s1, b1, a1, s2, b2, a2, b3, a4, x0, xs, xr, sems):
     pipe = lax.axis_index("pipe")
     dp = lax.axis_index("dp")
     inner = lax.axis_index("inner")
     core = lax.rem(dp, 2)
     y = dp // 2
-    z_hi = inner // 2
-    z_lo = lax.rem(inner, 2)
     rows, width = dw0.shape
     cols = width // 2
     partners = total_partners()
@@ -706,7 +748,7 @@
     late = first_hop(0, dw0, b0, sems)
     started += early + late
     going = list(zip(late, early))
-    small = send(0, x0, xr.at[pl.ds(0, 2)], 20)
+    small = send(0, x0, xr.at[pl.ds(0, 2)], 32)
     mine = part(core, half)
     hops = []
     for c in range(2):
@@ -720,10 +762,10 @@
         else:
             for k in range(2):
                 s1[1, pl.ds(k * quarter, quarter)] = a0[1, k, part(1 - y, quarter)].astype(s1.dtype)
-            hops.append(send(2, s1.at[1], b1.at[1], 12))
+            hops.append(send(2, s1.at[1], b1.at[1], 19))
     small.wait_recv()
     xs[pl.ds(0, 2)] = x0[...] + xr[pl.ds(0, 2)]
-    small = send(1, xs.at[1 - pipe], xr.at[2], 21)
+    small = send(1, xs.at[1 - pipe], xr.at[2], 33)
     hops[0].wait_recv()
     a1[0] = a0[0, pipe] + b1[0].astype(F32)
     s2[0] = a1[0, part(1 - y, quarter)].astype(s2.dtype)
@@ -733,36 +775,64 @@
         there = pl.ds(k * quarter, quarter)
         a1[1, there] = a0[1, k, part(y, quarter)] + b1[1, there].astype(F32)
     s2[1] = a1[1, part(1 - pipe, quarter)].astype(s2.dtype)
-    hops[1] = send(1, s2.at[1], b2.at[1], 13)
+    hops[1] = send(1, s2.at[1], b2.at[1], 18)
     small.wait_recv()
     xs[2] = xs[pipe] + xr[2]
-    small = send(2, xs.at[2], xr.at[3], 22)
-    source, bits, size = a1, (y, pipe), quarter
-    for k, nxt, acc, got in ((3, z_lo, a2, b2), (4, z_hi, a3, b3), (5, None, a4, b4)):
+    small = send(2, xs.at[2], xr.at[3], 34)
+    count = b3.shape[1] + 1
+    size = quarter // count
+    peers = [lax.rem(inner + k, count) for k in range(1, count)]
+    hops_in = [[], []]
+    for c, bit in enumerate((y, pipe)):
+        hops[c].wait_recv()
+        a2[c] = a1[c, part(bit, quarter)] + b2[c].astype(F32)
+        for k, dev in enumerate(peers):
+            copy = push(a2.at[c, part(dev, size)], b3.at[c, k], sems, 16 * c + 4 + k, {"inner": dev})
+            hops_in[c].append(copy)
+    small.wait_recv()
+    xs[3] = xs[2] + xr[3]
+    small = send(3, xs.at[3], xr.at[4], 35)
+
+    def shard(y_at, inner_at):
+        return pl.ds(pl.multiple_of(core * half + y_at * quarter + inner_at * size, size), size)
+
+    ins = [[], []]
+    ys = [[], []]
+    for c in range(2):
+        for copy in hops_in[c]:
+            copy.wait_recv()
+        own = a2[c, part(inner, size)]
+        for k in range(count - 1):
+            own = own + b3[c, k]
+        a4[c] = own
+        here = shard(y, inner)
+        res[c, here] = own
+        for k, dev in enumerate(peers):
+            ins[c].append(push(a4.at[c], res.at[c, here], sems, 16 * c + 7 + k, {"inner": dev}))
+        ys[c].append(send(2, a4.at[c], res.at[c, here], 16 * c + 10))
+    started += hops_in[0] + hops_in[1] + ins[0] + ins[1]
+    small.wait_recv()
+    xs[4] = xs[3] + xr[4]
+    small = send(4, xs.at[4], xr.at[5], 36)
+    for k in range(1, count):
+        here = shard(y, lax.rem(inner + count - k, count))
         for c in range(2):
-            hops[c].wait_recv()
-            acc[c] = source[c, part(bits[c], size)] + got[c].astype(F32)
-            if nxt is not None:
-                smaller = size // 2
-                landing = b3 if k == 3 else b4
-                hops[c] = send(k, acc.at[c, part(1 - nxt, smaller)], landing.at[c], 10 * c + k + 1)
-        small.wait_recv()
-        xs[k] = xs[k - 1] + xr[k]
-        if nxt is not None:
-            small = send(k, xs.at[k], xr.at[k + 1], 20 + k)
-            source, bits, size = acc, (nxt, nxt), size // 2
-    start = core * half + y * quarter + z_lo * (quarter // 2) + z_hi * size
-    gathers = [None, None]
-    for n, (k, bit) in enumerate(((4, z_hi), (3, z_lo), (2, y), (0, core))):
-        here = pl.ds(pl.multiple_of(start, size), size)
-        for c in range(2):
-            if n == 0:
-                res[c, here] = a4[c]
-            else:
-                gathers[c].wait_recv()
-            gathers[c] = send(k, res.at[c, here], res.at[c, here], 10 * c + 6 + n)
-        start = start - bit * size
-        size *= 2
+            ins[c][k - 1].wait_recv()
+            ys[c].append(send(2, res.at[c, here], res.at[c, here], 16 * c + 10 + k))
+    gathers = []
+
+    def to_core(c, y_at, sem):
+        here = pl.ds(pl.multiple_of(core * half + y_at * quarter, quarter), quarter)
+        gathers.append(send(0, res.at[c, here], res.at[c, here], 16 * c + sem))
+
+    for c in range(2):
+        to_core(c, y, 14)
+    small.wait_recv()
+    xs[5] = xs[4] + xr[5]
+    for c in range(2):
+        for copy in ys[c]:
+            copy.wait_recv()
+        to_core(c, 1 - y, 15)
     osmall[...] = xs[5]
     for copy in gathers:
         copy.wait_recv()
@@ -787,7 +857,7 @@
     return (-(-(classes + 3) // 8) * 8, width)
 
 
-def total_scratch(rows, width, classes):
+def total_scratch(rows, width, classes, inner_count):
     half, cols = rows // 2, width // 2
     extra = small_shape(classes, width // 4)
     return [
@@ -799,10 +869,8 @@
         pltpu.VMEM((2, half // 2, cols), BF16),
         pltpu.VMEM((2, half // 2, cols), BF16),
         pltpu.VMEM((2, half // 2, cols), F32),
-        pltpu.VMEM((2, half // 4, cols), F32),
-        pltpu.VMEM((2, half // 4, cols), F32),
-        pltpu.VMEM((2, half // 8, cols), F32),
-        pltpu.VMEM((2, half // 8, cols), F32),
+        pltpu.VMEM((2, inner_count - 1, half // 2 // inner_count, cols), F32),
+        pltpu.VMEM((2, half // 2 // inner_count, cols), F32),
         pltpu.VMEM((2,) + extra, F32),
         pltpu.VMEM((6,) + extra, F32),
         pltpu.VMEM((6,) + extra, F32),
@@ -861,26 +929,26 @@
     saved = take(8)
     kept = take(9)
     dw0, dg0, dw1, dg1, dcls, dhead, loss = take(7)
-    parts = take(15)
+    parts = take(13)
     sems = take(2)
     inner = lax.axis_index("inner")
     count = recv_ref.shape[0]
     along = total_partners()
     enter(along[:3] + [{"inner": lax.rem(inner + k, count)} for k in range(1, count)])
-    started = bring_weights(wq_own, wo_own, g_own, w_ref, wo_ref, g_ref, sems, 25)
-    temporal_fwd(tiles, pix_ref, enc_ref, count_ref, cls_ref, g_ref, w_ref, wo_ref, send_ref, *saved)
-    copies = swap(send_ref, recv_ref, sems, 30, False)
+    started, before_out = bring_weights(wq_own, wo_own, g_own, w_ref, wo_ref, g_ref, sems, 37)
+    temporal_fwd(before_out, tiles, pix_ref, enc_ref, count_ref, cls_ref, g_ref, w_ref, wo_ref, send_ref, *saved)
+    copies = swap(send_ref, recv_ref, sems, 42, False)
     for copy in copies:
         copy.wait_recv()
     started += copies
     spatial_fwd(kinds, tiles, recv_ref, g_ref, w_ref, wo_ref, head_ref, *kept, sums_ref)
-    copies = swap(sums_ref, totals_ref, sems, 30 + count, True)
+    copies = swap(sums_ref, totals_ref, sems, 42 + count, True)
     for copy in copies:
         copy.wait_recv()
     started += copies
     spatial_bwd(kinds, tiles, total_tiles, batch_norm, totals_ref, label_ref, slot_ref,
                 g_ref, w_ref, wo_ref, head_ref, *kept, back_ref, dw1, dg1, dhead, loss)
-    copies = swap(back_ref, returned_ref, sems, 30 + 2 * count, False)
+    copies = swap(back_ref, returned_ref, sems, 42 + 2 * count, False)
     early = first_hop(1, dw1, parts[0], sems)
     for copy in copies:
         copy.wait_recv()
@@ -909,13 +977,13 @@
         ((2,) + section_out.shape[1:], BF16),
         ((2,) + section_gain.shape, F32),
         exchanged, exchanged, exchanged, exchanged,
-        ((per, 128), F32), ((inner_count, per, 128), F32),
+        ((8, 128), F32), ((inner_count, 8, 128), F32),
     ]
     shapes += saved_shapes(rows, width) + kept_shapes(kinds, per, width) + grad_shapes(width) * 2
     shapes += [((CLASSES, width), F32), ((1, width), F32), ((1, width), F32)]
     specs = vmem(10)
     specs[5] = specs[6] = pl.BlockSpec(memory_space=pltpu.SMEM)
-    sems = 30 + 3 * inner_count
+    sems = 42 + 3 * inner_count
     grads, small = pl.pallas_call(
         functools.partial(everything, tiles, kinds, total_tiles, batch_norm),
         out_shape=[
@@ -925,7 +993,7 @@
         in_specs=specs,
         out_specs=vmem(2),
         scratch_shapes=[pltpu.VMEM(s, t) for s, t in shapes]
-        + total_scratch(width, 4 * width, CLASSES)
+        + total_scratch(width, 4 * width, CLASSES, inner_count)
         + [pltpu.SemaphoreType.DMA((sems,))] * 2,
         compiler_params=params(collective_id=0, has_side_effects=True),
     )(segment_probe_lookup_content, section_out, section_gain, pixels, enc, clear_count, batch_slot,
@@ -958,6 +1026,7 @@
         pairs = tiles_dev // 2 * patches_dev
         sizes = tuple(mesh.shape[a] for a in ("pipe", "dp", "inner"))
         fits = sizes == (2, 4, 4) and pairs % 8 == 0 and dates == CLASSES and width == 256
+        fits = fits and tiles_dev // 2 * PATCHES <= 128
         return (shards if fits else shards_general)(*args)
 
     return jax.shard_map(

time: 89.8 us -> 82.9 us (0.923)
  Pallas kernels: 87.3 us -> 80.5 us
    pallas_call x1, Pallas kernels: 85.1 us -> 78.3 us  [shards(): pl.pallas_call(functools.partial(everything, tiles, kinds, total_tiles, b...]
where the time goes in v4:
time: 82.9 us; the launch traced here: 82.8 us
  Pallas kernels  80.5 us (97%)
  other arithmetic  0.96 us (1%)
    pallas_call x1, Pallas kernels, shards(): pl.pallas_call(functools.partial(everything, tiles, kinds, total_tiles, b...  78.3 us
    pallas_call x1, Pallas kernels, local(): pl.pallas_call(fn, out_shape=[jax.ShapeDtypeStruct(s, t) for s, t in outs...  2.22 us

profile of v4, /device:TPU:0, one launch (start us, length us, event | category | flops | bytes accessed | tf_op | source)
XLA Modules:
  0.0 82.8 jit_solution(18204027483196341376)
XLA Ops:
  0.6 0.0 copy-start
  0.7 0.6 copy-done
  1.3 0.9 %fusion.enc_ref = f32[4,16,256]{2,1,0:T(8,128)} fusion(f32[256]{0:T(256)S(1)} %fusion.4, f32[4,16]{1,0:T(4,128)S(1)} %convert_element_type.10, pred[256]{0:T(512)(128)(4,1)S(1)} %fusion.6), kind=kLoop, calls=%fused_computation.2 | loop fusion | flops 32768 | bytes 67072 | tf_op jit(solution)/shard_map/jit(_where)/select_n | solution.py:897
  2.3 78.3 %shard_map.145 = (f32[2,256,512]{2,1,0:T(8,128)}, f32[24,256]{1,0:T(8,128)}) custom-call(bf16[1,256,768]{2,1,0:T(8,128)(2,1)} %wq_own.1, bf16[1,256,256]{2,1,0:T(8,128)(2,1)} %wo_own.1, f32[1,256]{1,0:T(1,128)} %g_own.1, bf16[4,12,16,256]{3,2,1,0:T(8,128)(2,1)} %pix_ref.1, f32[4,16,256]{2,1,0:T(8,128)} %fusion.enc_ref, s32[4]{0:T(128)} %count_ref.1, ...), custom_call_target="tpu_custom_call" | custom-call | tf_op jit(solution)/shard_map/pallas_call | solution.py:987
  80.5 2.2 %shard_map.146 = (f32[1,256,768]{2,1,0:T(8,128)}, f32[1,256,256]{2,1,0:T(8,128)}, f32[16,256]{1,0:T(8,128)}, f32[1,256]{1,0:T(1,128)}, f32[1,256]{1,0:T(1,128)}, /*index=5*/f32[1,4]{1,0:T(1,128)}) custom-call(f32[2,256,512]{2,1,0:T(8,128)} %get-tuple-element.14.res, f32[24,256]{1,0:T(8,128)} %get-tuple-element.15.small), custom_call_target="tpu_custom_call" | custom-call | tf_op jit(solution)/shard_map/pallas_call | solution.py:884
  (3 shorter events, 0.0 us)
Async XLA Ops:
  0.6 0.7 copy-start

commit v5 on v4

--- a/solution.py
+++ b/solution.py
@@ -391,7 +391,7 @@
     return (g == c).astype(F32)
 
 
-def temporal_bwd(tiles, back_ref, pix_ref, enc_ref, cls_ref, gain_ref, w_ref, wo_ref,
+def temporal_bwd(advance, tiles, back_ref, pix_ref, enc_ref, cls_ref, gain_ref, w_ref, wo_ref,
                  nd_ref, kn_ref, rk_ref, v_ref, ad_ref, ac_ref, att_ref, cq_ref,
                  dw_ref, dgain_ref, dcls_ref):
     d = pix_ref.shape[-1]
@@ -436,6 +436,7 @@
     dnc = jnp.zeros((classes, d), F32)
     dgain = jnp.zeros((1, d), F32)
     xhat = x * norm_scale(x)
+    das, dvs = [], []
     for g in range(bps // group):
         lanes = slice(g * 128, (g + 1) * 128)
         ad = ad_ref[:, lanes]
@@ -445,8 +446,16 @@
         vst = jnp.concatenate([v_ref[lanes, :], vct], axis=0)
         doe = expand_heads(do[lanes], hmb)
         da = jnp.sum(mm(doe, vst, 1, 1).reshape(HEADS, group, classes, 256) * bm[None], axis=1)
-        da = rounded(da.reshape(HEADS * classes, 256))
+        das.append(rounded(da.reshape(HEADS * classes, 256)))
         dvst = mm(aexp, doe, 0, 0).astype(BF16)
+        dvs.append(dvst)
+        dwv += mm(nd[lanes], dvst[:128], 0, 0) + mm(nct, dvst[128:], 0, 0)
+    dw_ref[:, 2 * d : 3 * d] = dwv
+    advance()
+    for g in range(bps // group):
+        lanes = slice(g * 128, (g + 1) * 128)
+        a2 = jnp.concatenate([ad_ref[:, lanes], ac_ref[:, lanes]], axis=1)
+        da, dvst = das[g], dvs[g]
         prod = da * a2
         dot = mm2(prod[:, :128] + prod[:, 128:], seg)
         ds = normalizer_sharpness * a2 * (da - jnp.concatenate([dot, dot], axis=1))
@@ -463,15 +472,14 @@
         ndg = nd[lanes]
         dwq += mm2r(nct, dq, 0, 0)
         dwk += mm2r(ndg, dk, 0, 0) + mm2r(nct, dkc, 0, 0)
-        dwv += mm(ndg, dvst[:128], 0, 0) + mm(nct, dvst[128:], 0, 0)
         dn_k = rounded(mm2(jnp.concatenate([dk, dkc], axis=0), wk, 1, 1))
         dn = rounded(rounded(mm(dvst, wv, 1, 1)) + dn_k)
         dn_c = rounded(dn[128:] + rounded(mm2(dq, wq, 1, 1)))
         dgain += jnp.sum(dn[:128] * xhat[lanes], axis=0, keepdims=True)
         dnc += jnp.sum(dn_c.reshape(group, classes, d), axis=0)
+        advance()
     dw_ref[:, :d] = dwq
     dw_ref[:, d : 2 * d] = dwk
-    dw_ref[:, 2 * d : 3 * d] = dwv
     dgain_ref[...] = dgain + jnp.sum(dnc * cls * inv_c, axis=0, keepdims=True)
     t = dnc * gain
     dcls = inv_c * (t - cls * (inv_c * inv_c * jnp.mean(t * cls, axis=-1, keepdims=True)))
@@ -561,7 +569,7 @@
     return jnp.broadcast_to(jnp.sum(labels, axis=-1, keepdims=True), slot_shape), slots
 
 
-def spatial_bwd(kinds, tiles, total_tiles, batch_norm, tot_ref, label_ref, slot_ref, gain_ref, w_ref, wo_ref, head_ref,
+def spatial_bwd(after_send, kinds, tiles, total_tiles, batch_norm, tot_ref, label_ref, slot_ref, gain_ref, w_ref, wo_ref, head_ref,
                 u_ref, n_ref, qk_ref, r_ref, v_ref, a_ref, o_ref, hid_ref, raw_ref,
                 send_ref, dw_ref, dgain_ref, dhead_ref, loss_ref):
     d = u_ref.shape[-1]
@@ -586,9 +594,6 @@
     draw = (jnp.exp(logits) / total - ind) / total_tiles * (1.0 - th * th)
     dr = jnp.concatenate([draw] * (d // 128), axis=1)
     head = head_ref[...]
-    dhead_ref[...] = jnp.sum(dr * hid_ref[...], axis=0, keepdims=True)
-    col = mm2r(o_ref[...], draw, 0, 0)
-    dw_ref[:, 3 * d :] = jnp.concatenate([col] * (d // 128), axis=1) * head
     head_back = mm2(jnp.broadcast_to(head, (8, d)), wo_ref[...], 1, 1)[:1]
     do = (dr * head_back).astype(BF16)
     ones = head_ones(d)
@@ -612,22 +617,26 @@
     dq = jnp.concatenate(dqs, axis=0)
     dk = jnp.concatenate(dks, axis=0)
     dv = jnp.concatenate(dvs, axis=0).astype(BF16)
-    n = n_ref[...]
-    dw_ref[:, :d] = mm2r(n, dq, 0, 0)
-    dw_ref[:, d : 2 * d] = mm2r(n, dk, 0, 0)
-    dw_ref[:, 2 * d : 3 * d] = mm(n, dv, 0, 0)
     w = w_ref[...]
     dn = rounded(rounded(mm(dv, w[:, 2 * d :], 1, 1)) + rounded(mm2(dk, w[:, d : 2 * d], 1, 1)))
     dn = rounded(dn + rounded(mm2(dq, w[:, :d], 1, 1)))
     u = u_ref[...]
     inv = norm_scale(u)
-    dgain_ref[...] = jnp.sum(dn * u * inv, axis=0, keepdims=True)
     t = dn * gain_ref[...]
     du = dr * head + inv * (t - u * (inv * inv * jnp.mean(t * u, axis=-1, keepdims=True)))
     m = per // sources
     for s in range(sources):
         parts = [du[k * per + s * m : k * per + (s + 1) * m] for k in range(kinds)]
         send_ref[s] = jnp.concatenate(parts, axis=0).astype(BF16)
+    after_send()
+    n = n_ref[...]
+    dw_ref[:, :d] = mm2r(n, dq, 0, 0)
+    dw_ref[:, d : 2 * d] = mm2r(n, dk, 0, 0)
+    dw_ref[:, 2 * d : 3 * d] = mm(n, dv, 0, 0)
+    col = mm2r(o_ref[...], draw, 0, 0)
+    dw_ref[:, 3 * d :] = jnp.concatenate([col] * (d // 128), axis=1) * head
+    dgain_ref[...] = jnp.sum(dn * u * inv, axis=0, keepdims=True)
+    dhead_ref[...] = jnp.sum(dr * hid_ref[...], axis=0, keepdims=True)
 
 
 MESH = pl.DeviceIdType.MESH
@@ -703,19 +712,19 @@
     ]
 
 
-def first_hop(layer, dw, b0, sems):
+def part(bit, size):
+    return pl.ds(pl.multiple_of(bit * size, size), size)
+
+
+def first_hop(c, layer, dw, b0, sems):
     core = lax.rem(lax.axis_index("dp"), 2)
     rows, width = dw.shape
     half, cols = rows // 2, width // 2
-    there = pl.ds(pl.multiple_of((1 - core) * half, half), half)
-    return [
-        push(dw.at[there, pl.ds(c * cols, cols)], b0.at[c, layer], sems, 16 * c + layer, total_partners()[0])
-        for c in range(2)
-    ]
-
-
-def total(early, dw0, dw1, dcls, dg0, dg1, dhead, loss, res, osmall,
-          b0, a0, s1, b1, a1, s2, b2, a2, b3, a4, x0, xs, xr, sems):
+    there = dw.at[part(1 - core, half), pl.ds(c * cols, cols)]
+    return push(there, b0.at[c, layer], sems, 16 * c + layer, total_partners()[0])
+
+
+def chunk_chain(c, early, dw0, dw1, res, started, sems, b0, a0, s1, b1, a1, s2, b2, a2, b3, a4):
     pipe = lax.axis_index("pipe")
     dp = lax.axis_index("dp")
     inner = lax.axis_index("inner")
@@ -723,121 +732,111 @@
     y = dp // 2
     rows, width = dw0.shape
     cols = width // 2
+    half = rows // 2
+    quarter = half // 2
     partners = total_partners()
-    started = []
-
-    def send(k, src, dst, sem):
-        started.append(push(src, dst, sems, sem, partners[k]))
+    count = b3.shape[1] + 1
+    size = quarter // count
+    peers = [lax.rem(inner + k, count) for k in range(1, count)]
+    base = 16 * c
+
+    def send(dev, src, dst, sem):
+        started.append(push(src, dst, sems, base + sem, dev))
         return started[-1]
 
-    def part(bit, size):
-        return pl.ds(pl.multiple_of(bit * size, size), size)
-
-    def span(c):
-        return pl.ds(c * cols, cols)
-
+    def shard(y_at, inner_at):
+        return pl.ds(pl.multiple_of(core * half + y_at * quarter + inner_at * size, size), size)
+
+    def to_core(y_at, sem):
+        here = res.at[c, pl.ds(pl.multiple_of(core * half + y_at * quarter, quarter), quarter)]
+        return send(partners[0], here, here, sem)
+
+    late = first_hop(c, 0, dw0, b0, sems)
+    started += [late, early]
+    yield
+    for k, (copy, dw) in enumerate(((late, dw0), (early, dw1))):
+        copy.wait_recv()
+        a0[c, k] = dw[part(core, half), pl.ds(c * cols, cols)] + b0[c, k]
+    if c == 0:
+        s1[0] = a0[0, 1 - pipe].astype(s1.dtype)
+        hop = send(partners[1], s1.at[0], b1.at[0], 2)
+    else:
+        for k in range(2):
+            s1[1, pl.ds(k * quarter, quarter)] = a0[1, k, part(1 - y, quarter)].astype(s1.dtype)
+        hop = send(partners[2], s1.at[1], b1.at[1], 3)
+    yield
+    hop.wait_recv()
+    if c == 0:
+        a1[0] = a0[0, pipe] + b1[0].astype(F32)
+        s2[0] = a1[0, part(1 - y, quarter)].astype(s2.dtype)
+        hop = send(partners[2], s2.at[0], b2.at[0], 3)
+    else:
+        for k in range(2):
+            there = pl.ds(k * quarter, quarter)
+            a1[1, there] = a0[1, k, part(y, quarter)] + b1[1, there].astype(F32)
+        s2[1] = a1[1, part(1 - pipe, quarter)].astype(s2.dtype)
+        hop = send(partners[1], s2.at[1], b2.at[1], 2)
+    yield
+    hop.wait_recv()
+    a2[c] = a1[c, part(y if c == 0 else pipe, quarter)] + b2[c].astype(F32)
+    hops = [
+        send({"inner": dev}, a2.at[c, part(dev, size)], b3.at[c, k], 4 + k) for k, dev in enumerate(peers)
+    ]
+    yield
+    for copy in hops:
+        copy.wait_recv()
+    own = a2[c, part(inner, size)]
+    for k in range(count - 1):
+        own = own + b3[c, k]
+    a4[c] = own
+    here = shard(y, inner)
+    res[c, here] = own
+    ins = [send({"inner": dev}, a4.at[c], res.at[c, here], 7 + k) for k, dev in enumerate(peers)]
+    ys = [send(partners[2], a4.at[c], res.at[c, here], 10)]
+    yield
+    for k in range(1, count):
+        here = shard(y, lax.rem(inner + count - k, count))
+        ins[k - 1].wait_recv()
+        ys.append(send(partners[2], res.at[c, here], res.at[c, here], 10 + k))
+    gathers = [to_core(y, 14)]
+    yield
+    for copy in ys:
+        copy.wait_recv()
+    gathers.append(to_core(1 - y, 15))
+    yield
+    for copy in gathers:
+        copy.wait_recv()
+
+
+def small_chain(dcls, dg0, dg1, dhead, loss, osmall, started, sems, x0, xs, xr):
+    pipe = lax.axis_index("pipe")
     nc = dcls.shape[0]
+    partners = total_partners()
+
+    def send(k, src, dst):
+        started.append(push(src, dst, sems, 32 + k, partners[k]))
+        return started[-1]
+
     x0[...] = jnp.zeros_like(x0)
     for k, gain in enumerate((dg0, dg1)):
         x0[k, :nc, :] = dcls[...]
         x0[k, nc : nc + 1, :] = gain[...]
         x0[k, nc + 1 : nc + 2, :] = dhead[...]
         x0[k, nc + 2 : nc + 3, :] = loss[...]
-    half = rows // 2
-    quarter = half // 2
-    late = first_hop(0, dw0, b0, sems)
-    started += early + late
-    going = list(zip(late, early))
-    small = send(0, x0, xr.at[pl.ds(0, 2)], 32)
-    mine = part(core, half)
-    hops = []
-    for c in range(2):
-        for copy in going[c]:
-            copy.wait_recv()
-        for k, dw in enumerate((dw0, dw1)):
-            a0[c, k] = dw[mine, span(c)] + b0[c, k]
-        if c == 0:
-            s1[0] = a0[0, 1 - pipe].astype(s1.dtype)
-            hops.append(send(1, s1.at[0], b1.at[0], 2))
-        else:
-            for k in range(2):
-                s1[1, pl.ds(k * quarter, quarter)] = a0[1, k, part(1 - y, quarter)].astype(s1.dtype)
-            hops.append(send(2, s1.at[1], b1.at[1], 19))
-    small.wait_recv()
+    copy = send(0, x0, xr.at[pl.ds(0, 2)])
+    yield
+    copy.wait_recv()
     xs[pl.ds(0, 2)] = x0[...] + xr[pl.ds(0, 2)]
-    small = send(1, xs.at[1 - pipe], xr.at[2], 33)
-    hops[0].wait_recv()
-    a1[0] = a0[0, pipe] + b1[0].astype(F32)
-    s2[0] = a1[0, part(1 - y, quarter)].astype(s2.dtype)
-    hops[0] = send(2, s2.at[0], b2.at[0], 3)
-    hops[1].wait_recv()
-    for k in range(2):
-        there = pl.ds(k * quarter, quarter)
-        a1[1, there] = a0[1, k, part(y, quarter)] + b1[1, there].astype(F32)
-    s2[1] = a1[1, part(1 - pipe, quarter)].astype(s2.dtype)
-    hops[1] = send(1, s2.at[1], b2.at[1], 18)
-    small.wait_recv()
+    copy = send(1, xs.at[1 - pipe], xr.at[2])
+    yield
+    copy.wait_recv()
     xs[2] = xs[pipe] + xr[2]
-    small = send(2, xs.at[2], xr.at[3], 34)
-    count = b3.shape[1] + 1
-    size = quarter // count
-    peers = [lax.rem(inner + k, count) for k in range(1, count)]
-    hops_in = [[], []]
-    for c, bit in enumerate((y, pipe)):
-        hops[c].wait_recv()
-        a2[c] = a1[c, part(bit, quarter)] + b2[c].astype(F32)
-        for k, dev in enumerate(peers):
-            copy = push(a2.at[c, part(dev, size)], b3.at[c, k], sems, 16 * c + 4 + k, {"inner": dev})
-            hops_in[c].append(copy)
-    small.wait_recv()
-    xs[3] = xs[2] + xr[3]
-    small = send(3, xs.at[3], xr.at[4], 35)
-
-    def shard(y_at, inner_at):
-        return pl.ds(pl.multiple_of(core * half + y_at * quarter + inner_at * size, size), size)
-
-    ins = [[], []]
-    ys = [[], []]
-    for c in range(2):
-        for copy in hops_in[c]:
-            copy.wait_recv()
-        own = a2[c, part(inner, size)]
-        for k in range(count - 1):
-            own = own + b3[c, k]
-        a4[c] = own
-        here = shard(y, inner)
-        res[c, here] = own
-        for k, dev in enumerate(peers):
-            ins[c].append(push(a4.at[c], res.at[c, here], sems, 16 * c + 7 + k, {"inner": dev}))
-        ys[c].append(send(2, a4.at[c], res.at[c, here], 16 * c + 10))
-    started += hops_in[0] + hops_in[1] + ins[0] + ins[1]
-    small.wait_recv()
-    xs[4] = xs[3] + xr[4]
-    small = send(4, xs.at[4], xr.at[5], 36)
-    for k in range(1, count):
-        here = shard(y, lax.rem(inner + count - k, count))
-        for c in range(2):
-            ins[c][k - 1].wait_recv()
-            ys[c].append(send(2, res.at[c, here], res.at[c, here], 16 * c + 10 + k))
-    gathers = []
-
-    def to_core(c, y_at, sem):
-        here = pl.ds(pl.multiple_of(core * half + y_at * quarter, quarter), quarter)
-        gathers.append(send(0, res.at[c, here], res.at[c, here], 16 * c + sem))
-
-    for c in range(2):
-        to_core(c, y, 14)
-    small.wait_recv()
-    xs[5] = xs[4] + xr[5]
-    for c in range(2):
-        for copy in ys[c]:
-            copy.wait_recv()
-        to_core(c, 1 - y, 15)
+    for k in (3, 4, 5):
+        copy = send(k - 1, xs.at[k - 1], xr.at[k])
+        yield
+        copy.wait_recv()
+        xs[k] = xs[k - 1] + xr[k]
     osmall[...] = xs[5]
-    for copy in gathers:
-        copy.wait_recv()
-    for copy in started:
-        copy.wait_send()
 
 
 def finish(res, small, oqkv, oout, ocls, ogain, ohead, oloss):
@@ -946,15 +945,22 @@
     for copy in copies:
         copy.wait_recv()
     started += copies
-    spatial_bwd(kinds, tiles, total_tiles, batch_norm, totals_ref, label_ref, slot_ref,
+    copies = []
+    spatial_bwd(lambda: copies.extend(swap(back_ref, returned_ref, sems, 42 + 2 * count, False)),
+                kinds, tiles, total_tiles, batch_norm, totals_ref, label_ref, slot_ref,
                 g_ref, w_ref, wo_ref, head_ref, *kept, back_ref, dw1, dg1, dhead, loss)
-    copies = swap(back_ref, returned_ref, sems, 42 + 2 * count, False)
-    early = first_hop(1, dw1, parts[0], sems)
+    early = [first_hop(c, 1, dw1, parts[0], sems) for c in range(2)]
     for copy in copies:
         copy.wait_recv()
     started += copies
-    temporal_bwd(tiles, returned_ref, pix_ref, enc_ref, cls_ref, g_ref, w_ref, wo_ref, *saved, dw0, dg0, dcls)
-    total(early, dw0, dw1, dcls, dg0, dg1, dhead, loss, res_ref, small_ref, *parts, sems)
+    chains = [
+        chunk_chain(c, early[c], dw0, dw1, res_ref, started, sems, *parts[:10]) for c in range(2)
+    ]
+    smalls = small_chain(dcls, dg0, dg1, dhead, loss, small_ref, started, sems, *parts[10:])
+    temporal_bwd(lambda: next(chains[1]), tiles, returned_ref, pix_ref, enc_ref, cls_ref, g_ref, w_ref, wo_ref, *saved, dw0, dg0, dcls)
+    chains.insert(1, smalls)
+    while chains:
+        chains = [chain for chain in chains if next(chain, True) is None]
     for copy in started:
         copy.wait_send()
 

time: 82.9 us -> 91.7 us (1.11)
  Pallas kernels: 80.5 us -> 89.3 us
    pallas_call x1, Pallas kernels: 78.3 us -> 87 us  [shards(): pl.pallas_call(functools.partial(everything, tiles, kinds, total_tiles, b...]
where the time goes in v5:
time: 91.7 us; the launch traced here: 91.5 us
  Pallas kernels  89.3 us (97%)
  other arithmetic  0.96 us (1%)
    pallas_call x1, Pallas kernels, shards(): pl.pallas_call(functools.partial(everything, tiles, kinds, total_tiles, b...  87 us
    pallas_call x1, Pallas kernels, local(): pl.pallas_call(fn, out_shape=[jax.ShapeDtypeStruct(s, t) for s, t in outs...  2.22 us

profile of v5, /device:TPU:0, one launch (start us, length us, event | category | flops | bytes accessed | tf_op | source)
XLA Modules:
  0.0 91.5 jit_solution(2780116314644298142)
XLA Ops:
  0.6 0.0 copy-start
  0.7 0.6 copy-done
  1.3 0.9 %fusion.enc_ref = f32[4,16,256]{2,1,0:T(8,128)} fusion(f32[256]{0:T(256)S(1)} %fusion.4, f32[4,16]{1,0:T(4,128)S(1)} %convert_element_type.10, pred[256]{0:T(512)(128)(4,1)S(1)} %fusion.6), kind=kLoop, calls=%fused_computation.2 | loop fusion | flops 32768 | bytes 67072 | tf_op jit(solution)/shard_map/jit(_where)/select_n | solution.py:896
  2.3 87.0 %shard_map.145 = (f32[2,256,512]{2,1,0:T(8,128)}, f32[24,256]{1,0:T(8,128)}) custom-call(bf16[1,256,768]{2,1,0:T(8,128)(2,1)} %wq_own.1, bf16[1,256,256]{2,1,0:T(8,128)(2,1)} %wo_own.1, f32[1,256]{1,0:T(1,128)} %g_own.1, bf16[4,12,16,256]{3,2,1,0:T(8,128)(2,1)} %pix_ref.1, f32[4,16,256]{2,1,0:T(8,128)} %fusion.enc_ref, s32[4]{0:T(128)} %count_ref.1, ...), custom_call_target="tpu_custom_call" | custom-call | tf_op jit(solution)/shard_map/pallas_call | solution.py:993
  89.3 2.2 %shard_map.146 = (f32[1,256,768]{2,1,0:T(8,128)}, f32[1,256,256]{2,1,0:T(8,128)}, f32[16,256]{1,0:T(8,128)}, f32[1,256]{1,0:T(1,128)}, f32[1,256]{1,0:T(1,128)}, /*index=5*/f32[1,4]{1,0:T(1,128)}) custom-call(f32[2,256,512]{2,1,0:T(8,128)} %get-tuple-element.14.res, f32[24,256]{1,0:T(8,128)} %get-tuple-element.15.small), custom_call_target="tpu_custom_call" | custom-call | tf_op jit(solution)/shard_map/pallas_call | solution.py:883
  (3 shorter events, 0.0 us)
Async XLA Ops:
  0.6 0.7 copy-start

commit v6 on v4

--- a/solution.py
+++ b/solution.py
@@ -391,7 +391,7 @@
     return (g == c).astype(F32)
 
 
-def temporal_bwd(tiles, back_ref, pix_ref, enc_ref, cls_ref, gain_ref, w_ref, wo_ref,
+def temporal_bwd(arrive, tiles, back_ref, pix_ref, enc_ref, cls_ref, gain_ref, w_ref, wo_ref,
                  nd_ref, kn_ref, rk_ref, v_ref, ad_ref, ac_ref, att_ref, cq_ref,
                  dw_ref, dgain_ref, dcls_ref):
     d = pix_ref.shape[-1]
@@ -410,10 +410,6 @@
     ones = head_ones(d)
     hmb = head_mask(d).astype(BF16)
     group = 128 // dates
-    back = jnp.concatenate([back_ref[k] for k in range(back_ref.shape[0])], axis=0)
-    du = mm(permutation(rows, rows // classes), back).astype(BF16)
-    dw_ref[:, 3 * d :] = mm(att_ref[...], du, 0, 0)
-    do = mm(du, wo_ref[...], 1, 1).astype(BF16)
     qn = cq_ref[0]
     rq = cq_ref[1]
     kcn = cq_ref[2]
@@ -436,6 +432,12 @@
     dnc = jnp.zeros((classes, d), F32)
     dgain = jnp.zeros((1, d), F32)
     xhat = x * norm_scale(x)
+    order = permutation(rows, rows // classes)
+    arrive()
+    back = jnp.concatenate([back_ref[k] for k in range(back_ref.shape[0])], axis=0)
+    du = mm(order, back).astype(BF16)
+    dw_ref[:, 3 * d :] = mm(att_ref[...], du, 0, 0)
+    do = mm(du, wo_ref[...], 1, 1).astype(BF16)
     for g in range(bps // group):
         lanes = slice(g * 128, (g + 1) * 128)
         ad = ad_ref[:, lanes]
@@ -561,7 +563,7 @@
     return jnp.broadcast_to(jnp.sum(labels, axis=-1, keepdims=True), slot_shape), slots
 
 
-def spatial_bwd(kinds, tiles, total_tiles, batch_norm, tot_ref, label_ref, slot_ref, gain_ref, w_ref, wo_ref, head_ref,
+def spatial_bwd(after_send, kinds, tiles, total_tiles, batch_norm, tot_ref, label_ref, slot_ref, gain_ref, w_ref, wo_ref, head_ref,
                 u_ref, n_ref, qk_ref, r_ref, v_ref, a_ref, o_ref, hid_ref, raw_ref,
                 send_ref, dw_ref, dgain_ref, dhead_ref, loss_ref):
     d = u_ref.shape[-1]
@@ -586,9 +588,6 @@
     draw = (jnp.exp(logits) / total - ind) / total_tiles * (1.0 - th * th)
     dr = jnp.concatenate([draw] * (d // 128), axis=1)
     head = head_ref[...]
-    dhead_ref[...] = jnp.sum(dr * hid_ref[...], axis=0, keepdims=True)
-    col = mm2r(o_ref[...], draw, 0, 0)
-    dw_ref[:, 3 * d :] = jnp.concatenate([col] * (d // 128), axis=1) * head
     head_back = mm2(jnp.broadcast_to(head, (8, d)), wo_ref[...], 1, 1)[:1]
     do = (dr * head_back).astype(BF16)
     ones = head_ones(d)
@@ -612,22 +611,26 @@
     dq = jnp.concatenate(dqs, axis=0)
     dk = jnp.concatenate(dks, axis=0)
     dv = jnp.concatenate(dvs, axis=0).astype(BF16)
-    n = n_ref[...]
-    dw_ref[:, :d] = mm2r(n, dq, 0, 0)
-    dw_ref[:, d : 2 * d] = mm2r(n, dk, 0, 0)
-    dw_ref[:, 2 * d : 3 * d] = mm(n, dv, 0, 0)
     w = w_ref[...]
     dn = rounded(rounded(mm(dv, w[:, 2 * d :], 1, 1)) + rounded(mm2(dk, w[:, d : 2 * d], 1, 1)))
     dn = rounded(dn + rounded(mm2(dq, w[:, :d], 1, 1)))
     u = u_ref[...]
     inv = norm_scale(u)
-    dgain_ref[...] = jnp.sum(dn * u * inv, axis=0, keepdims=True)
     t = dn * gain_ref[...]
     du = dr * head + inv * (t - u * (inv * inv * jnp.mean(t * u, axis=-1, keepdims=True)))
     m = per // sources
     for s in range(sources):
         parts = [du[k * per + s * m : k * per + (s + 1) * m] for k in range(kinds)]
         send_ref[s] = jnp.concatenate(parts, axis=0).astype(BF16)
+    after_send()
+    n = n_ref[...]
+    dw_ref[:, :d] = mm2r(n, dq, 0, 0)
+    dw_ref[:, d : 2 * d] = mm2r(n, dk, 0, 0)
+    dw_ref[:, 2 * d : 3 * d] = mm(n, dv, 0, 0)
+    col = mm2r(o_ref[...], draw, 0, 0)
+    dw_ref[:, 3 * d :] = jnp.concatenate([col] * (d // 128), axis=1) * head
+    dgain_ref[...] = jnp.sum(dn * u * inv, axis=0, keepdims=True)
+    dhead_ref[...] = jnp.sum(dr * hid_ref[...], axis=0, keepdims=True)
 
 
 MESH = pl.DeviceIdType.MESH
@@ -946,14 +949,18 @@
     for copy in copies:
         copy.wait_recv()
     started += copies
-    spatial_bwd(kinds, tiles, total_tiles, batch_norm, totals_ref, label_ref, slot_ref,
+    copies = []
+    spatial_bwd(lambda: copies.extend(swap(back_ref, returned_ref, sems, 42 + 2 * count, False)),
+                kinds, tiles, total_tiles, batch_norm, totals_ref, label_ref, slot_ref,
                 g_ref, w_ref, wo_ref, head_ref, *kept, back_ref, dw1, dg1, dhead, loss)
-    copies = swap(back_ref, returned_ref, sems, 42 + 2 * count, False)
     early = first_hop(1, dw1, parts[0], sems)
-    for copy in copies:
-        copy.wait_recv()
     started += copies
-    temporal_bwd(tiles, returned_ref, pix_ref, enc_ref, cls_ref, g_ref, w_ref, wo_ref, *saved, dw0, dg0, dcls)
+
+    def arrive():
+        for copy in copies:
+            copy.wait_recv()
+
+    temporal_bwd(arrive, tiles, returned_ref, pix_ref, enc_ref, cls_ref, g_ref, w_ref, wo_ref, *saved, dw0, dg0, dcls)
     total(early, dw0, dw1, dcls, dg0, dg1, dhead, loss, res_ref, small_ref, *parts, sems)
     for copy in started:
         copy.wait_send()

time: 82.9 us -> 83.2 us (level)
  no operation moved by 1% of the time
where the time goes in v6:
time: 83.2 us; the launch traced here: 83 us
  Pallas kernels  80.7 us (97%)
  other arithmetic  0.96 us (1%)
    pallas_call x1, Pallas kernels, shards(): pl.pallas_call(functools.partial(everything, tiles, kinds, total_tiles, b...  78.5 us
    pallas_call x1, Pallas kernels, local(): pl.pallas_call(fn, out_shape=[jax.ShapeDtypeStruct(s, t) for s, t in outs...  2.22 us

profile of v6, /device:TPU:0, one launch (start us, length us, event | category | flops | bytes accessed | tf_op | source)
XLA Modules:
  0.0 83.0 jit_solution(2360066337023476833)
XLA Ops:
  0.6 0.0 copy-start
  0.7 0.6 copy-done
  1.3 0.9 %fusion.enc_ref = f32[4,16,256]{2,1,0:T(8,128)} fusion(f32[256]{0:T(256)S(1)} %fusion.4, f32[4,16]{1,0:T(4,128)S(1)} %convert_element_type.10, pred[256]{0:T(512)(128)(4,1)S(1)} %fusion.6), kind=kLoop, calls=%fused_computation.2 | loop fusion | flops 32768 | bytes 67072 | tf_op jit(solution)/shard_map/jit(_where)/select_n | solution.py:900
  2.3 78.5 %shard_map.145 = (f32[2,256,512]{2,1,0:T(8,128)}, f32[24,256]{1,0:T(8,128)}) custom-call(bf16[1,256,768]{2,1,0:T(8,128)(2,1)} %wq_own.1, bf16[1,256,256]{2,1,0:T(8,128)(2,1)} %wo_own.1, f32[1,256]{1,0:T(1,128)} %g_own.1, bf16[4,12,16,256]{3,2,1,0:T(8,128)(2,1)} %pix_ref.1, f32[4,16,256]{2,1,0:T(8,128)} %fusion.enc_ref, s32[4]{0:T(128)} %count_ref.1, ...), custom_call_target="tpu_custom_call" | custom-call | tf_op jit(solution)/shard_map/pallas_call | solution.py:994
  80.8 2.2 %shard_map.146 = (f32[1,256,768]{2,1,0:T(8,128)}, f32[1,256,256]{2,1,0:T(8,128)}, f32[16,256]{1,0:T(8,128)}, f32[1,256]{1,0:T(1,128)}, f32[1,256]{1,0:T(1,128)}, /*index=5*/f32[1,4]{1,0:T(1,128)}) custom-call(f32[2,256,512]{2,1,0:T(8,128)} %get-tuple-element.14.res, f32[24,256]{1,0:T(8,128)} %get-tuple-element.15.small), custom_call_target="tpu_custom_call" | custom-call | tf_op jit(solution)/shard_map/pallas_call | solution.py:887
  (3 shorter events, 0.0 us)
Async XLA Ops:
  0.6 0.7 copy-start
